TPU v7x, 128 devices: a whole 4x4x4 slice. The times are simulated.
128 devices in a mesh: sample: 16 (over z_lo, x, core), tensor: 8 (over y, z_hi).
Axes of the slice: x: 4, y: 4, z: 4 (z_hi: 2, z_lo: 2; z = z_hi * 2 + z_lo), core: 2. Of those that a mesh axis runs over, the one named last changes fastest.
Arguments:
- branch_tokens: bfloat16 [4096, 8192], P('sample', 'tensor'), may hold values from -6 to 6
- norm_gain: bfloat16 [8192], replicated, may hold values from 0.099609375 to 1.8984375
- query_weight: bfloat16 [8192, 8192], P(None, 'tensor'), may hold values from -0.0625 to 0.0625
- key_weight: bfloat16 [8192, 1024], P(None, 'tensor'), may hold values from -0.21875 to 0.21875
- value_weight: bfloat16 [8192, 1024], P(None, 'tensor'), may hold values from -0.0625 to 0.0625
- kv_pool: bfloat16 [640, 2, 128, 1024], P('sample', None, None, 'tensor'), may hold values from -200 to 200
- parent_owner: int32 [128], replicated, may hold values from 0 to 15, as said below
- parent_pages: int32 [128], replicated, may hold values from 1 to 5
- page_table: int32 [128, 5], replicated, may hold values from 0 to 39, as said below
- child_parent: int32 [1024], replicated, may hold values from 0 to 127, as said below
Outputs:
- attn_out: bfloat16 [4096, 8192], P('sample', 'tensor')
Inputs may be any that keep to these rules, and one draw needn't show every extreme that they name: `parent_owner`: every index of sample holds the pages of exactly 8 parents. `page_table`: entries are pages of the owner's pool; all 5 entries of all parents of one owner are distinct. `child_parent`: every parent is named by exactly 8 children.
All inputs are finite; a program needn't handle non-finite values.
Results may differ from a plain program's by a relative error of at most 0.007.
The roundings to bfloat16 on the way count: a program that leaves them out, or rounds other values in their place, can miss the bound.
Values may be sent and summed in bfloat16 or wider, within the bound.
No kernel may reach another device: no remote copies, remote signals or barrier semaphores. Data moves between devices by JAX's collectives and lax.ppermute only.
A program may use at most 192 MiB of HBM per device.

v0:
```python
import functools
import math

import jax
import jax.numpy as jnp
from jax import lax
from jax.experimental import pallas as pl
from jax.experimental.pallas import tpu as pltpu
from jax.sharding import PartitionSpec as P

HEAD = 128
PAGE = 128
STEPS = 4
FORK = 8
PARENTS_HERE = 8
MOST_PAGES = 5
ROPE_THETA = 10000.0
EPSILON = 1e-06
SLOTS = 10

BF16 = jnp.bfloat16
F32 = jnp.float32


def iota(shape, dim):
    return lax.broadcasted_iota(jnp.int32, shape, dim)


def one(mask):
    return jnp.where(mask, 1.0, 0.0).astype(BF16)


def mm(a, b):
    return lax.dot_general(a, b, (((1,), (0,)), ((), ())), preferred_element_type=F32)


def mm_nt(a, b):
    return lax.dot_general(a, b, (((1,), (1,)), ((), ())), preferred_element_type=F32)


def mm_tn(a, b):
    return lax.dot_general(a, b, (((0,), (0,)), ((), ())), preferred_element_type=F32)


def leave_kernel(slots, me_ref, child_ref, owner_ref, own_ref, other_ref, fits_ref, mask_ref):
    groups = mask_ref.shape[0]
    me = me_ref[0]
    core = lax.rem(me, 2)
    children = child_ref.shape[1]
    parents = owner_ref.shape[1]
    rows = own_ref.shape[1]
    here = rows // STEPS
    parent_hot = one(iota((parents, children), 0) == child_ref[...])
    owner = jnp.broadcast_to(owner_ref[...].astype(F32), (16, parents)).astype(BF16)
    owner_of = mm(owner, parent_hot)[0:1].astype(jnp.int32)
    mask = jnp.where(iota((groups, children), 0) == owner_of, 1.0, 0.0)
    mask_ref[...] = mask
    counted = iota((children, 128), 1) == iota((children, 128), 0) // (2 * here)
    most = jnp.max(mm(mask.astype(BF16), one(counted))).astype(jnp.int32)
    fits_ref[0] = jnp.where(most <= 2 * slots, 1, 0)

    chip = lax.div(me, 2)
    mask = mask_ref[:, pl.ds(pl.multiple_of(chip * 2 * here, 2 * here), 2 * here)]
    ahead = mm(mask.astype(BF16), one(iota((128, 128), 0) < iota((128, 128), 1)))
    rank = jnp.sum(mask * ahead, axis=0, keepdims=True).astype(jnp.int32)
    owner = jnp.sum(mask * iota(mask.shape, 0).astype(F32), axis=0, keepdims=True)
    keep = jnp.where(rank % 2 == core, 1.0, 0.0)
    turn = (rank // 2).astype(F32)
    at = iota((16, 2 * here), 0)
    facts = jnp.where(at == 0, owner, jnp.where(at == 1, turn, keep)).astype(BF16)
    for ref, side in ((own_ref, core), (other_ref, 1 - core)):
        grow = one(iota((2 * here, rows), 0) == side * here + iota((2 * here, rows), 1) // STEPS)
        of_row = mm(facts, grow)
        target = of_row[0:1] * (slots * STEPS) + of_row[1:2] * STEPS
        target = target.astype(jnp.int32) + iota((1, rows), 1) % STEPS
        target = jnp.where(of_row[2:3] > 0.5, target, -1)
        ref[...] = one(iota(ref.shape, 0) == target)


def leave(slots, groups, me, child_parent, parent_owner, rows):
    vmem = pl.BlockSpec(memory_space=pltpu.VMEM)
    smem = pl.BlockSpec(memory_space=pltpu.SMEM)
    hot = jax.ShapeDtypeStruct((groups * slots * STEPS, rows), BF16)
    return pl.pallas_call(
        functools.partial(leave_kernel, slots),
        out_shape=(hot, hot, jax.ShapeDtypeStruct((1,), jnp.int32)),
        in_specs=[smem, vmem, vmem],
        out_specs=(vmem, vmem, smem),
        scratch_shapes=[pltpu.VMEM((groups, child_parent.shape[0]), F32)],
        compiler_params=pltpu.CompilerParams(vmem_limit_bytes=32 * 2**20),
        cost_estimate=pl.CostEstimate(flops=10**9, bytes_accessed=2**20, transcendentals=0),
    )(me, child_parent.reshape(1, -1), parent_owner.reshape(1, -1))


def arrive_kernel(
    slots, me_ref, child_ref, owner_ref, pages_ref, table_ref, from_ref, info_ref
):
    me = me_ref[0]
    children = child_ref.shape[1]
    parents = owner_ref.shape[1]
    rows, wide = from_ref.shape
    here = rows // STEPS
    deep = wide // STEPS
    owner = owner_ref[...]
    parent_hot = one(iota((parents, children), 0) == child_ref[...])
    mine_parent = owner == me
    tri = one(iota((128, 128), 0) < iota((128, 128), 1))
    parent_rank = mm(one(jnp.broadcast_to(mine_parent, (16, parents))), tri)
    parent_rank = parent_rank[0:1].astype(jnp.int32)
    mine_hot = (iota((PARENTS_HERE, parents), 0) == parent_rank) & mine_parent
    pages = jnp.sum(jnp.where(mine_hot, pages_ref[...], 0), axis=1, keepdims=True)
    mine_hot = one(mine_hot)
    table = mm(mine_hot, table_ref[...].astype(F32).astype(BF16)).astype(jnp.int32)
    info_ref[...] = jnp.where(iota((PARENTS_HERE, 8), 1) == MOST_PAGES, pages, table)
    member = mm(mine_hot, parent_hot)
    carry = jnp.zeros((PARENTS_HERE, 1), F32)
    places, spots = [], []
    for block in range(children // 128):
        part = member[:, block * 128 : (block + 1) * 128]
        ahead = mm(part.astype(BF16), tri) + carry
        carry = carry + jnp.sum(part, axis=1, keepdims=True)
        is_mine = jnp.sum(part, axis=0, keepdims=True)
        place = jnp.sum(
            part * (iota((PARENTS_HERE, 128), 0).astype(F32) * FORK + ahead), axis=0, keepdims=True
        ).astype(jnp.int32)
        in_chip = mm(jnp.broadcast_to(is_mine, (16, 128)).astype(BF16), tri)[0:1].astype(jnp.int32)
        chip = (block * 128 + iota((1, 128), 1)) // (2 * here)
        spot = (chip * 2 + in_chip % 2) * slots + in_chip // 2
        places.append(jnp.where(is_mine > 0.5, place, -1))
        spots.append(jnp.where(is_mine > 0.5, spot, -1))
    place_hot = one(iota((here, children), 0) == jnp.concatenate(places, axis=1))
    spot_hot = one(iota((deep, children), 0) == jnp.concatenate(spots, axis=1))
    by_child = mm_nt(place_hot, spot_hot).astype(BF16)
    grow_rows = one(iota((rows, here), 0) // STEPS == iota((rows, here), 1))
    grow_columns = one(iota((deep, wide), 0) == iota((deep, wide), 1) // STEPS)
    by_row = mm(mm(grow_rows, by_child).astype(BF16), grow_columns)
    same_step = iota((rows, wide), 0) % STEPS == iota((rows, wide), 1) % STEPS
    from_ref[...] = jnp.where(same_step, by_row, 0.0).astype(BF16)


def arrive(slots, groups, me, child_parent, parent_owner, parent_pages, page_table, rows):
    vmem = pl.BlockSpec(memory_space=pltpu.VMEM)
    smem = pl.BlockSpec(memory_space=pltpu.SMEM)
    return pl.pallas_call(
        functools.partial(arrive_kernel, slots),
        out_shape=(
            jax.ShapeDtypeStruct((rows, groups * slots * STEPS), BF16),
            jax.ShapeDtypeStruct((PARENTS_HERE, 8), jnp.int32),
        ),
        in_specs=[smem] + [vmem] * 4,
        out_specs=(vmem, vmem),
        compiler_params=pltpu.CompilerParams(vmem_limit_bytes=32 * 2**20),
        cost_estimate=pl.CostEstimate(flops=2 * 10**9, bytes_accessed=2**20, transcendentals=0),
    )(
        me,
        child_parent.reshape(1, -1),
        parent_owner.reshape(1, -1),
        parent_pages.reshape(1, -1),
        jnp.pad(page_table, ((0, 0), (0, 8 - page_table.shape[1]))),
    )


def fill_kernel(own_hot_ref, other_hot_ref, own_ref, other_ref, out_ref):
    filled = mm(own_hot_ref[...], own_ref[...]) + mm(other_hot_ref[...], other_ref[...])
    out_ref[...] = filled.astype(BF16)


def fill_slots(own_hot, other_hot, own, other):
    vmem = pl.BlockSpec(memory_space=pltpu.VMEM)
    return pl.pallas_call(
        fill_kernel,
        out_shape=jax.ShapeDtypeStruct((own_hot.shape[0], own.shape[1]), BF16),
        in_specs=[vmem] * 4,
        out_specs=vmem,
        compiler_params=pltpu.CompilerParams(vmem_limit_bytes=48 * 2**20),
    )(own_hot, other_hot, own, other)


def fetch(from_ref, held_ref, sems):
    parts = sems.shape[0]
    deep = held_ref.shape[0] // parts
    copies = []
    for i in range(parts):
        cut = pl.ds(i * deep, deep)
        copies.append(pltpu.make_async_copy(from_ref.at[cut], held_ref.at[cut], sems.at[i]))
        copies[-1].start()
    return copies


def settle_kernel(own_hot_ref, other_hot_ref, rows_ref, own_ref, other_ref, held_ref, sems):
    for copy in fetch(rows_ref, held_ref, sems):
        copy.wait()
    rows = held_ref[...]
    other_ref[...] = mm_tn(other_hot_ref[...], rows).astype(BF16)
    own_ref[...] = mm_tn(own_hot_ref[...], rows).astype(BF16)


def settle(own_hot, other_hot, rows):
    vmem = pl.BlockSpec(memory_space=pltpu.VMEM)
    out = jax.ShapeDtypeStruct((own_hot.shape[1], rows.shape[1]), BF16)
    return pl.pallas_call(
        settle_kernel,
        out_shape=(out, out),
        in_specs=[vmem, vmem, pl.BlockSpec(memory_space=pltpu.HBM)],
        out_specs=(vmem, vmem),
        scratch_shapes=[pltpu.VMEM(rows.shape, BF16), pltpu.SemaphoreType.DMA((2,))],
        compiler_params=pltpu.CompilerParams(vmem_limit_bytes=32 * 2**20),
    )(own_hot, other_hot, rows)


def pick_sum_kernel(hot_ref, rows_ref, out_ref, sum_ref, held_ref, sems):
    x = jnp.zeros(out_ref.shape, F32)
    deep = held_ref.shape[0] // sems.shape[0]
    for i, copy in enumerate(fetch(rows_ref, held_ref, sems)):
        copy.wait()
        cut = slice(i * deep, (i + 1) * deep)
        x = x + mm(hot_ref[:, cut], held_ref[cut])
    out_ref[...] = x.astype(BF16)
    total = jnp.sum(x * x, axis=1, keepdims=True)
    total = jnp.broadcast_to(total, (total.shape[0], 128)).T
    sum_ref[...] = jnp.broadcast_to(total[0:1], sum_ref.shape[:1] + total.shape[1:])[:, None, :]


def pick_and_sum(hot, rows, copies):
    vmem = pl.BlockSpec(memory_space=pltpu.VMEM)
    count = hot.shape[0]
    return pl.pallas_call(
        pick_sum_kernel,
        out_shape=(
            jax.ShapeDtypeStruct((count, rows.shape[1]), BF16),
            jax.ShapeDtypeStruct((copies, 1, count), F32),
        ),
        in_specs=[vmem, pl.BlockSpec(memory_space=pltpu.HBM)],
        out_specs=(vmem, vmem),
        scratch_shapes=[pltpu.VMEM(rows.shape, BF16), pltpu.SemaphoreType.DMA((2,))],
        compiler_params=pltpu.CompilerParams(vmem_limit_bytes=48 * 2**20),
    )(hot, rows)


def row_scale(sum_ref, width):
    total = jnp.sum(sum_ref[:, 0, :], axis=0, keepdims=True)
    scale = lax.rsqrt(total * (1.0 / width) + EPSILON)
    return jnp.broadcast_to(scale, (128, scale.shape[1])).T


def normed(x, scale, gain):
    return (x.astype(F32) * scale * gain.astype(F32)).astype(BF16)


def add_products(acc, x, wq_ref, wk_ref, wv_ref, wkv_ref):
    wide = wq_ref.shape[1]
    wkv_ref[:, :HEAD] = wk_ref[...]
    wkv_ref[:, HEAD:] = wv_ref[...]
    acc[:, :wide] += mm(x, wq_ref[...])
    acc[:, wide:] += mm(x, wkv_ref[...])


def project_kernel(width, count, first, order_ref, sum_ref, *refs):
    blocks = refs[:count]
    gain_ref, wq_ref, wk_ref, wv_ref = refs[count : count + 4]
    before = None if first else refs[count + 4]
    acc_ref, x_ref, scale_ref, wkv_ref = refs[-4:]
    step = pl.program_id(0)

    @pl.when(step == 0)
    def _():
        scale_ref[...] = row_scale(sum_ref, width)
        acc_ref[...] = jnp.zeros_like(acc_ref) if first else before[...]

    for i, block in enumerate(blocks):

        @pl.when(step == i)
        def _(block=block):
            x_ref[...] = normed(block[...], scale_ref[:, 0:1], gain_ref[0])

    add_products(acc_ref, x_ref[...], wq_ref, wk_ref, wv_ref, wkv_ref)


def project(order, sums, blocks, gain, wq, wk, wv, before=None):
    rows, part = blocks[0].shape
    columns = wq.shape[1] + wk.shape[1] + wv.shape[1]
    count = len(blocks)

    def whole(a):
        return pl.BlockSpec(a.shape, lambda i, order: (0,) * a.ndim)

    extra = [] if before is None else [before]
    return pl.pallas_call(
        functools.partial(project_kernel, wq.shape[0], count, before is None),
        out_shape=jax.ShapeDtypeStruct((rows, columns), F32),
        grid_spec=pltpu.PrefetchScalarGridSpec(
            num_scalar_prefetch=1,
            grid=(count,),
            in_specs=[whole(sums)]
            + [whole(b) for b in blocks]
            + [pl.BlockSpec((1, 1, part), lambda i, order: (order[i], 0, 0))]
            + [
                pl.BlockSpec((part, w.shape[1]), lambda i, order: (order[i], 0))
                for w in (wq, wk, wv)
            ]
            + [whole(a) for a in extra],
            out_specs=pl.BlockSpec((rows, columns), lambda i, order: (0, 0)),
            scratch_shapes=[
                pltpu.VMEM((rows, part), BF16),
                pltpu.VMEM((rows, 128), F32),
                pltpu.VMEM((part, 2 * HEAD), BF16),
            ],
        ),
        compiler_params=pltpu.CompilerParams(vmem_limit_bytes=32 * 2**20),
        cost_estimate=pl.CostEstimate(
            flops=2 * rows * part * count * columns * 3,
            bytes_accessed=2 * part * count * columns,
            transcendentals=0,
        ),
    )(order, sums, *blocks, gain, wq, wk, wv, *extra)


def attend_kernel(
    width,
    info_ref,
    sum_ref,
    low_ref,
    high_ref,
    gain_ref,
    wq_ref,
    wk_ref,
    wv_ref,
    before_ref,
    cos_ref,
    sin_ref,
    pool_ref,
    back_ref,
    out_ref,
    acc_ref,
    x_ref,
    wkv_ref,
    q_ref,
    k_ref,
    v_ref,
    o_ref,
):
    scale = row_scale(sum_ref, width)[:, 0:1]
    half = low_ref.shape[0]
    x_ref[:half] = normed(low_ref[...], scale[:half], gain_ref[...])
    x_ref[half:] = normed(high_ref[...], scale[half:], gain_ref[...])
    acc_ref[...] = before_ref[...]
    add_products(acc_ref, x_ref[...], wq_ref, wk_ref, wv_ref, wkv_ref)

    cos = cos_ref[...]
    sin = sin_ref[...]

    def turn(part):
        return (part * cos + pltpu.roll(part, HEAD // 2, 1) * sin).astype(BF16)

    heads = wq_ref.shape[1] // HEAD
    for h in range(heads):
        cut = slice(h * HEAD, (h + 1) * HEAD)
        q_ref[:, cut] = turn(acc_ref[:, cut])
    k_ref[...] = turn(acc_ref[:, heads * HEAD : (heads + 1) * HEAD])
    v_ref[...] = acc_ref[:, (heads + 1) * HEAD :].astype(BF16)

    family = FORK * STEPS
    scale = 1.0 / math.sqrt(HEAD)
    row_at = iota((heads * family, family), 0) % family
    key_at = iota((heads * family, family), 1)
    own_mask = (row_at // STEPS == key_at // STEPS) & (row_at >= key_at)

    @pl.loop(0, PARENTS_HERE)
    def _(j):
        at = pl.ds(pl.multiple_of(j * family, family), family)
        q = jnp.concatenate([q_ref[at, h * HEAD : (h + 1) * HEAD] for h in range(heads)], axis=0)
        own = jnp.where(own_mask, mm_nt(q, k_ref[at, :]) * scale, -jnp.inf)
        own_top = jnp.max(own, axis=1, keepdims=True)
        own_weight = jnp.exp(own - own_top)
        own_total = jnp.sum(own_weight, axis=1, keepdims=True)
        own_mix = mm(own_weight.astype(BF16), v_ref[at, :])
        length = info_ref[j, MOST_PAGES]
        for n in range(1, MOST_PAGES + 1):

            @pl.when(length == n)
            def _(n=n):
                ids = [info_ref[j, i] for i in range(n)]
                keys = jnp.concatenate([pool_ref[i, 0] for i in ids], axis=0)
                values = jnp.concatenate([pool_ref[i, 1] for i in ids], axis=0)
                path = mm_nt(q, keys) * scale
                path_top = jnp.max(path, axis=1, keepdims=True)
                weight = jnp.exp(path - path_top)
                path_total = jnp.sum(weight, axis=1, keepdims=True)
                path_mix = mm(weight.astype(BF16), values)
                top = jnp.maximum(path_top, own_top)
                path_factor = jnp.exp(path_top - top)
                own_factor = jnp.exp(own_top - top)
                both = path_mix * path_factor + own_mix * own_factor
                out = both / (path_total * path_factor + own_total * own_factor)
                out = out.astype(BF16)
                for h in range(heads):
                    o_ref[at, h * HEAD : (h + 1) * HEAD] = out[h * family : (h + 1) * family]

    out_ref[...] = mm_tn(back_ref[...], o_ref[...]).astype(BF16)


def attend(info, sums, low, high, gain, wq, wk, wv, before, cos, sin, pool, back):
    rows, columns = before.shape
    part = low.shape[1]
    wide = back.shape[1]
    vmem = pl.BlockSpec(memory_space=pltpu.VMEM)
    smem = pl.BlockSpec(memory_space=pltpu.SMEM)
    return pl.pallas_call(
        functools.partial(attend_kernel, 8 * part),
        out_shape=jax.ShapeDtypeStruct((wide, wq.shape[1]), BF16),
        in_specs=[smem] + [vmem] * 12,
        out_specs=vmem,
        scratch_shapes=[
            pltpu.VMEM((rows, columns), F32),
            pltpu.VMEM((rows, part), BF16),
            pltpu.VMEM((part, 2 * HEAD), BF16),
            pltpu.VMEM((rows, wq.shape[1]), BF16),
            pltpu.VMEM((rows, HEAD), BF16),
            pltpu.VMEM((rows, HEAD), BF16),
            pltpu.VMEM((rows, wq.shape[1]), BF16),
        ],
        compiler_params=pltpu.CompilerParams(vmem_limit_bytes=32 * 2**20),
        cost_estimate=pl.CostEstimate(
            flops=2 * rows * part * columns * 6, bytes_accessed=2 * part * columns, transcendentals=0
        ),
    )(info, sums, low, high, gain, wq, wk, wv, before, cos, sin, pool, back)


def moves(dy, dz):
    return [(t, ((t // 2 + dy) % 4) * 2 + (t + dz) % 2) for t in range(8)]


def after_leave(slots, groups, me, tables, arrays, send, own_hot, other_hot):
    (norm_gain, wq, wk, wv, kv_pool) = arrays
    wide, width = send.shape
    rows = PARENTS_HERE * FORK * STEPS
    team = lax.axis_size("tensor")
    t = lax.axis_index("tensor")
    came = lax.all_to_all(send.reshape(groups, wide // groups, width), "sample", 0, 0)
    from_hot, info = arrive(slots, groups, me, *tables, rows)

    def place(dy, dz):
        return ((t // 2 + dy) % 4) * 2 + (t + dz) % 2

    def order(*keys):
        return jnp.stack([place(*key) for key in keys]).astype(jnp.int32)

    last = [lax.dynamic_slice_in_dim(w, place(2, 1) * width, width) for w in (wq, wk, wv)]
    gain = norm_gain.reshape(team, 1, -1)
    last_gain = lax.dynamic_slice_in_dim(norm_gain, place(2, 1) * width, width).reshape(1, -1)

    pages = info[:, MOST_PAGES]
    positions = (
        jnp.repeat(pages * PAGE, FORK * STEPS)
        + jnp.tile(jnp.arange(STEPS, dtype=jnp.int32), PARENTS_HERE * FORK)
    ).astype(F32)
    inverse = ROPE_THETA ** (-2.0 * jnp.arange(HEAD // 2, dtype=F32) / HEAD)
    angles = positions[:, None] * inverse[None, :]
    cos, sin = jnp.cos(angles), jnp.sin(angles)
    cos = jnp.concatenate([cos, cos], axis=1)
    sin = jnp.concatenate([-sin, sin], axis=1)
    came, from_hot, info, cos, sin, gain, last_gain, *last = lax.optimization_barrier(
        (came, from_hot, info, cos, sin, gain, last_gain, *last)
    )
    mine, sums = pick_and_sum(from_hot, came.reshape(wide, width), team)

    def shift(block, dy, dz):
        return lax.ppermute(block, "tensor", moves(dy, dz))

    sums = lax.all_to_all(sums, "tensor", 0, 0)
    b30, b10, b01 = shift(mine, 1, 0), shift(mine, -1, 0), shift(mine, 0, 1)
    (b30,) = lax.optimization_barrier((b30,))
    b20, b31 = shift(b30, 1, 0), shift(b30, 0, 1)
    b10, b01 = lax.optimization_barrier((b10, b01))
    second = (b20, shift(b01, -1, 0), b31)
    acc = project(
        order((0, 0), (3, 0), (1, 0), (0, 1)), sums, [mine, b30, b10, b01], gain, wq, wk, wv
    )
    b20, b11, b31, acc = lax.optimization_barrier((*second, acc))
    half = rows // 2
    low, high = shift(b31[:half], 1, 0), shift(b11[half:], -1, 0)
    acc = project(order((2, 0), (1, 1), (3, 1)), sums, [b20, b11, b31], gain, wq, wk, wv, acc)
    low, high, acc = lax.optimization_barrier((low, high, acc))
    back = attend(
        info, sums, low, high, last_gain, *last, acc, cos, sin, kv_pool, from_hot
    )
    home = lax.all_to_all(back.reshape(groups, -1, back.shape[1]), "sample", 0, 0)
    own, other = settle(own_hot, other_hot, home.reshape(-1, back.shape[1]))
    return own + lax.ppermute(other, "sample", swap(groups))


def swap(groups):
    return [(i, i ^ 1) for i in range(groups)]


def local(
    branch_tokens,
    norm_gain,
    query_weight,
    key_weight,
    value_weight,
    kv_pool,
    parent_owner,
    parent_pages,
    page_table,
    child_parent,
):
    groups = lax.axis_size("sample")
    rows = branch_tokens.shape[0]
    me = lax.axis_index("sample").astype(jnp.int32).reshape(1)
    tables = (child_parent, parent_owner, parent_pages, page_table)
    arrays = (norm_gain, query_weight, key_weight, value_weight, kv_pool)
    other = lax.ppermute(branch_tokens, "sample", swap(groups))
    own_hot, other_hot, fits = leave(SLOTS, groups, me, *tables[:2], rows)
    other, own_hot, other_hot, fits = lax.optimization_barrier((other, own_hot, other_hot, fits))
    send = fill_slots(own_hot, other_hot, branch_tokens, other)

    def usual():
        return after_leave(SLOTS, groups, me, tables, arrays, send, own_hot, other_hot)

    def crowded():
        most = rows // STEPS // 2
        own, others, _ = leave(most, groups, me, *tables[:2], rows)
        wider = fill_slots(own, others, branch_tokens, other)
        return after_leave(most, groups, me, tables, arrays, wider, own, others)

    return lax.cond(fits[0] == 1, usual, crowded)


def solution(mesh):
    return jax.shard_map(
        local,
        mesh=mesh,
        in_specs=(
            P("sample", "tensor"),
            P(),
            P(None, "tensor"),
            P(None, "tensor"),
            P(None, "tensor"),
            P("sample", None, None, "tensor"),
            P(),
            P(),
            P(),
            P(),
        ),
        out_specs=P("sample", "tensor"),
        check_vma=False,
    )
```

profile of v0, /device:TPU:1, one launch (start us, length us, event | category | flops | bytes accessed | tf_op | source)
XLA Modules:
  0.0 114.4 jit_solution(16085259459089384093)
XLA Ops:
  0.0 1.4 %collective-permute-start.18 = (bf16[256,1024]{1,0:T(8,128)(2,1)}, bf16[256,1024]{1,0:T(8,128)(2,1)S(1)}, u32[]{:S(2)}, u32[]{:S(2)}) collective-permute-start(bf16[256,1024]{1,0:T(8,128)(2,1)} %own_ref.1), channel_id=1, source_target_pairs={{0,8},{8,0},{16,24},{24,16},{32,40},{40,32},{48,56},{56,48},{64,72... | collective-permute-start | bytes 1572872 | tf_op jit(solution)/shard_map/ppermute | solution.py:513
  1.4 2.1 %shard_map.102 = (bf16[640,256]{1,0:T(8,128)(2,1)}, bf16[640,256]{1,0:T(8,128)(2,1)}, s32[1]{0:T(128)}) custom-call(s32[1]{0:T(128)} %bitcast.28.me_ref, s32[1,1024]{1,0:T(1,128)} %bitcast.39, s32[1,128]{1,0:T(1,128)} %bitcast.43), custom_call_target="tpu_custom_call" | custom-call | flops 1000000000 | bytes 1048576 | tf_op jit(solution)/shard_map/pallas_call | solution.py:84
  3.6 0.0 copy-start.25
  3.6 0.0 copy-start.26
  3.6 0.0 copy-start.28
  3.6 0.0 copy-start.29
  3.6 0.0 copy-start.30
  3.6 0.0 collective-permute-done.18.other_ref
  4.3 0.0 copy-done.23
  4.3 3.0 %shard_map.103 = bf16[640,1024]{1,0:T(8,128)(2,1)} custom-call(bf16[640,256]{1,0:T(8,128)(2,1)} %get-tuple-element.147.own_hot_ref, bf16[640,256]{1,0:T(8,128)(2,1)} %get-tuple-element.148.other_hot_ref, bf16[256,1024]{1,0:T(8,128)(2,1)S(1)} %copy-done.23, bf16[256,1024]{1,0:T(8,128)(2,1)S(1)} %collective-permute-done.18.other_ref), custom_call_target="tpu_custom_call" | custom-call | tf_op jit(solution)/shard_map/pallas_call | solution.py:170
  7.3 0.0 copy-done.25
  7.3 0.0 copy-done.26
  7.3 0.0 copy-done.28
  7.3 106.3 %conditional.1 = (bf16[256,1024]{1,0:T(8,128)(2,1)S(1)}) conditional(s32[]{:T(128)} %bitcast.31, (s32[1024]{0:T(1024)S(1)}, s32[128]{0:T(128)S(1)}, s32[1]{0:T(128)}, bf16[256,1024]{1,0:T(8,128)(2,1)S(1)}, bf16[256,1024]{1,0:T(8,128)(2,1)S(1)}, /*index=5*/s32[128]{0:T(128)S(1)}, s32[128,5]{0,1:T(8,128)S(1)}, bf16[8192]{0:T(1024)(128)(2,1)S(1)}, ...), branch_computations={%region_0.1_spmd, %region_1.2_spmd} | conditional | flops 21119754240 | bytes 176414560 | solution.py:527
  7.6 5.9 %all-to-all-start.3 = ((bf16[16,40,1024]{2,1,0:T(8,128)(2,1)}), bf16[16,40,1024]{2,1,0:T(8,128)(2,1)S(1)}, u32[]{:S(2)}, u32[]{:S(2)}) async-start(bf16[16,40,1024]{2,1,0:T(8,128)(2,1)} %bitcast.38), calls=%async_computation.3 | async-start | bytes 2621440 | tf_op jit(solution)/shard_map/cond/branch_1_fun/all_to_all | solution.py:439
  13.5 0.1 copy.20
  13.6 1.1 branch_1_fun.6
  14.7 0.0 copy-start.3
  14.7 0.7 copy-done.3
  15.5 0.2 multiply_reduce_fusion.1
  15.6 0.1 broadcast_in_dim.6
  15.7 0.1 reshape.100
  15.8 0.1 tile.12
  16.0 0.5 fusion.1
  16.6 0.9 pad_maximum_fusion.2
  17.4 1.9 %constant_dynamic-slice_fusion.3 = (bf16[1024,128]{1,0:T(8,128)(2,1)}, bf16[1024,128]{1,0:T(8,128)(2,1)}) fusion(bf16[8192,128]{1,0:T(8,128)(2,1)} %get-tuple-element.110.refs_7_.refs_6_, s32[]{:T(128)S(6)} %select_n.149, bf16[8192,128]{1,0:T(8,128)(2,1)} %get-tuple-element.109.refs_6_.refs_5_), kind=kLoop, calls=%fused_computation.20 | loop fusion | bytes 1048580 | tf_op jit(solution)/shard_map/cond/branch_1_fun/dynamic_slice | solution.py:448
  19.3 1.8 %constant_dynamic-slice_fusion.5.wq_ref = bf16[1024,1024]{1,0:T(8,128)(2,1)S(1)} fusion(bf16[8192,1024]{1,0:T(8,128)(2,1)} %get-tuple-element.108.refs_5_.refs_4_, s32[]{:T(128)S(6)} %select_n.149), kind=kLoop, calls=%fused_computation.22 | loop fusion | bytes 4194308 | tf_op jit(solution)/shard_map/cond/branch_1_fun/dynamic_slice | solution.py:448
  21.1 11.1 %all-to-all-done.3 = bf16[16,40,1024]{2,1,0:T(8,128)(2,1)S(1)} async-done(((bf16[16,40,1024]{2,1,0:T(8,128)(2,1)}), bf16[16,40,1024]{2,1,0:T(8,128)(2,1)S(1)}, u32[]{:S(2)}, u32[]{:S(2)}) %all-to-all-start.3) | async-done | bytes 1310752 | tf_op jit(solution)/shard_map/cond/branch_1_fun/all_to_all | solution.py:439
  32.1 1.0 copy-done.4
  33.1 2.0 %branch_1_fun.7 = (bf16[256,1024]{1,0:T(8,128)(2,1)}, f32[8,1,256]{2,1,0:T(1,128)}) custom-call(bf16[256,640]{1,0:T(8,128)(2,1)S(1)} %copy-done.4, bf16[640,1024]{1,0:T(8,128)(2,1)S(1)} %bitcast.33), custom_call_target="tpu_custom_call" | custom-call | tf_op jit(solution)/shard_map/cond/branch_1_fun/pallas_call | solution.py:227
  35.1 1.4 %collective-permute-start.9 = (bf16[256,1024]{1,0:T(8,128)(2,1)}, bf16[256,1024]{1,0:T(8,128)(2,1)}, u32[]{:S(2)}, u32[]{:S(2)}) collective-permute-start(bf16[256,1024]{1,0:T(8,128)(2,1)} %get-tuple-element.115.refs_0_), channel_id=1, source_target_pairs={{0,2},{1,3},{2,4},{3,5},{4,6},{5,7},{6,0},{7,1},{8,10},{9,11},{10,... | collective-permute-start | bytes 1572872 | tf_op jit(solution)/shard_map/cond/branch_1_fun/ppermute | solution.py:468
  36.5 1.5 %collective-permute-start.11 = (bf16[256,1024]{1,0:T(8,128)(2,1)}, bf16[256,1024]{1,0:T(8,128)(2,1)S(1)}, u32[]{:S(2)}, u32[]{:S(2)}) collective-permute-start(bf16[256,1024]{1,0:T(8,128)(2,1)} %get-tuple-element.115.refs_0_), channel_id=1, source_target_pairs={{0,6},{1,7},{2,0},{3,1},{4,2},{5,3},{6,4},{7,5},{8,14},{9,15},{10,... | collective-permute-start | bytes 1572872 | tf_op jit(solution)/shard_map/cond/branch_1_fun/ppermute | solution.py:468
  38.0 3.3 %collective-permute-start.12 = (bf16[256,1024]{1,0:T(8,128)(2,1)}, bf16[256,1024]{1,0:T(8,128)(2,1)}, u32[]{:S(2)}, u32[]{:S(2)}) collective-permute-start(bf16[256,1024]{1,0:T(8,128)(2,1)} %get-tuple-element.115.refs_0_), channel_id=1, source_target_pairs={{0,1},{1,0},{2,3},{3,2},{4,5},{5,4},{6,7},{7,6},{8,9},{9,8},{10,11... | collective-permute-start | bytes 1572872 | tf_op jit(solution)/shard_map/cond/branch_1_fun/ppermute | solution.py:468
  41.3 0.1 pad_add_fusion.3.order_ref
  41.4 3.3 %all-to-all-start.4 = ((f32[8,1,256]{2,1,0:T(1,128)}), f32[8,1,256]{2,1,0:T(1,128)S(1)}, u32[]{:S(2)}, u32[]{:S(2)}) async-start(f32[8,1,256]{2,1,0:T(1,128)} %get-tuple-element.114), calls=%async_computation.4 | async-start | bytes 16384 | tf_op jit(solution)/shard_map/cond/branch_1_fun/all_to_all | solution.py:470
  44.7 0.1 pad_add_fusion.2.order_ref
  44.9 4.7 %collective-permute-done.9.refs_1_ = bf16[256,1024]{1,0:T(8,128)(2,1)} collective-permute-done((bf16[256,1024]{1,0:T(8,128)(2,1)}, bf16[256,1024]{1,0:T(8,128)(2,1)}, u32[]{:S(2)}, u32[]{:S(2)}) %collective-permute-start.9) | collective-permute-done | bytes 524320 | tf_op jit(solution)/shard_map/cond/branch_1_fun/ppermute | solution.py:468
  49.6 0.0 collective-permute-start.10
  49.6 3.3 %collective-permute-start.14 = (bf16[256,1024]{1,0:T(8,128)(2,1)}, bf16[256,1024]{1,0:T(8,128)(2,1)S(1)}, u32[]{:S(2)}, u32[]{:S(2)}) collective-permute-start(bf16[256,1024]{1,0:T(8,128)(2,1)} %collective-permute-done.9.refs_1_), channel_id=1, source_target_pairs={{0,1},{1,0},{2,3},{3,2},{4,5},{5,4},{6,7},{7,6},{8,9},{9,8},{10,11... | collective-permute-start | bytes 1572872 | tf_op jit(solution)/shard_map/cond/branch_1_fun/ppermute | solution.py:468
  52.9 0.0 collective-permute-done.11.refs_2_
  52.9 0.8 copy-done.15
  53.7 0.0 collective-permute-done.12.refs_3_
  53.7 2.7 %collective-permute-start.13 = (bf16[256,1024]{1,0:T(8,128)(2,1)}, bf16[256,1024]{1,0:T(8,128)(2,1)S(1)}, u32[]{:S(2)}, u32[]{:S(2)}) collective-permute-start(bf16[256,1024]{1,0:T(8,128)(2,1)} %collective-permute-done.12.refs_3_), channel_id=1, source_target_pairs={{0,6},{1,7},{2,0},{3,1},{4,2},{5,3},{6,4},{7,5},{8,14},{9,15},{10,... | collective-permute-start | bytes 1572872 | tf_op jit(solution)/shard_map/cond/branch_1_fun/ppermute | solution.py:468
  56.4 0.0 all-to-all-done.4.sum_ref
  56.4 1.0 copy-done.16
  57.4 9.0 %branch_1_fun.8.refs_7_ = f32[256,1280]{1,0:T(8,128)S(1)} custom-call(s32[4]{0:T(128)S(1)} %pad_add_fusion.2.order_ref, f32[8,1,256]{2,1,0:T(1,128)S(1)} %all-to-all-done.4.sum_ref, bf16[256,1024]{1,0:T(8,128)(2,1)} %get-tuple-element.115.refs_0_, bf16[256,1024]{1,0:T(8,128)(2,1)} %collective-permute-done.9.refs_1_, bf16[256,1024]{1,0:T(8,128)(2,1)S(1)} %copy-done.16, ...), custom_call_target="tpu_custom_call" | custom-call | flops 8053063680 | bytes 10485760 | tf_op jit(solution)/shard_map/cond/branch_1_fun/pallas_call | solution.py:288
  66.4 0.0 collective-permute-done.10.refs_0_
  66.4 0.0 collective-permute-done.13.refs_1_
  66.4 0.0 collective-permute-done.14.refs_2_
  66.5 0.1 collective-permute-start.15
  66.6 0.0 copy-start.27
  66.7 2.7 %collective-permute-start.16 = (bf16[128,1024]{1,0:T(8,128)(2,1)S(1)}, bf16[128,1024]{1,0:T(8,128)(2,1)S(1)}, u32[]{:S(2)}, u32[]{:S(2)}) collective-permute-start(bf16[128,1024]{1,0:T(8,128)(2,1)S(1)} %slice.17), channel_id=1, source_target_pairs={{0,6},{1,7},{2,0},{3,1},{4,2},{5,3},{6,4},{7,5},{8,14},{9,15},{10,... | collective-permute-start | bytes 786440 | tf_op jit(solution)/shard_map/cond/branch_1_fun/ppermute | solution.py:468
  69.4 0.0 copy-done.18
  69.4 4.9 %branch_1_fun.9.before_ref = f32[256,1280]{1,0:T(8,128)S(1)} custom-call(s32[3]{0:T(128)S(1)} %pad_add_fusion.3.order_ref, f32[8,1,256]{2,1,0:T(1,128)S(1)} %all-to-all-done.4.sum_ref, bf16[256,1024]{1,0:T(8,128)(2,1)} %collective-permute-done.10.refs_0_, bf16[256,1024]{1,0:T(8,128)(2,1)S(1)} %collective-permute-done.13.refs_1_, ...), custom_call_target="tpu_custom_call" | custom-call | flops 6039797760 | bytes 7864320 | tf_op jit(solution)/shard_map/cond/branch_1_fun/pallas_call | solution.py:288
  74.3 0.0 collective-permute-done.15.low_ref
  74.3 0.0 collective-permute-done.16.high_ref
  74.4 9.0 %branch_1_fun.10 = bf16[640,1024]{1,0:T(8,128)(2,1)S(1)} custom-call(s32[8,8]{1,0:T(8,128)S(1)} %get-tuple-element.111.info_ref, f32[8,1,256]{2,1,0:T(1,128)S(1)} %all-to-all-done.4.sum_ref, bf16[128,1024]{1,0:T(8,128)(2,1)S(1)} %collective-permute-done.15.low_ref, bf16[128,1024]{1,0:T(8,128)(2,1)S(1)} %collective-permute-done.16.high_ref, ...), custom_call_target="tpu_custom_call" | custom-call | flops 4026531840 | bytes 2621440 | tf_op jit(solution)/shard_map/cond/branch_1_fun/pallas_call | solution.py:408
  83.4 25.1 %all_to_all.25 = bf16[16,40,1024]{2,1,0:T(8,128)(2,1)S(1)} all-to-all(bf16[16,40,1024]{2,1,0:T(8,128)(2,1)S(1)} %bitcast.36), channel_id=1, replica_groups=mesh['sample'=16,'tensor'=8] {'sample'}, dimensions={0} | all-to-all | bytes 2621440 | tf_op jit(solution)/shard_map/cond/branch_1_fun/all_to_all | solution.py:487
  108.5 2.5 %branch_1_fun.11 = (bf16[256,1024]{1,0:T(8,128)(2,1)S(1)}, bf16[256,1024]{1,0:T(8,128)(2,1)S(1)}) custom-call(bf16[640,256]{1,0:T(8,128)(2,1)} %get-tuple-element.97.own_hot_ref, bf16[640,256]{1,0:T(8,128)(2,1)} %get-tuple-element.98.other_hot_ref, bf16[640,1024]{1,0:T(8,128)(2,1)S(1)} %bitcast.34), custom_call_target="tpu_custom_call" | custom-call | tf_op jit(solution)/shard_map/cond/branch_1_fun/pallas_call | solution.py:201
  111.0 0.9 collective-permute-start.17
  111.9 1.5 %collective-permute-done.17 = bf16[256,1024]{1,0:T(8,128)(2,1)S(1)} collective-permute-done((bf16[256,1024]{1,0:T(8,128)(2,1)S(1)}, bf16[256,1024]{1,0:T(8,128)(2,1)S(1)}, u32[]{:S(2)}, u32[]{:S(2)}) %collective-permute-start.17) | collective-permute-done | bytes 524320 | tf_op jit(solution)/shard_map/cond/branch_1_fun/ppermute | solution.py:489
  113.5 0.2 add.208
  113.6 0.0 copy-start.24
  113.7 0.8 copy-done.24
  (32 shorter events, 0.2 us)
Async XLA Ops:
  0.0 4.3 %copy-start.23 = (bf16[256,1024]{1,0:T(8,128)(2,1)S(1)}, bf16[256,1024]{1,0:T(8,128)(2,1)}, u32[]{:S(2)}) copy-start(bf16[256,1024]{1,0:T(8,128)(2,1)} %own_ref.1) | copy-start | bytes 1572868
  0.0 3.6 %collective-permute-start.18 = (bf16[256,1024]{1,0:T(8,128)(2,1)}, bf16[256,1024]{1,0:T(8,128)(2,1)S(1)}, u32[]{:S(2)}, u32[]{:S(2)}) collective-permute-start(bf16[256,1024]{1,0:T(8,128)(2,1)} %own_ref.1), channel_id=1, source_target_pairs={{0,8},{8,0},{16,24},{24,16},{32,40},{40,32},{48,56},{56,48},{64,72... | collective-permute-start | bytes 1572872 | tf_op jit(solution)/shard_map/ppermute | solution.py:513
  3.6 3.8 %copy-start.25 = (bf16[8192]{0:T(1024)(128)(2,1)S(1)}, bf16[8192]{0:T(1024)(128)(2,1)}, u32[]{:S(2)}) copy-start(bf16[8192]{0:T(1024)(128)(2,1)} %param.13) | copy-start | bytes 49156
  3.6 3.7 %copy-start.26 = (s32[128,5]{0,1:T(8,128)S(1)}, s32[128,5]{0,1:T(8,128)}, u32[]{:S(2)}) copy-start(s32[128,5]{0,1:T(8,128)} %param.20) | copy-start | bytes 7684
  3.6 3.7 %copy-start.28 = (s32[1024]{0:T(1024)S(1)}, s32[1024]{0:T(1024)}, u32[]{:S(2)}) copy-start(s32[1024]{0:T(1024)} %param.21) | copy-start | bytes 12292
  3.6 3.7 %copy-start.29 = (s32[128]{0:T(128)S(1)}, s32[128]{0:T(128)}, u32[]{:S(2)}) copy-start(s32[128]{0:T(128)} %param.18) | copy-start | bytes 1540
  3.6 3.7 %copy-start.30 = (s32[128]{0:T(128)S(1)}, s32[128]{0:T(128)}, u32[]{:S(2)}) copy-start(s32[128]{0:T(128)} %param.19) | copy-start | bytes 1540
  7.6 24.5 %all-to-all-start.3 = ((bf16[16,40,1024]{2,1,0:T(8,128)(2,1)}), bf16[16,40,1024]{2,1,0:T(8,128)(2,1)S(1)}, u32[]{:S(2)}, u32[]{:S(2)}) async-start(bf16[16,40,1024]{2,1,0:T(8,128)(2,1)} %bitcast.38), calls=%async_computation.3 | async-start | bytes 2621440 | tf_op jit(solution)/shard_map/cond/branch_1_fun/all_to_all | solution.py:439
  14.7 0.8 copy-start.3
  32.1 1.0 copy-start.4
  35.1 14.5 %collective-permute-start.9 = (bf16[256,1024]{1,0:T(8,128)(2,1)}, bf16[256,1024]{1,0:T(8,128)(2,1)}, u32[]{:S(2)}, u32[]{:S(2)}) collective-permute-start(bf16[256,1024]{1,0:T(8,128)(2,1)} %get-tuple-element.115.refs_0_), channel_id=1, source_target_pairs={{0,2},{1,3},{2,4},{3,5},{4,6},{5,7},{6,0},{7,1},{8,10},{9,11},{10,... | collective-permute-start | bytes 1572872 | tf_op jit(solution)/shard_map/cond/branch_1_fun/ppermute | solution.py:468
  36.5 16.4 %collective-permute-start.11 = (bf16[256,1024]{1,0:T(8,128)(2,1)}, bf16[256,1024]{1,0:T(8,128)(2,1)S(1)}, u32[]{:S(2)}, u32[]{:S(2)}) collective-permute-start(bf16[256,1024]{1,0:T(8,128)(2,1)} %get-tuple-element.115.refs_0_), channel_id=1, source_target_pairs={{0,6},{1,7},{2,0},{3,1},{4,2},{5,3},{6,4},{7,5},{8,14},{9,15},{10,... | collective-permute-start | bytes 1572872 | tf_op jit(solution)/shard_map/cond/branch_1_fun/ppermute | solution.py:468
  38.0 15.7 %collective-permute-start.12 = (bf16[256,1024]{1,0:T(8,128)(2,1)}, bf16[256,1024]{1,0:T(8,128)(2,1)}, u32[]{:S(2)}, u32[]{:S(2)}) collective-permute-start(bf16[256,1024]{1,0:T(8,128)(2,1)} %get-tuple-element.115.refs_0_), channel_id=1, source_target_pairs={{0,1},{1,0},{2,3},{3,2},{4,5},{5,4},{6,7},{7,6},{8,9},{9,8},{10,11... | collective-permute-start | bytes 1572872 | tf_op jit(solution)/shard_map/cond/branch_1_fun/ppermute | solution.py:468
  41.4 15.0 %all-to-all-start.4 = ((f32[8,1,256]{2,1,0:T(1,128)}), f32[8,1,256]{2,1,0:T(1,128)S(1)}, u32[]{:S(2)}, u32[]{:S(2)}) async-start(f32[8,1,256]{2,1,0:T(1,128)} %get-tuple-element.114), calls=%async_computation.4 | async-start | bytes 16384 | tf_op jit(solution)/shard_map/cond/branch_1_fun/all_to_all | solution.py:470
  49.6 16.8 %collective-permute-start.10 = (bf16[256,1024]{1,0:T(8,128)(2,1)}, bf16[256,1024]{1,0:T(8,128)(2,1)}, u32[]{:S(2)}, u32[]{:S(2)}) collective-permute-start(bf16[256,1024]{1,0:T(8,128)(2,1)} %collective-permute-done.9.refs_1_), channel_id=1, source_target_pairs={{0,2},{1,3},{2,4},{3,5},{4,6},{5,7},{6,0},{7,1},{8,10},{9,11},{10,... | collective-permute-start | bytes 1572872 | tf_op jit(solution)/shard_map/cond/branch_1_fun/ppermute | solution.py:468
  49.6 16.9 %collective-permute-start.14 = (bf16[256,1024]{1,0:T(8,128)(2,1)}, bf16[256,1024]{1,0:T(8,128)(2,1)S(1)}, u32[]{:S(2)}, u32[]{:S(2)}) collective-permute-start(bf16[256,1024]{1,0:T(8,128)(2,1)} %collective-permute-done.9.refs_1_), channel_id=1, source_target_pairs={{0,1},{1,0},{2,3},{3,2},{4,5},{5,4},{6,7},{7,6},{8,9},{9,8},{10,11... | collective-permute-start | bytes 1572872 | tf_op jit(solution)/shard_map/cond/branch_1_fun/ppermute | solution.py:468
  52.9 0.8 copy-start.15
  53.7 12.7 %collective-permute-start.13 = (bf16[256,1024]{1,0:T(8,128)(2,1)}, bf16[256,1024]{1,0:T(8,128)(2,1)S(1)}, u32[]{:S(2)}, u32[]{:S(2)}) collective-permute-start(bf16[256,1024]{1,0:T(8,128)(2,1)} %collective-permute-done.12.refs_3_), channel_id=1, source_target_pairs={{0,6},{1,7},{2,0},{3,1},{4,2},{5,3},{6,4},{7,5},{8,14},{9,15},{10,... | collective-permute-start | bytes 1572872 | tf_op jit(solution)/shard_map/cond/branch_1_fun/ppermute | solution.py:468
  56.4 1.0 copy-start.16
  57.4 11.9 %copy-start.18 = (bf16[8192,1024]{1,0:T(8,128)(2,1)S(1)}, bf16[8192,1024]{1,0:T(8,128)(2,1)}, u32[]{:S(2)}) copy-start(bf16[8192,1024]{1,0:T(8,128)(2,1)} %get-tuple-element.108.refs_5_.refs_4_) | copy-start | bytes 50331652 | tf_op jit(solution)/shard_map/cond
  57.4 11.9 %copy-start.20 = (bf16[8192,128]{1,0:T(8,128)(2,1)S(1)}, bf16[8192,128]{1,0:T(8,128)(2,1)}, u32[]{:S(2)}) copy-start(bf16[8192,128]{1,0:T(8,128)(2,1)} %get-tuple-element.109.refs_6_.refs_5_) | copy-start | bytes 6291460 | tf_op jit(solution)/shard_map/cond
  57.4 11.9 %copy-start.22 = (bf16[8192,128]{1,0:T(8,128)(2,1)S(1)}, bf16[8192,128]{1,0:T(8,128)(2,1)}, u32[]{:S(2)}) copy-start(bf16[8192,128]{1,0:T(8,128)(2,1)} %get-tuple-element.110.refs_7_.refs_6_) | copy-start | bytes 6291460 | tf_op jit(solution)/shard_map/cond
  66.5 7.8 %collective-permute-start.15 = (bf16[128,1024]{1,0:T(8,128)(2,1)S(1)}, bf16[128,1024]{1,0:T(8,128)(2,1)S(1)}, u32[]{:S(2)}, u32[]{:S(2)}) collective-permute-start(bf16[128,1024]{1,0:T(8,128)(2,1)S(1)} %slice.16), channel_id=1, source_target_pairs={{0,2},{1,3},{2,4},{3,5},{4,6},{5,7},{6,0},{7,1},{8,10},{9,11},{10,... | collective-permute-start | bytes 786440 | tf_op jit(solution)/shard_map/cond/branch_1_fun/ppermute | solution.py:468
  66.6 7.7 %copy-start.5 = (bf16[256,640]{1,0:T(8,128)(2,1)S(1)}, bf16[256,640]{1,0:T(8,128)(2,1)}, u32[]{:S(2)}) copy-start(bf16[256,640]{1,0:T(8,128)(2,1)} %copy-done.3) | copy-start | bytes 983044 | tf_op jit(solution)/shard_map/cond
  66.6 7.7 %copy-start.7 = (bf16[1024,128]{1,0:T(8,128)(2,1)S(1)}, bf16[1024,128]{1,0:T(8,128)(2,1)}, u32[]{:S(2)}) copy-start(bf16[1024,128]{1,0:T(8,128)(2,1)} %get-tuple-element.128.wv_ref) | copy-start | bytes 786436 | tf_op jit(solution)/shard_map/cond
  66.6 7.7 %copy-start.8 = (bf16[1024,128]{1,0:T(8,128)(2,1)S(1)}, bf16[1024,128]{1,0:T(8,128)(2,1)}, u32[]{:S(2)}) copy-start(bf16[1024,128]{1,0:T(8,128)(2,1)} %get-tuple-element.127.wk_ref) | copy-start | bytes 786436 | tf_op jit(solution)/shard_map/cond
  66.6 7.7 %copy-start.11 = (f32[256,128]{1,0:T(8,128)S(1)}, f32[256,128]{1,0:T(8,128)}, u32[]{:S(2)}) copy-start(f32[256,128]{1,0:T(8,128)} %get-tuple-element.130.cos_ref) | copy-start | bytes 393220 | tf_op jit(solution)/shard_map/cond
  66.6 7.7 %copy-start.12 = (f32[256,128]{1,0:T(8,128)S(1)}, f32[256,128]{1,0:T(8,128)}, u32[]{:S(2)}) copy-start(f32[256,128]{1,0:T(8,128)} %get-tuple-element.131.sin_ref) | copy-start | bytes 393220 | tf_op jit(solution)/shard_map/cond
  66.6 7.7 %copy-start.27 = (bf16[40,2,128,128]{3,2,1,0:T(8,128)(2,1)S(1)}, bf16[40,2,128,128]{3,2,1,0:T(8,128)(2,1)}, u32[]{:S(2)}) copy-start(bf16[40,2,128,128]{3,2,1,0:T(8,128)(2,1)} %get-tuple-element.132.pool_ref) | copy-start | bytes 7864324 | tf_op jit(solution)/shard_map/cond
  66.7 7.7 %collective-permute-start.16 = (bf16[128,1024]{1,0:T(8,128)(2,1)S(1)}, bf16[128,1024]{1,0:T(8,128)(2,1)S(1)}, u32[]{:S(2)}, u32[]{:S(2)}) collective-permute-start(bf16[128,1024]{1,0:T(8,128)(2,1)S(1)} %slice.17), channel_id=1, source_target_pairs={{0,6},{1,7},{2,0},{3,1},{4,2},{5,3},{6,4},{7,5},{8,14},{9,15},{10,... | collective-permute-start | bytes 786440 | tf_op jit(solution)/shard_map/cond/branch_1_fun/ppermute | solution.py:468
  111.0 2.4 %collective-permute-start.17 = (bf16[256,1024]{1,0:T(8,128)(2,1)S(1)}, bf16[256,1024]{1,0:T(8,128)(2,1)S(1)}, u32[]{:S(2)}, u32[]{:S(2)}) collective-permute-start(bf16[256,1024]{1,0:T(8,128)(2,1)S(1)} %get-tuple-element.134), channel_id=1, source_target_pairs={{0,8},{8,0},{16,24},{24,16},{32,40},{40,32},{48,56},{56,48},{64,72... | collective-permute-start | bytes 1572872 | tf_op jit(solution)/shard_map/cond/branch_1_fun/ppermute | solution.py:489
  113.6 0.8 copy-start.24
where the time goes:
time: 115 us; the launch traced here: 114 us
  Pallas kernels  33.7 us (29%)
  starting transfers between devices  26.5 us (23%)
  blocking collectives  25.1 us (22%)
  waiting for transfers between devices  17.4 us (15%)
  local copies, waits for them, and re-layouts  8.54 us (7%)
  other arithmetic  1.93 us (2%)
    all_to_all x1, blocking collectives, after_leave(): lax.all_to_all(back.reshape(groups, -1, back.shape[1]), 'sample', 0, 0)  25.1 us
    ppermute x8, starting transfers between devices, shift(): return lax.ppermute(block, 'tensor', moves(dy, dz))  15 us
    pallas_call x2, Pallas kernels, project(): pl.pallas_call(functools.partial(project_kernel, wq.shape[0], count, befo...  13.9 us
    all_to_all x1, waiting for transfers between devices, after_leave(): lax.all_to_all(send.reshape(groups, wide // groups, width), 'sample', 0, 0)  11.1 us
    pallas_call x1, Pallas kernels, attend(): pl.pallas_call(functools.partial(attend_kernel, 8 * part), out_shape=jax....  9.04 us
    all_to_all x1, starting transfers between devices, after_leave(): lax.all_to_all(send.reshape(groups, wide // groups, width), 'sample', 0, 0)  5.88 us
    ppermute x8, waiting for transfers between devices, shift(): return lax.ppermute(block, 'tensor', moves(dy, dz))  4.76 us
    dynamic_slice x2, local copies, waits for them, and re-layouts, after_leave(): lax.dynamic_slice_in_dim(w, place(2, 1) * width, width)  3.64 us
  transfers between devices with their start and end apart: 12, of which 3 were waited for; matrix products, arithmetic and copies ran while one was open for 5% of the time, Pallas kernels for 15%

commit v1 on v0

v1 whole, which is shorter than its diff:
```python
import functools
import math

import jax
import jax.numpy as jnp
from jax import lax
from jax.experimental import pallas as pl
from jax.experimental.pallas import tpu as pltpu
from jax.sharding import PartitionSpec as P

HEAD = 128
PAGE = 128
STEPS = 4
FORK = 8
PARENTS_HERE = 8
MOST_PAGES = 5
ROPE_THETA = 10000.0
EPSILON = 1e-06
SLOTS = 10
CHUNK = 640

BF16 = jnp.bfloat16
F32 = jnp.float32


def iota(shape, dim):
    return lax.broadcasted_iota(jnp.int32, shape, dim)


def one(mask):
    return jnp.where(mask, 1.0, 0.0).astype(BF16)


def mm(a, b):
    return lax.dot_general(a, b, (((1,), (0,)), ((), ())), preferred_element_type=F32)


def over(count, body):
    if count == 1:
        body(0)
    else:
        pl.loop(0, count)(body)


def chunk(i, size):
    return pl.ds(pl.multiple_of(i * size, size), size)


def mm_nt(a, b):
    return lax.dot_general(a, b, (((1,), (1,)), ((), ())), preferred_element_type=F32)


def owners(child_ref, owner_ref, mask_ref):
    groups, children = mask_ref.shape
    parents = owner_ref.shape[1]
    parent_hot = one(iota((parents, children), 0) == child_ref[...])
    owner = jnp.broadcast_to(owner_ref[...].astype(F32), (16, parents)).astype(BF16)
    owner_of = mm(owner, parent_hot)[0:1].astype(jnp.int32)
    mask_ref[...] = jnp.where(iota((groups, children), 0) == owner_of, 1.0, 0.0)


def targets(slots, me, mask_ref, rows):
    here = rows // STEPS
    core = lax.rem(me, 2)
    chip = lax.div(me, 2)
    mask = mask_ref[:, pl.ds(pl.multiple_of(chip * 2 * here, 2 * here), 2 * here)]
    ahead = mm(mask.astype(BF16), one(iota((128, 128), 0) < iota((128, 128), 1)))
    rank = jnp.sum(mask * ahead, axis=0, keepdims=True).astype(jnp.int32)
    owner = jnp.sum(mask * iota(mask.shape, 0).astype(F32), axis=0, keepdims=True)
    keep = jnp.where(rank % 2 == core, 1.0, 0.0)
    turn = (rank // 2).astype(F32)
    at = iota((16, 2 * here), 0)
    facts = jnp.where(at == 0, owner, jnp.where(at == 1, turn, keep)).astype(BF16)
    found = []
    for side in (core, 1 - core):
        grow = one(iota((2 * here, rows), 0) == side * here + iota((2 * here, rows), 1) // STEPS)
        of_row = mm(facts, grow)
        target = of_row[0:1] * (slots * STEPS) + of_row[1:2] * STEPS
        target = target.astype(jnp.int32) + iota((1, rows), 1) % STEPS
        found.append(jnp.where(of_row[2:3] > 0.5, target, -1))
    return found


def leave_kernel(slots, me_ref, child_ref, owner_ref, own_ref, other_ref, fits_ref, mask_ref):
    me = me_ref[0]
    rows = own_ref.shape[1]
    here = rows // STEPS
    children = child_ref.shape[1]
    owners(child_ref, owner_ref, mask_ref)
    counted = iota((children, 128), 1) == iota((children, 128), 0) // (2 * here)
    most = jnp.max(mm(mask_ref[...].astype(BF16), one(counted))).astype(jnp.int32)
    fits_ref[0] = jnp.where(most <= 2 * slots, 1, 0)

    for ref, target in zip((own_ref, other_ref), targets(slots, me, mask_ref, rows)):

        def fill(i, ref=ref, target=target):
            ref[chunk(i, CHUNK), :] = one(iota((CHUNK, rows), 0) + i * CHUNK == target)

        over(ref.shape[0] // CHUNK, fill)


def leave(slots, groups, me, child_parent, parent_owner, rows):
    vmem = pl.BlockSpec(memory_space=pltpu.VMEM)
    smem = pl.BlockSpec(memory_space=pltpu.SMEM)
    hot = jax.ShapeDtypeStruct((groups * slots * STEPS, rows), BF16)
    return pl.pallas_call(
        functools.partial(leave_kernel, slots),
        out_shape=(hot, hot, jax.ShapeDtypeStruct((1,), jnp.int32)),
        in_specs=[smem, vmem, vmem],
        out_specs=(vmem, vmem, smem),
        scratch_shapes=[pltpu.VMEM((groups, child_parent.shape[0]), F32)],
        compiler_params=pltpu.CompilerParams(vmem_limit_bytes=24 * 2**20),
        cost_estimate=pl.CostEstimate(flops=10**9, bytes_accessed=2**20, transcendentals=0),
    )(me, child_parent.reshape(1, -1), parent_owner.reshape(1, -1))


def arrive_kernel(
    slots,
    me_ref,
    child_ref,
    owner_ref,
    pages_ref,
    table_ref,
    from_ref,
    own_ref,
    other_ref,
    info_ref,
    mask_ref,
):
    me = me_ref[0]
    children = child_ref.shape[1]
    parents = owner_ref.shape[1]
    rows, wide = from_ref.shape
    here = rows // STEPS
    owner = owner_ref[...]
    parent_hot = one(iota((parents, children), 0) == child_ref[...])
    mine_parent = owner == me
    tri = one(iota((128, 128), 0) < iota((128, 128), 1))
    parent_rank = mm(one(jnp.broadcast_to(mine_parent, (16, parents))), tri)
    parent_rank = parent_rank[0:1].astype(jnp.int32)
    mine_hot = (iota((PARENTS_HERE, parents), 0) == parent_rank) & mine_parent
    pages = jnp.sum(jnp.where(mine_hot, pages_ref[...], 0), axis=1, keepdims=True)
    mine_hot = one(mine_hot)
    table = mm(mine_hot, table_ref[...].astype(F32).astype(BF16)).astype(jnp.int32)
    info_ref[...] = jnp.where(iota((PARENTS_HERE, 8), 1) == MOST_PAGES, pages, table)
    member = mm(mine_hot, parent_hot)
    carry = jnp.zeros((PARENTS_HERE, 1), F32)
    places, spots = [], []
    for block in range(children // 128):
        part = member[:, block * 128 : (block + 1) * 128]
        ahead = mm(part.astype(BF16), tri) + carry
        carry = carry + jnp.sum(part, axis=1, keepdims=True)
        is_mine = jnp.sum(part, axis=0, keepdims=True)
        place = jnp.sum(
            part * (iota((PARENTS_HERE, 128), 0).astype(F32) * FORK + ahead), axis=0, keepdims=True
        ).astype(jnp.int32)
        in_chip = mm(jnp.broadcast_to(is_mine, (16, 128)).astype(BF16), tri)[0:1].astype(jnp.int32)
        chip = (block * 128 + iota((1, 128), 1)) // (2 * here)
        spot = (chip * 2 + in_chip % 2) * slots + in_chip // 2
        places.append(jnp.where(is_mine > 0.5, place, -1))
        spots.append(jnp.where(is_mine > 0.5, spot, -1))
    place_hot = one(iota((here, children), 0) == jnp.concatenate(places, axis=1))
    spot = jnp.concatenate(spots, axis=1)
    grow_rows = one(iota((rows, here), 0) // STEPS == iota((rows, here), 1))
    size, deep = CHUNK, CHUNK // STEPS
    grow_columns = one(iota((deep, size), 0) == iota((deep, size), 1) // STEPS)
    same_step = iota((rows, size), 0) % STEPS == iota((rows, size), 1) % STEPS

    def fill(i):
        spot_hot = one(iota((deep, children), 0) + i * deep == spot)
        by_child = mm_nt(place_hot, spot_hot).astype(BF16)
        by_row = mm(mm(grow_rows, by_child).astype(BF16), grow_columns)
        from_ref[:, chunk(i, size)] = jnp.where(same_step, by_row, 0.0).astype(BF16)

    over(wide // CHUNK, fill)

    owners(child_ref, owner_ref, mask_ref)
    for ref, target in zip((own_ref, other_ref), targets(slots, me, mask_ref, rows)):
        column = jnp.broadcast_to(target.astype(F32), (128, rows)).T[:, 0:1].astype(jnp.int32)

        def put(i, ref=ref, column=column):
            ref[:, chunk(i, size)] = one(iota((rows, size), 1) + i * size == column)

        over(wide // CHUNK, put)


def arrive(slots, groups, me, child_parent, parent_owner, parent_pages, page_table, rows):
    hot = jax.ShapeDtypeStruct((rows, groups * slots * STEPS), BF16)
    vmem = pl.BlockSpec(memory_space=pltpu.VMEM)
    smem = pl.BlockSpec(memory_space=pltpu.SMEM)
    return pl.pallas_call(
        functools.partial(arrive_kernel, slots),
        out_shape=(
            hot,
            hot,
            hot,
            jax.ShapeDtypeStruct((PARENTS_HERE, 8), jnp.int32),
        ),
        in_specs=[smem] + [vmem] * 4,
        out_specs=(vmem, vmem, vmem, vmem),
        scratch_shapes=[pltpu.VMEM((groups, child_parent.shape[0]), F32)],
        compiler_params=pltpu.CompilerParams(vmem_limit_bytes=24 * 2**20),
        cost_estimate=pl.CostEstimate(flops=2 * 10**9, bytes_accessed=2**20, transcendentals=0),
    )(
        me,
        child_parent.reshape(1, -1),
        parent_owner.reshape(1, -1),
        parent_pages.reshape(1, -1),
        jnp.pad(page_table, ((0, 0), (0, 8 - page_table.shape[1]))),
    )


def fill_kernel(own_hot_ref, other_hot_ref, own_ref, other_ref, out_ref):
    def fill(i):
        at = chunk(i, CHUNK)
        filled = mm(own_hot_ref[at, :], own_ref[...]) + mm(other_hot_ref[at, :], other_ref[...])
        out_ref[at, :] = filled.astype(BF16)

    over(out_ref.shape[0] // CHUNK, fill)


def fill_slots(own_hot, other_hot, own, other):
    vmem = pl.BlockSpec(memory_space=pltpu.VMEM)
    return pl.pallas_call(
        fill_kernel,
        out_shape=jax.ShapeDtypeStruct((own_hot.shape[0], own.shape[1]), BF16),
        in_specs=[vmem] * 4,
        out_specs=vmem,
        compiler_params=pltpu.CompilerParams(vmem_limit_bytes=24 * 2**20),
    )(own_hot, other_hot, own, other)


def place_rows(hot_ref, rows_ref, acc_ref):
    if rows_ref.shape[0] == CHUNK:
        return mm(hot_ref[...], rows_ref[...])
    acc_ref[...] = jnp.zeros_like(acc_ref)

    @pl.loop(0, rows_ref.shape[0] // CHUNK)
    def _(i):
        at = chunk(i, CHUNK)
        acc_ref[...] += mm(hot_ref[:, at], rows_ref[at, :])

    return acc_ref[...]


def settle_kernel(hot_ref, rows_ref, out_ref, acc_ref):
    out_ref[...] = place_rows(hot_ref, rows_ref, acc_ref).astype(BF16)


def settle(hot, rows):
    vmem = pl.BlockSpec(memory_space=pltpu.VMEM)
    return pl.pallas_call(
        settle_kernel,
        out_shape=jax.ShapeDtypeStruct((hot.shape[0], rows.shape[1]), BF16),
        in_specs=[vmem, vmem],
        out_specs=vmem,
        scratch_shapes=[pltpu.VMEM((hot.shape[0], rows.shape[1]), F32)],
        compiler_params=pltpu.CompilerParams(vmem_limit_bytes=24 * 2**20),
        cost_estimate=pl.CostEstimate(
            flops=2 * hot.shape[0] * hot.shape[1] * rows.shape[1],
            bytes_accessed=2 * rows.shape[0] * rows.shape[1],
            transcendentals=0,
        ),
    )(hot, rows)


def pick_sum_kernel(hot_ref, rows_ref, out_ref, sum_ref, acc_ref, held_ref, sem):
    copy = pltpu.make_async_copy(hot_ref, held_ref, sem)
    copy.start()
    copy.wait()
    x = place_rows(held_ref, rows_ref, acc_ref)
    out_ref[...] = x.astype(BF16)
    total = jnp.sum(x * x, axis=1, keepdims=True)
    total = jnp.broadcast_to(total, (total.shape[0], 128)).T
    sum_ref[...] = jnp.broadcast_to(total[0:1], sum_ref.shape[:1] + total.shape[1:])[:, None, :]


def pick_and_sum(hot, rows, copies):
    vmem = pl.BlockSpec(memory_space=pltpu.VMEM)
    count = hot.shape[0]
    return pl.pallas_call(
        pick_sum_kernel,
        out_shape=(
            jax.ShapeDtypeStruct((count, rows.shape[1]), BF16),
            jax.ShapeDtypeStruct((copies, 1, count), F32),
        ),
        in_specs=[pl.BlockSpec(memory_space=pltpu.HBM), vmem],
        out_specs=(vmem, vmem),
        scratch_shapes=[
            pltpu.VMEM((count, rows.shape[1]), F32),
            pltpu.VMEM(hot.shape, BF16),
            pltpu.SemaphoreType.DMA,
        ],
        compiler_params=pltpu.CompilerParams(vmem_limit_bytes=24 * 2**20),
    )(hot, rows)


def row_scale(sum_ref, width):
    total = jnp.sum(sum_ref[:, 0, :], axis=0, keepdims=True)
    scale = lax.rsqrt(total * (1.0 / width) + EPSILON)
    return jnp.broadcast_to(scale, (128, scale.shape[1])).T


def normed(x, scale, gain):
    return (x.astype(F32) * scale * gain.astype(F32)).astype(BF16)


def add_products(acc, x, wq, wkv):
    wide = wq.shape[1]
    acc[:, :wide] += mm(x, wq)
    acc[:, wide:] += mm(x, wkv)


def project_kernel(width, count, first, order_ref, sum_ref, *refs):
    blocks = refs[:count]
    gain_ref, wq_ref, wk_ref, wv_ref = refs[count : count + 4]
    before = None if first else refs[count + 4]
    acc_ref, x_ref, wq_held, wkv_held, x_sems, w_sems = refs[-6:]
    part = x_ref.shape[2]

    def copies(i, block):
        at = chunk(order_ref[i], part)
        return [
            pltpu.make_async_copy(block, x_ref.at[i], x_sems.at[i]),
            pltpu.make_async_copy(wq_ref.at[at], wq_held.at[i], w_sems.at[i, 0]),
            pltpu.make_async_copy(wk_ref.at[at], wkv_held.at[i, :, :HEAD], w_sems.at[i, 1]),
            pltpu.make_async_copy(wv_ref.at[at], wkv_held.at[i, :, HEAD:], w_sems.at[i, 2]),
        ]

    for i in range(count):
        for copy in copies(i, blocks[i]):
            copy.start()
    scale = row_scale(sum_ref, width)[:, 0:1]
    acc_ref[...] = jnp.zeros_like(acc_ref) if first else before[...]

    @pl.loop(0, count)
    def _(i):
        for copy in copies(i, blocks[0]):
            copy.wait()
        x = normed(x_ref[i], scale, gain_ref[order_ref[i]])
        add_products(acc_ref, x, wq_held[i], wkv_held[i])


def project(order, sums, blocks, gain, wq, wk, wv, before=None):
    rows, part = blocks[0].shape
    columns = wq.shape[1] + wk.shape[1] + wv.shape[1]
    count = len(blocks)
    smem = pl.BlockSpec(memory_space=pltpu.SMEM)
    vmem = pl.BlockSpec(memory_space=pltpu.VMEM)
    hbm = pl.BlockSpec(memory_space=pltpu.HBM)
    extra = [] if before is None else [before]
    return pl.pallas_call(
        functools.partial(project_kernel, wq.shape[0], count, before is None),
        out_shape=jax.ShapeDtypeStruct((rows, columns), F32),
        in_specs=[smem, vmem] + [hbm] * count + [vmem, hbm, hbm, hbm] + [vmem] * len(extra),
        out_specs=vmem,
        scratch_shapes=[
            pltpu.VMEM((count, rows, part), BF16),
            pltpu.VMEM((count, part, wq.shape[1]), BF16),
            pltpu.VMEM((count, part, 2 * HEAD), BF16),
            pltpu.SemaphoreType.DMA((count,)),
            pltpu.SemaphoreType.DMA((count, 3)),
        ],
        compiler_params=pltpu.CompilerParams(vmem_limit_bytes=28 * 2**20),
        cost_estimate=pl.CostEstimate(
            flops=2 * rows * part * count * columns * 2,
            bytes_accessed=2 * part * count * columns,
            transcendentals=0,
        ),
    )(order, sums, *blocks, gain, wq, wk, wv, *extra)


def attend_kernel(
    width,
    info_ref,
    sum_ref,
    low_ref,
    high_ref,
    gain_ref,
    wq_ref,
    wk_ref,
    wv_ref,
    before_ref,
    cos_ref,
    sin_ref,
    pool_ref,
    back_ref,
    out_ref,
    acc_ref,
    x_ref,
    wkv_ref,
    q_ref,
    k_ref,
    v_ref,
    o_ref,
):
    scale = row_scale(sum_ref, width)[:, 0:1]
    half = low_ref.shape[0]
    x_ref[:half] = normed(low_ref[...], scale[:half], gain_ref[...])
    x_ref[half:] = normed(high_ref[...], scale[half:], gain_ref[...])
    acc_ref[...] = before_ref[...]
    wkv_ref[:, :HEAD] = wk_ref[...]
    wkv_ref[:, HEAD:] = wv_ref[...]
    add_products(acc_ref, x_ref[...], wq_ref[...], wkv_ref[...])

    cos = cos_ref[...]
    sin = sin_ref[...]

    def turn(part):
        return (part * cos + pltpu.roll(part, HEAD // 2, 1) * sin).astype(BF16)

    heads = wq_ref.shape[1] // HEAD
    for h in range(heads):
        cut = slice(h * HEAD, (h + 1) * HEAD)
        q_ref[:, cut] = turn(acc_ref[:, cut])
    k_ref[...] = turn(acc_ref[:, heads * HEAD : (heads + 1) * HEAD])
    v_ref[...] = acc_ref[:, (heads + 1) * HEAD :].astype(BF16)

    family = FORK * STEPS
    scale = 1.0 / math.sqrt(HEAD)
    row_at = iota((heads * family, family), 0) % family
    key_at = iota((heads * family, family), 1)
    page_at = iota((heads * family, MOST_PAGES * PAGE), 1) // PAGE
    own_mask = (row_at // STEPS == key_at // STEPS) & (row_at >= key_at)

    @pl.loop(0, PARENTS_HERE, unroll=4)
    def _(j):
        at = pl.ds(pl.multiple_of(j * family, family), family)
        q = jnp.concatenate([q_ref[at, h * HEAD : (h + 1) * HEAD] for h in range(heads)], axis=0)
        own = jnp.where(own_mask, mm_nt(q, k_ref[at, :]) * scale, -jnp.inf)
        own_top = jnp.max(own, axis=1, keepdims=True)
        own_weight = jnp.exp(own - own_top)
        own_total = jnp.sum(own_weight, axis=1, keepdims=True)
        own_mix = mm(own_weight.astype(BF16), v_ref[at, :])
        length = info_ref[j, MOST_PAGES]
        ids = [info_ref[j, i] for i in range(MOST_PAGES)]
        keys = jnp.concatenate([pool_ref[i, 0] for i in ids], axis=0)
        values = jnp.concatenate([pool_ref[i, 1] for i in ids], axis=0)
        path = jnp.where(page_at < length, mm_nt(q, keys) * scale, -jnp.inf)
        path_top = jnp.max(path, axis=1, keepdims=True)
        weight = jnp.exp(path - path_top)
        path_total = jnp.sum(weight, axis=1, keepdims=True)
        path_mix = mm(weight.astype(BF16), values)
        top = jnp.maximum(path_top, own_top)
        path_factor = jnp.exp(path_top - top)
        own_factor = jnp.exp(own_top - top)
        both = path_mix * path_factor + own_mix * own_factor
        out = both / (path_total * path_factor + own_total * own_factor)
        out = out.astype(BF16)
        for h in range(heads):
            o_ref[at, h * HEAD : (h + 1) * HEAD] = out[h * family : (h + 1) * family]


    def fill(i):
        at = chunk(i, CHUNK)
        out_ref[at, :] = mm(back_ref[at, :], o_ref[...]).astype(BF16)

    over(out_ref.shape[0] // CHUNK, fill)


def attend(info, sums, low, high, gain, wq, wk, wv, before, cos, sin, pool, back):
    rows, columns = before.shape
    part = low.shape[1]
    wide = back.shape[0]
    vmem = pl.BlockSpec(memory_space=pltpu.VMEM)
    smem = pl.BlockSpec(memory_space=pltpu.SMEM)
    return pl.pallas_call(
        functools.partial(attend_kernel, 8 * part),
        out_shape=jax.ShapeDtypeStruct((wide, wq.shape[1]), BF16),
        in_specs=[smem] + [vmem] * 12,
        out_specs=vmem,
        scratch_shapes=[
            pltpu.VMEM((rows, columns), F32),
            pltpu.VMEM((rows, part), BF16),
            pltpu.VMEM((part, 2 * HEAD), BF16),
            pltpu.VMEM((rows, wq.shape[1]), BF16),
            pltpu.VMEM((rows, HEAD), BF16),
            pltpu.VMEM((rows, HEAD), BF16),
            pltpu.VMEM((rows, wq.shape[1]), BF16),
        ],
        compiler_params=pltpu.CompilerParams(vmem_limit_bytes=24 * 2**20),
        cost_estimate=pl.CostEstimate(
            flops=2 * rows * part * columns * 6, bytes_accessed=2 * part * columns, transcendentals=0
        ),
    )(info, sums, low, high, gain, wq, wk, wv, before, cos, sin, pool, back)


def moves(dy, dz):
    return [(t, ((t // 2 + dy) % 4) * 2 + (t + dz) % 2) for t in range(8)]


def after_leave(slots, groups, me, tables, arrays, send):
    (norm_gain, wq, wk, wv, kv_pool) = arrays
    wide, width = send.shape
    rows = PARENTS_HERE * FORK * STEPS
    team = lax.axis_size("tensor")
    t = lax.axis_index("tensor")
    came = lax.all_to_all(send.reshape(groups, wide // groups, width), "sample", 0, 0)
    from_hot, own_hot, other_hot, info = arrive(slots, groups, me, *tables, rows)
    back_hot = from_hot.T

    def place(dy, dz):
        return ((t // 2 + dy) % 4) * 2 + (t + dz) % 2

    def order(*keys):
        return jnp.stack([place(*key) for key in keys]).astype(jnp.int32)

    last = [lax.dynamic_slice_in_dim(w, place(2, 1) * width, width) for w in (wq, wk, wv)]
    gain = norm_gain.reshape(team, 1, -1)
    last_gain = lax.dynamic_slice_in_dim(norm_gain, place(2, 1) * width, width).reshape(1, -1)

    pages = info[:, MOST_PAGES]
    positions = (
        jnp.repeat(pages * PAGE, FORK * STEPS)
        + jnp.tile(jnp.arange(STEPS, dtype=jnp.int32), PARENTS_HERE * FORK)
    ).astype(F32)
    inverse = ROPE_THETA ** (-2.0 * jnp.arange(HEAD // 2, dtype=F32) / HEAD)
    angles = positions[:, None] * inverse[None, :]
    cos, sin = jnp.cos(angles), jnp.sin(angles)
    cos = jnp.concatenate([cos, cos], axis=1)
    sin = jnp.concatenate([-sin, sin], axis=1)
    came, from_hot, info, cos, sin, gain, last_gain, *last = lax.optimization_barrier(
        (came, from_hot, info, cos, sin, gain, last_gain, *last)
    )
    back_hot, own_hot, other_hot, from_hot = lax.optimization_barrier(
        (back_hot, own_hot, other_hot, from_hot)
    )
    mine, sums = pick_and_sum(from_hot, came.reshape(wide, width), team)

    def shift(block, dy, dz):
        return lax.ppermute(block, "tensor", moves(dy, dz))

    sums = lax.all_to_all(sums, "tensor", 0, 0)
    b30, b10, b01 = shift(mine, 1, 0), shift(mine, -1, 0), shift(mine, 0, 1)
    (b30,) = lax.optimization_barrier((b30,))
    b20, b31 = shift(b30, 1, 0), shift(b30, 0, 1)
    second = (b20, shift(b01, -1, 0), b31)
    acc = project(
        order((0, 0), (3, 0), (1, 0), (0, 1)), sums, [mine, b30, b10, b01], gain, wq, wk, wv
    )
    b20, b11, b31, acc = lax.optimization_barrier((*second, acc))
    half = rows // 2
    low, high = shift(b31[:half], 1, 0), shift(b11[half:], -1, 0)
    acc = project(order((2, 0), (1, 1), (3, 1)), sums, [b20, b11, b31], gain, wq, wk, wv, acc)
    low, high, acc = lax.optimization_barrier((low, high, acc))
    back = attend(
        info, sums, low, high, last_gain, *last, acc, cos, sin, kv_pool, back_hot
    )
    home = lax.all_to_all(back.reshape(groups, -1, back.shape[1]), "sample", 0, 0)
    home = home.reshape(-1, back.shape[1])
    other = settle(other_hot, home)
    return settle(own_hot, home) + lax.ppermute(other, "sample", swap(groups))


def swap(groups):
    return [(i, i ^ 1) for i in range(groups)]


def local(
    branch_tokens,
    norm_gain,
    query_weight,
    key_weight,
    value_weight,
    kv_pool,
    parent_owner,
    parent_pages,
    page_table,
    child_parent,
):
    groups = lax.axis_size("sample")
    rows = branch_tokens.shape[0]
    me = lax.axis_index("sample").astype(jnp.int32).reshape(1)
    tables = (child_parent, parent_owner, parent_pages, page_table)
    arrays = (norm_gain, query_weight, key_weight, value_weight, kv_pool)
    other = lax.ppermute(branch_tokens, "sample", swap(groups))
    own_hot, other_hot, fits = leave(SLOTS, groups, me, *tables[:2], rows)
    other, own_hot, other_hot, fits = lax.optimization_barrier((other, own_hot, other_hot, fits))
    send = fill_slots(own_hot, other_hot, branch_tokens, other)

    def usual():
        return after_leave(SLOTS, groups, me, tables, arrays, send)

    def crowded():
        most = 4 * SLOTS
        own, others, _ = leave(most, groups, me, *tables[:2], rows)
        wider = fill_slots(own, others, branch_tokens, other)
        return after_leave(most, groups, me, tables, arrays, wider)

    return lax.switch(fits[0], [crowded, usual])


def solution(mesh):
    return jax.shard_map(
        local,
        mesh=mesh,
        in_specs=(
            P("sample", "tensor"),
            P(),
            P(None, "tensor"),
            P(None, "tensor"),
            P(None, "tensor"),
            P("sample", None, None, "tensor"),
            P(),
            P(),
            P(),
            P(),
        ),
        out_specs=P("sample", "tensor"),
        check_vma=False,
    )
```

time: 115 us -> 111 us (0.965)
  Pallas kernels: 33.7 us -> 27.5 us
    ppermute x8, waiting for transfers between devices: 4.76 us -> 8.44 us  [shift(): return lax.ppermute(block, 'tensor', moves(dy, dz))]
    all_to_all x1, waiting for transfers between devices: 11.1 us -> 8.4 us  [after_leave(): lax.all_to_all(send.reshape(groups, wide // groups, width), 'sample', 0, 0)]
    pallas_call x1, Pallas kernels: 9.04 us -> 7.29 us  [attend(): pl.pallas_call(functools.partial(attend_kernel, 8 * part), out_shape=jax....]
    pallas_call x2, Pallas kernels: 13.9 us -> 12.3 us  [project(): pl.pallas_call(functools.partial(project_kernel, wq.shape[0], count, befo...]
    cond x26 -> x28, local copies, waits for them, and re-layouts: 3.6 us -> 2.47 us
    pallas_call x2 -> x3, Pallas kernels: 3.62 us -> 2.85 us  [the longest x1 1.71 us: arrive(): pl.pallas_call(functools.partial(arrive_kernel, slots), out_shape=(hot, h...]
  transfers between devices with their start and end apart: 12 -> 12, of which waited for: 3 -> 7; matrix products, arithmetic and copies ran while one was open for 5% -> 7% of each run, Pallas kernels for 15% -> 15%
where the time goes in v1:
time: 111 us; the launch traced here: 110 us
  Pallas kernels  27.5 us (25%)
  starting transfers between devices  26.3 us (24%)
  blocking collectives  26 us (23%)
  waiting for transfers between devices  17.9 us (16%)
  local copies, waits for them, and re-layouts  9.62 us (9%)
  other arithmetic  1.86 us (2%)
    all_to_all x1, blocking collectives, after_leave(): lax.all_to_all(back.reshape(groups, -1, back.shape[1]), 'sample', 0, 0)  26 us
    ppermute x8, starting transfers between devices, shift(): return lax.ppermute(block, 'tensor', moves(dy, dz))  14.5 us
    pallas_call x2, Pallas kernels, project(): pl.pallas_call(functools.partial(project_kernel, wq.shape[0], count, befo...  12.3 us
    ppermute x8, waiting for transfers between devices, shift(): return lax.ppermute(block, 'tensor', moves(dy, dz))  8.44 us
    all_to_all x1, waiting for transfers between devices, after_leave(): lax.all_to_all(send.reshape(groups, wide // groups, width), 'sample', 0, 0)  8.4 us
    pallas_call x1, Pallas kernels, attend(): pl.pallas_call(functools.partial(attend_kernel, 8 * part), out_shape=jax....  7.29 us
    all_to_all x1, starting transfers between devices, after_leave(): lax.all_to_all(send.reshape(groups, wide // groups, width), 'sample', 0, 0)  6.13 us
    dynamic_slice x2, local copies, waits for them, and re-layouts, after_leave(): lax.dynamic_slice_in_dim(w, place(2, 1) * width, width)  3.62 us
  transfers between devices with their start and end apart: 12, of which 7 were waited for; matrix products, arithmetic and copies ran while one was open for 7% of the time, Pallas kernels for 15%

profile of v1, /device:TPU:1, one launch (start us, length us, event | category | flops | bytes accessed | tf_op | source)
XLA Modules:
  0.0 110.4 jit_solution(17780248764299709365)
XLA Ops:
  0.0 1.4 %collective-permute-start.18 = (bf16[256,1024]{1,0:T(8,128)(2,1)}, bf16[256,1024]{1,0:T(8,128)(2,1)S(1)}, u32[]{:S(2)}, u32[]{:S(2)}) collective-permute-start(bf16[256,1024]{1,0:T(8,128)(2,1)} %own_ref.1), channel_id=1, source_target_pairs={{0,8},{8,0},{16,24},{24,16},{32,40},{40,32},{48,56},{56,48},{64,72... | collective-permute-start | bytes 1572872 | tf_op jit(solution)/shard_map/ppermute | solution.py:576
  1.4 1.6 %shard_map.102 = (bf16[640,256]{1,0:T(8,128)(2,1)S(1)}, bf16[640,256]{1,0:T(8,128)(2,1)S(1)}, s32[1]{0:T(128)}) custom-call(s32[1]{0:T(128)} %bitcast.30.me_ref, s32[1,1024]{1,0:T(1,128)} %bitcast.45, s32[1,128]{1,0:T(1,128)} %bitcast.49), custom_call_target="tpu_custom_call" | custom-call | flops 1000000000 | bytes 1048576 | tf_op jit(solution)/shard_map/pallas_call | solution.py:106
  3.0 0.0 copy-start.26
  3.0 0.0 copy-start.27
  3.1 0.0 copy-start.30
  3.1 0.0 copy-start.31
  3.1 0.0 copy-start.32
  3.1 0.1 collective-permute-done.18.other_ref
  3.2 1.9 %shard_map.103 = bf16[640,1024]{1,0:T(8,128)(2,1)} custom-call(bf16[640,256]{1,0:T(8,128)(2,1)S(1)} %get-tuple-element.145.own_hot_ref, bf16[640,256]{1,0:T(8,128)(2,1)S(1)} %get-tuple-element.146.other_hot_ref, bf16[256,1024]{1,0:T(8,128)(2,1)S(1)} %copy-done.24, bf16[256,1024]{1,0:T(8,128)(2,1)S(1)} %collective-permute-done.18.other_ref), custom_call_target="tpu_custom_call" | custom-call | tf_op jit(solution)/shard_map/pallas_call | solution.py:224
  5.8 103.8 %conditional.1 = (bf16[256,1024]{1,0:T(8,128)(2,1)S(1)}) conditional(s32[]{:T(128)} %bitcast.33, (s32[1024]{0:T(1024)S(1)}, s32[128]{0:T(128)S(1)}, s32[128]{0:T(128)S(1)}, s32[128,5]{0,1:T(8,128)S(1)}, s32[1]{0:T(128)}, /*index=5*/bf16[256,1024]{1,0:T(8,128)(2,1)S(1)}, bf16[256,1024]{1,0:T(8,128)(2,1)S(1)}, bf16[8192]{0:T(1024)(128)(2,1)S(1)}, ...), branch_computations={%region_0.1_spmd, %region_1.2_spmd} | conditional | flops 19106488320 | bytes 164880288 | solution.py:590
  6.0 6.1 %all-to-all-start.3 = ((bf16[16,40,1024]{2,1,0:T(8,128)(2,1)}), bf16[16,40,1024]{2,1,0:T(8,128)(2,1)S(1)}, u32[]{:S(2)}, u32[]{:S(2)}) async-start(bf16[16,40,1024]{2,1,0:T(8,128)(2,1)} %bitcast.44), calls=%async_computation.3 | async-start | bytes 2621440 | tf_op jit(solution)/shard_map/cond/branch_1_fun/all_to_all | solution.py:498
  12.2 0.6 reshape.100
  12.8 0.1 tile.12
  12.9 0.1 copy.24
  13.0 1.7 %branch_1_fun.7 = (bf16[256,640]{1,0:T(8,128)(2,1)S(1)}, bf16[256,640]{1,0:T(8,128)(2,1)S(1)}, bf16[256,640]{1,0:T(8,128)(2,1)S(1)}, s32[8,8]{1,0:T(8,128)S(1)}) custom-call(s32[1]{0:T(128)} %get-tuple-element.95.me_ref, s32[1,1024]{1,0:T(1,128)S(1)} %bitcast.48, s32[1,128]{1,0:T(1,128)S(1)} %bitcast.52, s32[1,128]{1,0:T(1,128)S(1)} %bitcast.54, ...), custom_call_target="tpu_custom_call" | custom-call | flops 2000000000 | bytes 1048576 | tf_op jit(solution)/shard_map/cond/branch_1_fun/pallas_call | solution.py:191
  14.8 0.7 copy-done.9
  15.5 0.7 copy-done.11
  16.2 0.2 multiply_reduce_fusion.1
  16.4 0.1 broadcast_in_dim.6
  16.5 0.1 reshape.99
  16.6 0.9 copy.20
  17.5 0.5 fusion.1
  18.0 0.8 pad_maximum_fusion.2
  18.8 1.9 %constant_dynamic-slice_fusion.3 = (bf16[1024,128]{1,0:T(8,128)(2,1)}, bf16[1024,128]{1,0:T(8,128)(2,1)}) fusion(bf16[8192,128]{1,0:T(8,128)(2,1)} %get-tuple-element.108.refs_7_.refs_6_, s32[]{:T(128)S(6)} %select_n.149, bf16[8192,128]{1,0:T(8,128)(2,1)} %get-tuple-element.107.refs_6_.refs_5_), kind=kLoop, calls=%fused_computation.20 | loop fusion | bytes 1048580 | tf_op jit(solution)/shard_map/cond/branch_1_fun/dynamic_slice | solution.py:508
  20.7 1.8 %constant_dynamic-slice_fusion.5.wq_ref = bf16[1024,1024]{1,0:T(8,128)(2,1)S(1)} fusion(bf16[8192,1024]{1,0:T(8,128)(2,1)} %get-tuple-element.106.refs_5_.refs_4_, s32[]{:T(128)S(6)} %select_n.149), kind=kLoop, calls=%fused_computation.22 | loop fusion | bytes 4194308 | tf_op jit(solution)/shard_map/cond/branch_1_fun/dynamic_slice | solution.py:508
  22.4 8.4 %all-to-all-done.3 = bf16[16,40,1024]{2,1,0:T(8,128)(2,1)S(1)} async-done(((bf16[16,40,1024]{2,1,0:T(8,128)(2,1)}), bf16[16,40,1024]{2,1,0:T(8,128)(2,1)S(1)}, u32[]{:S(2)}, u32[]{:S(2)}) %all-to-all-start.3) | async-done | bytes 1310752 | tf_op jit(solution)/shard_map/cond/branch_1_fun/all_to_all | solution.py:498
  30.8 1.0 copy-done.7
  31.8 1.5 %branch_1_fun.8 = (bf16[256,1024]{1,0:T(8,128)(2,1)}, f32[8,1,256]{2,1,0:T(1,128)}) custom-call(bf16[256,640]{1,0:T(8,128)(2,1)S(1)} %copy-done.7, bf16[640,1024]{1,0:T(8,128)(2,1)S(1)} %bitcast.40), custom_call_target="tpu_custom_call" | custom-call | tf_op jit(solution)/shard_map/cond/branch_1_fun/pallas_call | solution.py:281
  33.3 1.4 %collective-permute-start.9 = (bf16[256,1024]{1,0:T(8,128)(2,1)}, bf16[256,1024]{1,0:T(8,128)(2,1)}, u32[]{:S(2)}, u32[]{:S(2)}) collective-permute-start(bf16[256,1024]{1,0:T(8,128)(2,1)} %get-tuple-element.115.refs_0_), channel_id=1, source_target_pairs={{0,2},{1,3},{2,4},{3,5},{4,6},{5,7},{6,0},{7,1},{8,10},{9,11},{10,... | collective-permute-start | bytes 1572872 | tf_op jit(solution)/shard_map/cond/branch_1_fun/ppermute | solution.py:531
  34.7 3.3 %collective-permute-start.11 = (bf16[256,1024]{1,0:T(8,128)(2,1)}, bf16[256,1024]{1,0:T(8,128)(2,1)}, u32[]{:S(2)}, u32[]{:S(2)}) collective-permute-start(bf16[256,1024]{1,0:T(8,128)(2,1)} %get-tuple-element.115.refs_0_), channel_id=1, source_target_pairs={{0,1},{1,0},{2,3},{3,2},{4,5},{5,4},{6,7},{7,6},{8,9},{9,8},{10,11... | collective-permute-start | bytes 1572872 | tf_op jit(solution)/shard_map/cond/branch_1_fun/ppermute | solution.py:531
  38.0 1.5 %collective-permute-start.14 = (bf16[256,1024]{1,0:T(8,128)(2,1)}, bf16[256,1024]{1,0:T(8,128)(2,1)}, u32[]{:S(2)}, u32[]{:S(2)}) collective-permute-start(bf16[256,1024]{1,0:T(8,128)(2,1)} %get-tuple-element.115.refs_0_), channel_id=1, source_target_pairs={{0,6},{1,7},{2,0},{3,1},{4,2},{5,3},{6,4},{7,5},{8,14},{9,15},{10,... | collective-permute-start | bytes 1572872 | tf_op jit(solution)/shard_map/cond/branch_1_fun/ppermute | solution.py:531
  39.5 0.1 pad_add_fusion.3.order_ref
  39.6 3.3 %all-to-all-start.4 = ((f32[8,1,256]{2,1,0:T(1,128)}), f32[8,1,256]{2,1,0:T(1,128)S(1)}, u32[]{:S(2)}, u32[]{:S(2)}) async-start(f32[8,1,256]{2,1,0:T(1,128)} %get-tuple-element.114), calls=%async_computation.4 | async-start | bytes 16384 | tf_op jit(solution)/shard_map/cond/branch_1_fun/all_to_all | solution.py:533
  42.9 4.9 %collective-permute-done.9.refs_1_ = bf16[256,1024]{1,0:T(8,128)(2,1)} collective-permute-done((bf16[256,1024]{1,0:T(8,128)(2,1)}, bf16[256,1024]{1,0:T(8,128)(2,1)}, u32[]{:S(2)}, u32[]{:S(2)}) %collective-permute-start.9) | collective-permute-done | bytes 524320 | tf_op jit(solution)/shard_map/cond/branch_1_fun/ppermute | solution.py:531
  47.8 3.3 %collective-permute-start.13 = (bf16[256,1024]{1,0:T(8,128)(2,1)}, bf16[256,1024]{1,0:T(8,128)(2,1)S(1)}, u32[]{:S(2)}, u32[]{:S(2)}) collective-permute-start(bf16[256,1024]{1,0:T(8,128)(2,1)} %collective-permute-done.9.refs_1_), channel_id=1, source_target_pairs={{0,1},{1,0},{2,3},{3,2},{4,5},{5,4},{6,7},{7,6},{8,9},{9,8},{10,11... | collective-permute-start | bytes 1572872 | tf_op jit(solution)/shard_map/cond/branch_1_fun/ppermute | solution.py:531
  51.1 0.0 collective-permute-start.10
  51.1 0.0 collective-permute-done.11.refs_3_
  51.1 2.7 %collective-permute-start.12 = (bf16[256,1024]{1,0:T(8,128)(2,1)}, bf16[256,1024]{1,0:T(8,128)(2,1)S(1)}, u32[]{:S(2)}, u32[]{:S(2)}) collective-permute-start(bf16[256,1024]{1,0:T(8,128)(2,1)} %collective-permute-done.11.refs_3_), channel_id=1, source_target_pairs={{0,6},{1,7},{2,0},{3,1},{4,2},{5,3},{6,4},{7,5},{8,14},{9,15},{10,... | collective-permute-start | bytes 1572872 | tf_op jit(solution)/shard_map/cond/branch_1_fun/ppermute | solution.py:531
  53.8 0.1 pad_add_fusion.2.order_ref
  53.8 0.7 copy.21.refs_4_.refs_3_
  54.6 0.0 all-to-all-done.4.sum_ref
  54.6 0.0 collective-permute-done.14.refs_2_
  54.6 0.0 copy-start.19
  54.6 0.0 copy-start.21
  54.6 0.0 copy-start.23
  54.6 7.9 %branch_1_fun.9.refs_7_ = f32[256,1280]{1,0:T(8,128)S(1)} custom-call(s32[4]{0:T(128)S(1)} %pad_add_fusion.2.order_ref, f32[8,1,256]{2,1,0:T(1,128)S(1)} %all-to-all-done.4.sum_ref, bf16[256,1024]{1,0:T(8,128)(2,1)} %get-tuple-element.115.refs_0_, bf16[256,1024]{1,0:T(8,128)(2,1)} %collective-permute-done.9.refs_1_, ...), custom_call_target="tpu_custom_call" | custom-call | flops 5368709120 | bytes 10485760 | tf_op jit(solution)/shard_map/cond/branch_1_fun/pallas_call | solution.py:352
  62.5 0.6 collective-permute-done.12.refs_1_
  63.2 0.0 collective-permute-done.13.refs_2_
  63.2 1.0 collective-permute-done.10.refs_0_
  64.3 0.0 copy-start.29
  64.3 2.4 %collective-permute-start.16 = (bf16[128,1024]{1,0:T(8,128)(2,1)S(1)}, bf16[128,1024]{1,0:T(8,128)(2,1)S(1)}, u32[]{:S(2)}, u32[]{:S(2)}) collective-permute-start(bf16[128,1024]{1,0:T(8,128)(2,1)S(1)} %slice.17), channel_id=1, source_target_pairs={{0,6},{1,7},{2,0},{3,1},{4,2},{5,3},{6,4},{7,5},{8,14},{9,15},{10,... | collective-permute-start | bytes 786440 | tf_op jit(solution)/shard_map/cond/branch_1_fun/ppermute | solution.py:531
  66.6 0.0 collective-permute-start.15
  66.7 4.4 %branch_1_fun.10.before_ref = f32[256,1280]{1,0:T(8,128)S(1)} custom-call(s32[3]{0:T(128)S(1)} %pad_add_fusion.3.order_ref, f32[8,1,256]{2,1,0:T(1,128)S(1)} %all-to-all-done.4.sum_ref, bf16[256,1024]{1,0:T(8,128)(2,1)} %collective-permute-done.10.refs_0_, bf16[256,1024]{1,0:T(8,128)(2,1)S(1)} %collective-permute-done.12.refs_1_, ...), custom_call_target="tpu_custom_call" | custom-call | flops 4026531840 | bytes 7864320 | tf_op jit(solution)/shard_map/cond/branch_1_fun/pallas_call | solution.py:352
  71.1 0.0 collective-permute-done.16.high_ref
  71.1 2.0 %collective-permute-done.15.low_ref = bf16[128,1024]{1,0:T(8,128)(2,1)S(1)} collective-permute-done((bf16[128,1024]{1,0:T(8,128)(2,1)S(1)}, bf16[128,1024]{1,0:T(8,128)(2,1)S(1)}, u32[]{:S(2)}, u32[]{:S(2)}) %collective-permute-start.15) | collective-permute-done | bytes 262176 | tf_op jit(solution)/shard_map/cond/branch_1_fun/ppermute | solution.py:531
  73.1 7.3 %branch_1_fun.11 = bf16[640,1024]{1,0:T(8,128)(2,1)S(1)} custom-call(s32[8,8]{1,0:T(8,128)S(1)} %get-tuple-element.111.info_ref, f32[8,1,256]{2,1,0:T(1,128)S(1)} %all-to-all-done.4.sum_ref, bf16[128,1024]{1,0:T(8,128)(2,1)S(1)} %collective-permute-done.15.low_ref, bf16[128,1024]{1,0:T(8,128)(2,1)S(1)} %collective-permute-done.16.high_ref, ...), custom_call_target="tpu_custom_call" | custom-call | flops 4026531840 | bytes 2621440 | tf_op jit(solution)/shard_map/cond/branch_1_fun/pallas_call | solution.py:467
  80.4 26.0 %all_to_all.25 = bf16[16,40,1024]{2,1,0:T(8,128)(2,1)S(1)} all-to-all(bf16[16,40,1024]{2,1,0:T(8,128)(2,1)S(1)} %bitcast.42), channel_id=1, replica_groups=mesh['sample'=16,'tensor'=8] {'sample'}, dimensions={0} | all-to-all | bytes 2621440 | tf_op jit(solution)/shard_map/cond/branch_1_fun/all_to_all | solution.py:549
  106.4 0.6 branch_1_fun.13
  107.0 0.9 collective-permute-start.17
  107.9 0.6 branch_1_fun.12
  108.4 1.0 collective-permute-done.17
  109.4 0.2 add.208
  109.6 0.0 copy-start.25
  109.6 0.8 copy-done.25
  (36 shorter events, 0.1 us)
Async XLA Ops:
  0.0 3.2 %copy-start.24 = (bf16[256,1024]{1,0:T(8,128)(2,1)S(1)}, bf16[256,1024]{1,0:T(8,128)(2,1)}, u32[]{:S(2)}) copy-start(bf16[256,1024]{1,0:T(8,128)(2,1)} %own_ref.1) | copy-start | bytes 1572868
  0.0 3.2 %collective-permute-start.18 = (bf16[256,1024]{1,0:T(8,128)(2,1)}, bf16[256,1024]{1,0:T(8,128)(2,1)S(1)}, u32[]{:S(2)}, u32[]{:S(2)}) collective-permute-start(bf16[256,1024]{1,0:T(8,128)(2,1)} %own_ref.1), channel_id=1, source_target_pairs={{0,8},{8,0},{16,24},{24,16},{32,40},{40,32},{48,56},{56,48},{64,72... | collective-permute-start | bytes 1572872 | tf_op jit(solution)/shard_map/ppermute | solution.py:576
  3.0 2.7 %copy-start.26 = (bf16[8192]{0:T(1024)(128)(2,1)S(1)}, bf16[8192]{0:T(1024)(128)(2,1)}, u32[]{:S(2)}) copy-start(bf16[8192]{0:T(1024)(128)(2,1)} %param.13) | copy-start | bytes 49156
  3.0 2.7 %copy-start.27 = (s32[128,5]{0,1:T(8,128)S(1)}, s32[128,5]{0,1:T(8,128)}, u32[]{:S(2)}) copy-start(s32[128,5]{0,1:T(8,128)} %param.20) | copy-start | bytes 7684
  3.1 2.7 %copy-start.30 = (s32[1024]{0:T(1024)S(1)}, s32[1024]{0:T(1024)}, u32[]{:S(2)}) copy-start(s32[1024]{0:T(1024)} %param.21) | copy-start | bytes 12292
  3.1 2.7 %copy-start.31 = (s32[128]{0:T(128)S(1)}, s32[128]{0:T(128)}, u32[]{:S(2)}) copy-start(s32[128]{0:T(128)} %param.18) | copy-start | bytes 1540
  3.1 2.7 %copy-start.32 = (s32[128]{0:T(128)S(1)}, s32[128]{0:T(128)}, u32[]{:S(2)}) copy-start(s32[128]{0:T(128)} %param.19) | copy-start | bytes 1540
  6.0 24.8 %all-to-all-start.3 = ((bf16[16,40,1024]{2,1,0:T(8,128)(2,1)}), bf16[16,40,1024]{2,1,0:T(8,128)(2,1)S(1)}, u32[]{:S(2)}, u32[]{:S(2)}) async-start(bf16[16,40,1024]{2,1,0:T(8,128)(2,1)} %bitcast.44), calls=%async_computation.3 | async-start | bytes 2621440 | tf_op jit(solution)/shard_map/cond/branch_1_fun/all_to_all | solution.py:498
  14.8 0.7 copy-start.9
  15.5 0.7 copy-start.11
  16.2 4.5 %copy-start.6 = (bf16[256,640]{1,0:T(8,128)(2,1)}, bf16[256,640]{1,0:T(8,128)(2,1)S(1)}, u32[]{:S(2)}) copy-start(bf16[256,640]{1,0:T(8,128)(2,1)S(1)} %get-tuple-element.112.hot_ref) | copy-start | bytes 983044 | tf_op jit(solution)/shard_map/cond
  30.8 1.0 copy-start.7
  33.3 14.4 %collective-permute-start.9 = (bf16[256,1024]{1,0:T(8,128)(2,1)}, bf16[256,1024]{1,0:T(8,128)(2,1)}, u32[]{:S(2)}, u32[]{:S(2)}) collective-permute-start(bf16[256,1024]{1,0:T(8,128)(2,1)} %get-tuple-element.115.refs_0_), channel_id=1, source_target_pairs={{0,2},{1,3},{2,4},{3,5},{4,6},{5,7},{6,0},{7,1},{8,10},{9,11},{10,... | collective-permute-start | bytes 1572872 | tf_op jit(solution)/shard_map/cond/branch_1_fun/ppermute | solution.py:531
  34.7 16.4 %collective-permute-start.11 = (bf16[256,1024]{1,0:T(8,128)(2,1)}, bf16[256,1024]{1,0:T(8,128)(2,1)}, u32[]{:S(2)}, u32[]{:S(2)}) collective-permute-start(bf16[256,1024]{1,0:T(8,128)(2,1)} %get-tuple-element.115.refs_0_), channel_id=1, source_target_pairs={{0,1},{1,0},{2,3},{3,2},{4,5},{5,4},{6,7},{7,6},{8,9},{9,8},{10,11... | collective-permute-start | bytes 1572872 | tf_op jit(solution)/shard_map/cond/branch_1_fun/ppermute | solution.py:531
  38.0 16.6 %collective-permute-start.14 = (bf16[256,1024]{1,0:T(8,128)(2,1)}, bf16[256,1024]{1,0:T(8,128)(2,1)}, u32[]{:S(2)}, u32[]{:S(2)}) collective-permute-start(bf16[256,1024]{1,0:T(8,128)(2,1)} %get-tuple-element.115.refs_0_), channel_id=1, source_target_pairs={{0,6},{1,7},{2,0},{3,1},{4,2},{5,3},{6,4},{7,5},{8,14},{9,15},{10,... | collective-permute-start | bytes 1572872 | tf_op jit(solution)/shard_map/cond/branch_1_fun/ppermute | solution.py:531
  39.6 15.0 %all-to-all-start.4 = ((f32[8,1,256]{2,1,0:T(1,128)}), f32[8,1,256]{2,1,0:T(1,128)S(1)}, u32[]{:S(2)}, u32[]{:S(2)}) async-start(f32[8,1,256]{2,1,0:T(1,128)} %get-tuple-element.114), calls=%async_computation.4 | async-start | bytes 16384 | tf_op jit(solution)/shard_map/cond/branch_1_fun/all_to_all | solution.py:533
  47.8 15.4 %collective-permute-start.13 = (bf16[256,1024]{1,0:T(8,128)(2,1)}, bf16[256,1024]{1,0:T(8,128)(2,1)S(1)}, u32[]{:S(2)}, u32[]{:S(2)}) collective-permute-start(bf16[256,1024]{1,0:T(8,128)(2,1)} %collective-permute-done.9.refs_1_), channel_id=1, source_target_pairs={{0,1},{1,0},{2,3},{3,2},{4,5},{5,4},{6,7},{7,6},{8,9},{9,8},{10,11... | collective-permute-start | bytes 1572872 | tf_op jit(solution)/shard_map/cond/branch_1_fun/ppermute | solution.py:531
  51.1 13.1 %collective-permute-start.10 = (bf16[256,1024]{1,0:T(8,128)(2,1)}, bf16[256,1024]{1,0:T(8,128)(2,1)}, u32[]{:S(2)}, u32[]{:S(2)}) collective-permute-start(bf16[256,1024]{1,0:T(8,128)(2,1)} %collective-permute-done.9.refs_1_), channel_id=1, source_target_pairs={{0,2},{1,3},{2,4},{3,5},{4,6},{5,7},{6,0},{7,1},{8,10},{9,11},{10,... | collective-permute-start | bytes 1572872 | tf_op jit(solution)/shard_map/cond/branch_1_fun/ppermute | solution.py:531
  51.1 12.1 %collective-permute-start.12 = (bf16[256,1024]{1,0:T(8,128)(2,1)}, bf16[256,1024]{1,0:T(8,128)(2,1)S(1)}, u32[]{:S(2)}, u32[]{:S(2)}) collective-permute-start(bf16[256,1024]{1,0:T(8,128)(2,1)} %collective-permute-done.11.refs_3_), channel_id=1, source_target_pairs={{0,6},{1,7},{2,0},{3,1},{4,2},{5,3},{6,4},{7,5},{8,14},{9,15},{10,... | collective-permute-start | bytes 1572872 | tf_op jit(solution)/shard_map/cond/branch_1_fun/ppermute | solution.py:531
  54.6 12.0 %copy-start.19 = (bf16[8192,1024]{1,0:T(8,128)(2,1)S(1)}, bf16[8192,1024]{1,0:T(8,128)(2,1)}, u32[]{:S(2)}) copy-start(bf16[8192,1024]{1,0:T(8,128)(2,1)} %get-tuple-element.106.refs_5_.refs_4_) | copy-start | bytes 50331652 | tf_op jit(solution)/shard_map/cond
  54.6 12.0 %copy-start.21 = (bf16[8192,128]{1,0:T(8,128)(2,1)S(1)}, bf16[8192,128]{1,0:T(8,128)(2,1)}, u32[]{:S(2)}) copy-start(bf16[8192,128]{1,0:T(8,128)(2,1)} %get-tuple-element.107.refs_6_.refs_5_) | copy-start | bytes 6291460 | tf_op jit(solution)/shard_map/cond
  54.6 12.0 %copy-start.23 = (bf16[8192,128]{1,0:T(8,128)(2,1)S(1)}, bf16[8192,128]{1,0:T(8,128)(2,1)}, u32[]{:S(2)}) copy-start(bf16[8192,128]{1,0:T(8,128)(2,1)} %get-tuple-element.108.refs_7_.refs_6_) | copy-start | bytes 6291460 | tf_op jit(solution)/shard_map/cond
  64.2 8.9 %copy-start.8 = (bf16[256,640]{0,1:T(8,128)(2,1)S(1)}, bf16[256,640]{0,1:T(8,128)(2,1)}, u32[]{:S(2)}) copy-start(bf16[256,640]{0,1:T(8,128)(2,1)} %copy.20) | copy-start | bytes 983044 | tf_op jit(solution)/shard_map/cond
  64.2 8.9 %copy-start.15 = (bf16[1024,128]{1,0:T(8,128)(2,1)S(1)}, bf16[1024,128]{1,0:T(8,128)(2,1)}, u32[]{:S(2)}) copy-start(bf16[1024,128]{1,0:T(8,128)(2,1)} %get-tuple-element.126.wv_ref) | copy-start | bytes 786436 | tf_op jit(solution)/shard_map/cond
  64.2 8.8 %copy-start.16 = (bf16[1024,128]{1,0:T(8,128)(2,1)S(1)}, bf16[1024,128]{1,0:T(8,128)(2,1)}, u32[]{:S(2)}) copy-start(bf16[1024,128]{1,0:T(8,128)(2,1)} %get-tuple-element.125.wk_ref) | copy-start | bytes 786436 | tf_op jit(solution)/shard_map/cond
  64.2 8.8 %copy-start.18 = (f32[256,128]{1,0:T(8,128)S(1)}, f32[256,128]{1,0:T(8,128)}, u32[]{:S(2)}) copy-start(f32[256,128]{1,0:T(8,128)} %get-tuple-element.129.sin_ref) | copy-start | bytes 393220 | tf_op jit(solution)/shard_map/cond
  64.3 8.8 %copy-start.29 = (bf16[40,2,128,128]{3,2,1,0:T(8,128)(2,1)S(1)}, bf16[40,2,128,128]{3,2,1,0:T(8,128)(2,1)}, u32[]{:S(2)}) copy-start(bf16[40,2,128,128]{3,2,1,0:T(8,128)(2,1)} %get-tuple-element.130.pool_ref) | copy-start | bytes 7864324 | tf_op jit(solution)/shard_map/cond
  64.3 6.8 %collective-permute-start.16 = (bf16[128,1024]{1,0:T(8,128)(2,1)S(1)}, bf16[128,1024]{1,0:T(8,128)(2,1)S(1)}, u32[]{:S(2)}, u32[]{:S(2)}) collective-permute-start(bf16[128,1024]{1,0:T(8,128)(2,1)S(1)} %slice.17), channel_id=1, source_target_pairs={{0,6},{1,7},{2,0},{3,1},{4,2},{5,3},{6,4},{7,5},{8,14},{9,15},{10,... | collective-permute-start | bytes 786440 | tf_op jit(solution)/shard_map/cond/branch_1_fun/ppermute | solution.py:531
  66.6 6.4 %collective-permute-start.15 = (bf16[128,1024]{1,0:T(8,128)(2,1)S(1)}, bf16[128,1024]{1,0:T(8,128)(2,1)S(1)}, u32[]{:S(2)}, u32[]{:S(2)}) collective-permute-start(bf16[128,1024]{1,0:T(8,128)(2,1)S(1)} %slice.16), channel_id=1, source_target_pairs={{0,2},{1,3},{2,4},{3,5},{4,6},{5,7},{6,0},{7,1},{8,10},{9,11},{10,... | collective-permute-start | bytes 786440 | tf_op jit(solution)/shard_map/cond/branch_1_fun/ppermute | solution.py:531
  80.4 26.0 %copy-start.12 = (bf16[256,640]{1,0:T(8,128)(2,1)S(1)}, bf16[256,640]{1,0:T(8,128)(2,1)}, u32[]{:S(2)}) copy-start(bf16[256,640]{1,0:T(8,128)(2,1)} %copy-done.11) | copy-start | bytes 983044 | tf_op jit(solution)/shard_map/cond
  80.4 27.5 %copy-start.10 = (bf16[256,640]{1,0:T(8,128)(2,1)S(1)}, bf16[256,640]{1,0:T(8,128)(2,1)}, u32[]{:S(2)}) copy-start(bf16[256,640]{1,0:T(8,128)(2,1)} %copy-done.9) | copy-start | bytes 983044 | tf_op jit(solution)/shard_map/cond
  107.0 2.4 %collective-permute-start.17 = (bf16[256,1024]{1,0:T(8,128)(2,1)S(1)}, bf16[256,1024]{1,0:T(8,128)(2,1)S(1)}, u32[]{:S(2)}, u32[]{:S(2)}) collective-permute-start(bf16[256,1024]{1,0:T(8,128)(2,1)S(1)} %branch_1_fun.13), channel_id=1, source_target_pairs={{0,8},{8,0},{16,24},{24,16},{32,40},{40,32},{48,56},{56,48},{64,72... | collective-permute-start | bytes 1572872 | tf_op jit(solution)/shard_map/cond/branch_1_fun/ppermute | solution.py:552
  109.6 0.8 copy-start.25

commit v2 on v1

--- a/solution.py
+++ b/solution.py
@@ -122,6 +122,7 @@
     pages_ref,
     table_ref,
     from_ref,
+    back_ref,
     own_ref,
     other_ref,
     info_ref,
@@ -170,7 +171,9 @@
         spot_hot = one(iota((deep, children), 0) + i * deep == spot)
         by_child = mm_nt(place_hot, spot_hot).astype(BF16)
         by_row = mm(mm(grow_rows, by_child).astype(BF16), grow_columns)
-        from_ref[:, chunk(i, size)] = jnp.where(same_step, by_row, 0.0).astype(BF16)
+        by_row = jnp.where(same_step, by_row, 0.0)
+        from_ref[:, chunk(i, size)] = by_row.astype(BF16)
+        back_ref[chunk(i, size), :] = by_row.T.astype(BF16)
 
     over(wide // CHUNK, fill)
 
@@ -192,12 +195,13 @@
         functools.partial(arrive_kernel, slots),
         out_shape=(
             hot,
+            jax.ShapeDtypeStruct(hot.shape[::-1], BF16),
             hot,
             hot,
             jax.ShapeDtypeStruct((PARENTS_HERE, 8), jnp.int32),
         ),
         in_specs=[smem] + [vmem] * 4,
-        out_specs=(vmem, vmem, vmem, vmem),
+        out_specs=(vmem,) * 5,
         scratch_shapes=[pltpu.VMEM((groups, child_parent.shape[0]), F32)],
         compiler_params=pltpu.CompilerParams(vmem_limit_bytes=24 * 2**20),
         cost_estimate=pl.CostEstimate(flops=2 * 10**9, bytes_accessed=2**20, transcendentals=0),
@@ -243,14 +247,14 @@
     return acc_ref[...]
 
 
-def settle_kernel(hot_ref, rows_ref, out_ref, acc_ref):
+def place_kernel(hot_ref, rows_ref, out_ref, acc_ref):
     out_ref[...] = place_rows(hot_ref, rows_ref, acc_ref).astype(BF16)
 
 
-def settle(hot, rows):
+def place_slots(hot, rows):
     vmem = pl.BlockSpec(memory_space=pltpu.VMEM)
     return pl.pallas_call(
-        settle_kernel,
+        place_kernel,
         out_shape=jax.ShapeDtypeStruct((hot.shape[0], rows.shape[1]), BF16),
         in_specs=[vmem, vmem],
         out_specs=vmem,
@@ -264,35 +268,22 @@
     )(hot, rows)
 
 
-def pick_sum_kernel(hot_ref, rows_ref, out_ref, sum_ref, acc_ref, held_ref, sem):
-    copy = pltpu.make_async_copy(hot_ref, held_ref, sem)
-    copy.start()
-    copy.wait()
-    x = place_rows(held_ref, rows_ref, acc_ref)
-    out_ref[...] = x.astype(BF16)
+def sum_kernel(rows_ref, sum_ref):
+    x = rows_ref[...].astype(F32)
     total = jnp.sum(x * x, axis=1, keepdims=True)
     total = jnp.broadcast_to(total, (total.shape[0], 128)).T
     sum_ref[...] = jnp.broadcast_to(total[0:1], sum_ref.shape[:1] + total.shape[1:])[:, None, :]
 
 
-def pick_and_sum(hot, rows, copies):
+def row_sums(rows, copies):
     vmem = pl.BlockSpec(memory_space=pltpu.VMEM)
-    count = hot.shape[0]
     return pl.pallas_call(
-        pick_sum_kernel,
-        out_shape=(
-            jax.ShapeDtypeStruct((count, rows.shape[1]), BF16),
-            jax.ShapeDtypeStruct((copies, 1, count), F32),
-        ),
-        in_specs=[pl.BlockSpec(memory_space=pltpu.HBM), vmem],
-        out_specs=(vmem, vmem),
-        scratch_shapes=[
-            pltpu.VMEM((count, rows.shape[1]), F32),
-            pltpu.VMEM(hot.shape, BF16),
-            pltpu.SemaphoreType.DMA,
-        ],
+        sum_kernel,
+        out_shape=jax.ShapeDtypeStruct((copies, 1, rows.shape[0]), F32),
+        in_specs=[vmem],
+        out_specs=vmem,
         compiler_params=pltpu.CompilerParams(vmem_limit_bytes=24 * 2**20),
-    )(hot, rows)
+    )(rows)
 
 
 def row_scale(sum_ref, width):
@@ -496,8 +487,7 @@
     team = lax.axis_size("tensor")
     t = lax.axis_index("tensor")
     came = lax.all_to_all(send.reshape(groups, wide // groups, width), "sample", 0, 0)
-    from_hot, own_hot, other_hot, info = arrive(slots, groups, me, *tables, rows)
-    back_hot = from_hot.T
+    from_hot, back_hot, own_hot, other_hot, info = arrive(slots, groups, me, *tables, rows)
 
     def place(dy, dz):
         return ((t // 2 + dy) % 4) * 2 + (t + dz) % 2
@@ -525,12 +515,12 @@
     back_hot, own_hot, other_hot, from_hot = lax.optimization_barrier(
         (back_hot, own_hot, other_hot, from_hot)
     )
-    mine, sums = pick_and_sum(from_hot, came.reshape(wide, width), team)
+    mine = place_slots(from_hot, came.reshape(wide, width))
 
     def shift(block, dy, dz):
         return lax.ppermute(block, "tensor", moves(dy, dz))
 
-    sums = lax.all_to_all(sums, "tensor", 0, 0)
+    sums = lax.all_to_all(row_sums(mine, team), "tensor", 0, 0)
     b30, b10, b01 = shift(mine, 1, 0), shift(mine, -1, 0), shift(mine, 0, 1)
     (b30,) = lax.optimization_barrier((b30,))
     b20, b31 = shift(b30, 1, 0), shift(b30, 0, 1)
@@ -548,8 +538,8 @@
     )
     home = lax.all_to_all(back.reshape(groups, -1, back.shape[1]), "sample", 0, 0)
     home = home.reshape(-1, back.shape[1])
-    other = settle(other_hot, home)
-    return settle(own_hot, home) + lax.ppermute(other, "sample", swap(groups))
+    other = place_slots(other_hot, home)
+    return place_slots(own_hot, home) + lax.ppermute(other, "sample", swap(groups))
 
 
 def swap(groups):

time: 111 us -> 108 us (0.973)
    dynamic_slice x2, local copies, waits for them, and re-layouts: 3.62 us -> 4.95 us  [after_leave(): lax.dynamic_slice_in_dim(w, place(2, 1) * width, width)]
    cond x28 -> x26, local copies, waits for them, and re-layouts: 2.47 us -> 1.5 us
    pallas_call x4 -> x5, Pallas kernels: 4.34 us -> 4.23 us  [the longest x1 1.71 us: arrive(): pl.pallas_call(functools.partial(arrive_kernel, slots), out_shape=(hot, j...]
  transfers between devices with their start and end apart: 12 -> 12, of which waited for: 7 -> 7; matrix products, arithmetic and copies ran while one was open for 7% -> 8% of each run, Pallas kernels for 15% -> 15%
where the time goes in v2:
time: 108 us
  Pallas kernels  26.8 us (25%)
  starting transfers between devices  26.3 us (24%)
  blocking collectives  26 us (24%)
  waiting for transfers between devices  16.8 us (16%)
  local copies, waits for them, and re-layouts  9.07 us (8%)
  other arithmetic  1.85 us (2%)
    all_to_all x1, blocking collectives, after_leave(): lax.all_to_all(back.reshape(groups, -1, back.shape[1]), 'sample', 0, 0)  26 us
    ppermute x8, starting transfers between devices, shift(): return lax.ppermute(block, 'tensor', moves(dy, dz))  14.6 us
    pallas_call x2, Pallas kernels, project(): pl.pallas_call(functools.partial(project_kernel, wq.shape[0], count, befo...  11.8 us
    all_to_all x1, waiting for transfers between devices, after_leave(): lax.all_to_all(send.reshape(groups, wide // groups, width), 'sample', 0, 0)  7.98 us
    ppermute x8, waiting for transfers between devices, shift(): return lax.ppermute(block, 'tensor', moves(dy, dz))  7.75 us
    pallas_call x1, Pallas kernels, attend(): pl.pallas_call(functools.partial(attend_kernel, 8 * part), out_shape=jax....  7.3 us
    all_to_all x1, starting transfers between devices, after_leave(): lax.all_to_all(send.reshape(groups, wide // groups, width), 'sample', 0, 0)  6.13 us
    dynamic_slice x2, local copies, waits for them, and re-layouts, after_leave(): lax.dynamic_slice_in_dim(w, place(2, 1) * width, width)  4.95 us
  transfers between devices with their start and end apart: 12, of which 7 were waited for; matrix products, arithmetic and copies ran while one was open for 8% of the time, Pallas kernels for 15%

profile of v2, /device:TPU:1, one launch (start us, length us, event | category | flops | bytes accessed | tf_op | source)
XLA Modules:
  0.0 108.0 jit_solution(7128690571271470544)
XLA Ops:
  0.0 1.4 %collective-permute-start.18 = (bf16[256,1024]{1,0:T(8,128)(2,1)}, bf16[256,1024]{1,0:T(8,128)(2,1)S(1)}, u32[]{:S(2)}, u32[]{:S(2)}) collective-permute-start(bf16[256,1024]{1,0:T(8,128)(2,1)} %own_ref.1), channel_id=1, source_target_pairs={{0,8},{8,0},{16,24},{24,16},{32,40},{40,32},{48,56},{56,48},{64,72... | collective-permute-start | bytes 1572872 | tf_op jit(solution)/shard_map/ppermute | solution.py:566
  1.4 1.6 %shard_map.102 = (bf16[640,256]{1,0:T(8,128)(2,1)S(1)}, bf16[640,256]{1,0:T(8,128)(2,1)S(1)}, s32[1]{0:T(128)}) custom-call(s32[1]{0:T(128)} %bitcast.28.me_ref, s32[1,1024]{1,0:T(1,128)} %bitcast.41, s32[1,128]{1,0:T(1,128)} %bitcast.45), custom_call_target="tpu_custom_call" | custom-call | flops 1000000000 | bytes 1048576 | tf_op jit(solution)/shard_map/pallas_call | solution.py:106
  3.0 0.0 copy-start.28
  3.0 0.0 copy-start.29
  3.1 0.0 copy-start.32
  3.1 0.0 copy-start.33
  3.1 0.0 copy-start.34
  3.1 0.1 collective-permute-done.18.other_ref
  3.2 1.9 %shard_map.103 = bf16[640,1024]{1,0:T(8,128)(2,1)} custom-call(bf16[640,256]{1,0:T(8,128)(2,1)S(1)} %get-tuple-element.143.own_hot_ref, bf16[640,256]{1,0:T(8,128)(2,1)S(1)} %get-tuple-element.144.other_hot_ref, bf16[256,1024]{1,0:T(8,128)(2,1)S(1)} %copy-done.26, bf16[256,1024]{1,0:T(8,128)(2,1)S(1)} %collective-permute-done.18.other_ref), custom_call_target="tpu_custom_call" | custom-call | tf_op jit(solution)/shard_map/pallas_call | solution.py:228
  5.8 101.4 %conditional.1 = (bf16[256,1024]{1,0:T(8,128)(2,1)S(1)}) conditional(s32[]{:T(128)} %bitcast.31, (s32[1024]{0:T(1024)S(1)}, s32[128]{0:T(128)S(1)}, s32[128]{0:T(128)S(1)}, s32[128,5]{0,1:T(8,128)S(1)}, s32[1]{0:T(128)}, /*index=5*/bf16[256,1024]{1,0:T(8,128)(2,1)S(1)}, bf16[256,1024]{1,0:T(8,128)(2,1)S(1)}, bf16[8192]{0:T(1024)(128)(2,1)S(1)}, ...), branch_computations={%region_0.1_spmd, %region_1.2_spmd} | conditional | flops 20448665600 | bytes 182706208 | solution.py:580
  6.0 6.1 %all-to-all-start.3 = ((bf16[16,40,1024]{2,1,0:T(8,128)(2,1)}), bf16[16,40,1024]{2,1,0:T(8,128)(2,1)S(1)}, u32[]{:S(2)}, u32[]{:S(2)}) async-start(bf16[16,40,1024]{2,1,0:T(8,128)(2,1)} %bitcast.40), calls=%async_computation.3 | async-start | bytes 2621440 | tf_op jit(solution)/shard_map/cond/branch_1_fun/all_to_all | solution.py:489
  12.2 0.6 reshape.100
  12.8 0.1 tile.12
  12.9 0.1 copy.20
  13.1 1.7 %branch_1_fun.8 = (bf16[256,640]{1,0:T(8,128)(2,1)S(1)}, bf16[640,256]{1,0:T(8,128)(2,1)S(1)}, bf16[256,640]{1,0:T(8,128)(2,1)S(1)}, bf16[256,640]{1,0:T(8,128)(2,1)S(1)}, s32[8,8]{1,0:T(8,128)S(1)}) custom-call(s32[1]{0:T(128)} %get-tuple-element.94.me_ref, s32[1,1024]{1,0:T(1,128)S(1)} %bitcast.44, s32[1,128]{1,0:T(1,128)S(1)} %bitcast.48, ...), custom_call_target="tpu_custom_call" | custom-call | flops 2000000000 | bytes 1048576 | tf_op jit(solution)/shard_map/cond/branch_1_fun/pallas_call | solution.py:194
  14.8 0.0 copy-start.8
  14.8 0.7 copy-done.8
  15.5 0.7 copy-done.10
  16.2 0.2 multiply_reduce_fusion.1
  16.4 0.1 broadcast_in_dim.6
  16.5 0.1 reshape.99
  16.6 0.5 fusion.1
  17.1 0.8 pad_maximum_fusion.2
  17.9 1.9 %constant_dynamic-slice_fusion.3 = (bf16[1024,128]{1,0:T(8,128)(2,1)}, bf16[1024,128]{1,0:T(8,128)(2,1)}) fusion(bf16[8192,128]{1,0:T(8,128)(2,1)} %get-tuple-element.108.refs_7_.refs_6_, s32[]{:T(128)S(6)} %select_n.149, bf16[8192,128]{1,0:T(8,128)(2,1)} %get-tuple-element.107.refs_6_.refs_5_), kind=kLoop, calls=%fused_computation.20 | loop fusion | bytes 1048580 | tf_op jit(solution)/shard_map/cond/branch_1_fun/dynamic_slice | solution.py:498
  19.8 3.1 %constant_dynamic-slice_fusion.5.wq_ref = bf16[1024,1024]{1,0:T(8,128)(2,1)} fusion(bf16[8192,1024]{1,0:T(8,128)(2,1)} %get-tuple-element.106.refs_5_.refs_4_, s32[]{:T(128)S(6)} %select_n.149), kind=kLoop, calls=%fused_computation.22 | loop fusion | bytes 4194308 | tf_op jit(solution)/shard_map/cond/branch_1_fun/dynamic_slice | solution.py:498
  22.9 8.0 %all-to-all-done.3 = bf16[16,40,1024]{2,1,0:T(8,128)(2,1)S(1)} async-done(((bf16[16,40,1024]{2,1,0:T(8,128)(2,1)}), bf16[16,40,1024]{2,1,0:T(8,128)(2,1)S(1)}, u32[]{:S(2)}, u32[]{:S(2)}) %all-to-all-start.3) | async-done | bytes 1310752 | tf_op jit(solution)/shard_map/cond/branch_1_fun/all_to_all | solution.py:489
  30.8 0.6 branch_1_fun.9.rows_ref.refs_0_
  31.4 1.4 %collective-permute-start.9 = (bf16[256,1024]{1,0:T(8,128)(2,1)S(1)}, bf16[256,1024]{1,0:T(8,128)(2,1)S(1)}, u32[]{:S(2)}, u32[]{:S(2)}) collective-permute-start(bf16[256,1024]{1,0:T(8,128)(2,1)S(1)} %branch_1_fun.9.rows_ref.refs_0_), channel_id=1, source_target_pairs={{0,2},{1,3},{2,4},{3,5},{4,6},{5,7},{6,0},{7,1},{8,10},{9,11},{10,... | collective-permute-start | bytes 1572872 | tf_op jit(solution)/shard_map/cond/branch_1_fun/ppermute | solution.py:521
  32.8 3.3 %collective-permute-start.11 = (bf16[256,1024]{1,0:T(8,128)(2,1)S(1)}, bf16[256,1024]{1,0:T(8,128)(2,1)S(1)}, u32[]{:S(2)}, u32[]{:S(2)}) collective-permute-start(bf16[256,1024]{1,0:T(8,128)(2,1)S(1)} %branch_1_fun.9.rows_ref.refs_0_), channel_id=1, source_target_pairs={{0,1},{1,0},{2,3},{3,2},{4,5},{5,4},{6,7},{7,6},{8,9},{9,8},{10,11... | collective-permute-start | bytes 1572872 | tf_op jit(solution)/shard_map/cond/branch_1_fun/ppermute | solution.py:521
  36.1 1.5 %collective-permute-start.14 = (bf16[256,1024]{1,0:T(8,128)(2,1)S(1)}, bf16[256,1024]{1,0:T(8,128)(2,1)S(1)}, u32[]{:S(2)}, u32[]{:S(2)}) collective-permute-start(bf16[256,1024]{1,0:T(8,128)(2,1)S(1)} %branch_1_fun.9.rows_ref.refs_0_), channel_id=1, source_target_pairs={{0,6},{1,7},{2,0},{3,1},{4,2},{5,3},{6,4},{7,5},{8,14},{9,15},{10,... | collective-permute-start | bytes 1572872 | tf_op jit(solution)/shard_map/cond/branch_1_fun/ppermute | solution.py:521
  37.6 0.1 pad_add_fusion.3.order_ref
  37.7 0.8 branch_1_fun.10
  38.5 3.3 %all-to-all-start.4 = ((f32[8,1,256]{2,1,0:T(1,128)}), f32[8,1,256]{2,1,0:T(1,128)S(1)}, u32[]{:S(2)}, u32[]{:S(2)}) async-start(f32[8,1,256]{2,1,0:T(1,128)} %branch_1_fun.10), calls=%async_computation.4 | async-start | bytes 16384 | tf_op jit(solution)/shard_map/cond/branch_1_fun/all_to_all | solution.py:523
  41.8 3.8 %collective-permute-done.9.refs_1_ = bf16[256,1024]{1,0:T(8,128)(2,1)S(1)} collective-permute-done((bf16[256,1024]{1,0:T(8,128)(2,1)S(1)}, bf16[256,1024]{1,0:T(8,128)(2,1)S(1)}, u32[]{:S(2)}, u32[]{:S(2)}) %collective-permute-start.9) | collective-permute-done | bytes 524320 | tf_op jit(solution)/shard_map/cond/branch_1_fun/ppermute | solution.py:521
  45.6 3.3 %collective-permute-start.13 = (bf16[256,1024]{1,0:T(8,128)(2,1)S(1)}, bf16[256,1024]{1,0:T(8,128)(2,1)S(1)}, u32[]{:S(2)}, u32[]{:S(2)}) collective-permute-start(bf16[256,1024]{1,0:T(8,128)(2,1)S(1)} %collective-permute-done.9.refs_1_), channel_id=1, source_target_pairs={{0,1},{1,0},{2,3},{3,2},{4,5},{5,4},{6,7},{7,6},{8,9},{9,8},{10,11... | collective-permute-start | bytes 1572872 | tf_op jit(solution)/shard_map/cond/branch_1_fun/ppermute | solution.py:521
  48.9 0.0 collective-permute-start.10
  48.9 0.0 collective-permute-done.11.refs_3_
  48.9 2.7 %collective-permute-start.12 = (bf16[256,1024]{1,0:T(8,128)(2,1)S(1)}, bf16[256,1024]{1,0:T(8,128)(2,1)S(1)}, u32[]{:S(2)}, u32[]{:S(2)}) collective-permute-start(bf16[256,1024]{1,0:T(8,128)(2,1)S(1)} %collective-permute-done.11.refs_3_), channel_id=1, source_target_pairs={{0,6},{1,7},{2,0},{3,1},{4,2},{5,3},{6,4},{7,5},{8,14},{9,15},{10,... | collective-permute-start | bytes 1572872 | tf_op jit(solution)/shard_map/cond/branch_1_fun/ppermute | solution.py:521
  51.6 0.1 pad_add_fusion.2.order_ref
  51.6 0.7 copy.17.refs_4_.refs_3_
  52.4 0.0 all-to-all-done.4.sum_ref
  52.4 0.0 collective-permute-done.14.refs_2_
  52.4 0.0 copy-start.23
  52.4 0.0 copy-start.25
  52.4 6.6 %branch_1_fun.11.refs_7_ = f32[256,1280]{1,0:T(8,128)S(1)} custom-call(s32[4]{0:T(128)S(1)} %pad_add_fusion.2.order_ref, f32[8,1,256]{2,1,0:T(1,128)S(1)} %all-to-all-done.4.sum_ref, bf16[256,1024]{1,0:T(8,128)(2,1)S(1)} %branch_1_fun.9.rows_ref.refs_0_, bf16[256,1024]{1,0:T(8,128)(2,1)S(1)} %collective-permute-done.9.refs_1_, ...), custom_call_target="tpu_custom_call" | custom-call | flops 5368709120 | bytes 10485760 | tf_op jit(solution)/shard_map/cond/branch_1_fun/pallas_call | solution.py:343
  59.0 1.6 %collective-permute-done.12.refs_1_ = bf16[256,1024]{1,0:T(8,128)(2,1)S(1)} collective-permute-done((bf16[256,1024]{1,0:T(8,128)(2,1)S(1)}, bf16[256,1024]{1,0:T(8,128)(2,1)S(1)}, u32[]{:S(2)}, u32[]{:S(2)}) %collective-permute-start.12) | collective-permute-done | bytes 524320 | tf_op jit(solution)/shard_map/cond/branch_1_fun/ppermute | solution.py:521
  60.6 0.0 collective-permute-done.13.refs_2_
  60.6 1.1 %collective-permute-done.10.refs_0_ = bf16[256,1024]{1,0:T(8,128)(2,1)} collective-permute-done((bf16[256,1024]{1,0:T(8,128)(2,1)S(1)}, bf16[256,1024]{1,0:T(8,128)(2,1)}, u32[]{:S(2)}, u32[]{:S(2)}) %collective-permute-start.10) | collective-permute-done | bytes 524320 | tf_op jit(solution)/shard_map/cond/branch_1_fun/ppermute | solution.py:521
  61.9 0.0 copy-start.31
  61.9 2.4 %collective-permute-start.16 = (bf16[128,1024]{1,0:T(8,128)(2,1)S(1)}, bf16[128,1024]{1,0:T(8,128)(2,1)S(1)}, u32[]{:S(2)}, u32[]{:S(2)}) collective-permute-start(bf16[128,1024]{1,0:T(8,128)(2,1)S(1)} %slice.17), channel_id=1, source_target_pairs={{0,6},{1,7},{2,0},{3,1},{4,2},{5,3},{6,4},{7,5},{8,14},{9,15},{10,... | collective-permute-start | bytes 786440 | tf_op jit(solution)/shard_map/cond/branch_1_fun/ppermute | solution.py:521
  64.2 0.0 collective-permute-start.15
  64.3 5.2 %branch_1_fun.12.before_ref = f32[256,1280]{1,0:T(8,128)S(1)} custom-call(s32[3]{0:T(128)S(1)} %pad_add_fusion.3.order_ref, f32[8,1,256]{2,1,0:T(1,128)S(1)} %all-to-all-done.4.sum_ref, bf16[256,1024]{1,0:T(8,128)(2,1)} %collective-permute-done.10.refs_0_, bf16[256,1024]{1,0:T(8,128)(2,1)S(1)} %collective-permute-done.12.refs_1_, ...), custom_call_target="tpu_custom_call" | custom-call | flops 4026531840 | bytes 7864320 | tf_op jit(solution)/shard_map/cond/branch_1_fun/pallas_call | solution.py:343
  69.4 0.0 collective-permute-done.16.high_ref
  69.4 1.2 %collective-permute-done.15.low_ref = bf16[128,1024]{1,0:T(8,128)(2,1)S(1)} collective-permute-done((bf16[128,1024]{1,0:T(8,128)(2,1)S(1)}, bf16[128,1024]{1,0:T(8,128)(2,1)S(1)}, u32[]{:S(2)}, u32[]{:S(2)}) %collective-permute-start.15) | collective-permute-done | bytes 262176 | tf_op jit(solution)/shard_map/cond/branch_1_fun/ppermute | solution.py:521
  70.7 7.3 %branch_1_fun.13 = bf16[640,1024]{1,0:T(8,128)(2,1)S(1)} custom-call(s32[8,8]{1,0:T(8,128)S(1)} %get-tuple-element.111.info_ref, f32[8,1,256]{2,1,0:T(1,128)S(1)} %all-to-all-done.4.sum_ref, bf16[128,1024]{1,0:T(8,128)(2,1)S(1)} %collective-permute-done.15.low_ref, bf16[128,1024]{1,0:T(8,128)(2,1)S(1)} %collective-permute-done.16.high_ref, ...), custom_call_target="tpu_custom_call" | custom-call | flops 4026531840 | bytes 2621440 | tf_op jit(solution)/shard_map/cond/branch_1_fun/pallas_call | solution.py:458
  78.0 0.0 copy-start.9
  78.0 26.0 %all_to_all.25 = bf16[16,40,1024]{2,1,0:T(8,128)(2,1)S(1)} all-to-all(bf16[16,40,1024]{2,1,0:T(8,128)(2,1)S(1)} %bitcast.39), channel_id=1, replica_groups=mesh['sample'=16,'tensor'=8] {'sample'}, dimensions={0} | all-to-all | bytes 2621440 | tf_op jit(solution)/shard_map/cond/branch_1_fun/all_to_all | solution.py:539
  104.0 0.6 branch_1_fun.15
  104.6 0.9 collective-permute-start.17
  105.5 0.6 branch_1_fun.14
  106.1 1.0 collective-permute-done.17
  107.0 0.2 add.208
  107.2 0.0 copy-start.27
  107.2 0.8 copy-done.27
  (34 shorter events, 0.1 us)
Async XLA Ops:
  0.0 3.2 %copy-start.26 = (bf16[256,1024]{1,0:T(8,128)(2,1)S(1)}, bf16[256,1024]{1,0:T(8,128)(2,1)}, u32[]{:S(2)}) copy-start(bf16[256,1024]{1,0:T(8,128)(2,1)} %own_ref.1) | copy-start | bytes 1572868
  0.0 3.2 %collective-permute-start.18 = (bf16[256,1024]{1,0:T(8,128)(2,1)}, bf16[256,1024]{1,0:T(8,128)(2,1)S(1)}, u32[]{:S(2)}, u32[]{:S(2)}) collective-permute-start(bf16[256,1024]{1,0:T(8,128)(2,1)} %own_ref.1), channel_id=1, source_target_pairs={{0,8},{8,0},{16,24},{24,16},{32,40},{40,32},{48,56},{56,48},{64,72... | collective-permute-start | bytes 1572872 | tf_op jit(solution)/shard_map/ppermute | solution.py:566
  3.0 2.7 %copy-start.28 = (bf16[8192]{0:T(1024)(128)(2,1)S(1)}, bf16[8192]{0:T(1024)(128)(2,1)}, u32[]{:S(2)}) copy-start(bf16[8192]{0:T(1024)(128)(2,1)} %param.13) | copy-start | bytes 49156
  3.0 2.7 %copy-start.29 = (s32[128,5]{0,1:T(8,128)S(1)}, s32[128,5]{0,1:T(8,128)}, u32[]{:S(2)}) copy-start(s32[128,5]{0,1:T(8,128)} %param.20) | copy-start | bytes 7684
  3.1 2.7 %copy-start.32 = (s32[1024]{0:T(1024)S(1)}, s32[1024]{0:T(1024)}, u32[]{:S(2)}) copy-start(s32[1024]{0:T(1024)} %param.21) | copy-start | bytes 12292
  3.1 2.7 %copy-start.33 = (s32[128]{0:T(128)S(1)}, s32[128]{0:T(128)}, u32[]{:S(2)}) copy-start(s32[128]{0:T(128)} %param.18) | copy-start | bytes 1540
  3.1 2.7 %copy-start.34 = (s32[128]{0:T(128)S(1)}, s32[128]{0:T(128)}, u32[]{:S(2)}) copy-start(s32[128]{0:T(128)} %param.19) | copy-start | bytes 1540
  6.0 24.8 %all-to-all-start.3 = ((bf16[16,40,1024]{2,1,0:T(8,128)(2,1)}), bf16[16,40,1024]{2,1,0:T(8,128)(2,1)S(1)}, u32[]{:S(2)}, u32[]{:S(2)}) async-start(bf16[16,40,1024]{2,1,0:T(8,128)(2,1)} %bitcast.40), calls=%async_computation.3 | async-start | bytes 2621440 | tf_op jit(solution)/shard_map/cond/branch_1_fun/all_to_all | solution.py:489
  14.8 0.7 copy-start.8
  15.5 0.7 copy-start.10
  16.2 6.6 %copy-start.20 = (bf16[640,256]{1,0:T(8,128)(2,1)}, bf16[640,256]{1,0:T(8,128)(2,1)S(1)}, u32[]{:S(2)}) copy-start(bf16[640,256]{1,0:T(8,128)(2,1)S(1)} %get-tuple-element.129.back_ref) | copy-start | bytes 983044 | tf_op jit(solution)/shard_map/cond
  31.4 14.1 %collective-permute-start.9 = (bf16[256,1024]{1,0:T(8,128)(2,1)S(1)}, bf16[256,1024]{1,0:T(8,128)(2,1)S(1)}, u32[]{:S(2)}, u32[]{:S(2)}) collective-permute-start(bf16[256,1024]{1,0:T(8,128)(2,1)S(1)} %branch_1_fun.9.rows_ref.refs_0_), channel_id=1, source_target_pairs={{0,2},{1,3},{2,4},{3,5},{4,6},{5,7},{6,0},{7,1},{8,10},{9,11},{10,... | collective-permute-start | bytes 1572872 | tf_op jit(solution)/shard_map/cond/branch_1_fun/ppermute | solution.py:521
  32.8 16.1 %collective-permute-start.11 = (bf16[256,1024]{1,0:T(8,128)(2,1)S(1)}, bf16[256,1024]{1,0:T(8,128)(2,1)S(1)}, u32[]{:S(2)}, u32[]{:S(2)}) collective-permute-start(bf16[256,1024]{1,0:T(8,128)(2,1)S(1)} %branch_1_fun.9.rows_ref.refs_0_), channel_id=1, source_target_pairs={{0,1},{1,0},{2,3},{3,2},{4,5},{5,4},{6,7},{7,6},{8,9},{9,8},{10,11... | collective-permute-start | bytes 1572872 | tf_op jit(solution)/shard_map/cond/branch_1_fun/ppermute | solution.py:521
  36.1 16.3 %collective-permute-start.14 = (bf16[256,1024]{1,0:T(8,128)(2,1)S(1)}, bf16[256,1024]{1,0:T(8,128)(2,1)S(1)}, u32[]{:S(2)}, u32[]{:S(2)}) collective-permute-start(bf16[256,1024]{1,0:T(8,128)(2,1)S(1)} %branch_1_fun.9.rows_ref.refs_0_), channel_id=1, source_target_pairs={{0,6},{1,7},{2,0},{3,1},{4,2},{5,3},{6,4},{7,5},{8,14},{9,15},{10,... | collective-permute-start | bytes 1572872 | tf_op jit(solution)/shard_map/cond/branch_1_fun/ppermute | solution.py:521
  38.5 13.9 %all-to-all-start.4 = ((f32[8,1,256]{2,1,0:T(1,128)}), f32[8,1,256]{2,1,0:T(1,128)S(1)}, u32[]{:S(2)}, u32[]{:S(2)}) async-start(f32[8,1,256]{2,1,0:T(1,128)} %branch_1_fun.10), calls=%async_computation.4 | async-start | bytes 16384 | tf_op jit(solution)/shard_map/cond/branch_1_fun/all_to_all | solution.py:523
  45.6 15.1 %collective-permute-start.13 = (bf16[256,1024]{1,0:T(8,128)(2,1)S(1)}, bf16[256,1024]{1,0:T(8,128)(2,1)S(1)}, u32[]{:S(2)}, u32[]{:S(2)}) collective-permute-start(bf16[256,1024]{1,0:T(8,128)(2,1)S(1)} %collective-permute-done.9.refs_1_), channel_id=1, source_target_pairs={{0,1},{1,0},{2,3},{3,2},{4,5},{5,4},{6,7},{7,6},{8,9},{9,8},{10,11... | collective-permute-start | bytes 1572872 | tf_op jit(solution)/shard_map/cond/branch_1_fun/ppermute | solution.py:521
  48.9 12.9 %collective-permute-start.10 = (bf16[256,1024]{1,0:T(8,128)(2,1)S(1)}, bf16[256,1024]{1,0:T(8,128)(2,1)}, u32[]{:S(2)}, u32[]{:S(2)}) collective-permute-start(bf16[256,1024]{1,0:T(8,128)(2,1)S(1)} %collective-permute-done.9.refs_1_), channel_id=1, source_target_pairs={{0,2},{1,3},{2,4},{3,5},{4,6},{5,7},{6,0},{7,1},{8,10},{9,11},{10,... | collective-permute-start | bytes 1572872 | tf_op jit(solution)/shard_map/cond/branch_1_fun/ppermute | solution.py:521
  48.9 11.8 %collective-permute-start.12 = (bf16[256,1024]{1,0:T(8,128)(2,1)S(1)}, bf16[256,1024]{1,0:T(8,128)(2,1)S(1)}, u32[]{:S(2)}, u32[]{:S(2)}) collective-permute-start(bf16[256,1024]{1,0:T(8,128)(2,1)S(1)} %collective-permute-done.11.refs_3_), channel_id=1, source_target_pairs={{0,6},{1,7},{2,0},{3,1},{4,2},{5,3},{6,4},{7,5},{8,14},{9,15},{10,... | collective-permute-start | bytes 1572872 | tf_op jit(solution)/shard_map/cond/branch_1_fun/ppermute | solution.py:521
  52.4 11.8 %copy-start.23 = (bf16[8192,128]{1,0:T(8,128)(2,1)S(1)}, bf16[8192,128]{1,0:T(8,128)(2,1)}, u32[]{:S(2)}) copy-start(bf16[8192,128]{1,0:T(8,128)(2,1)} %get-tuple-element.107.refs_6_.refs_5_) | copy-start | bytes 6291460 | tf_op jit(solution)/shard_map/cond
  52.4 11.8 %copy-start.25 = (bf16[8192,128]{1,0:T(8,128)(2,1)S(1)}, bf16[8192,128]{1,0:T(8,128)(2,1)}, u32[]{:S(2)}) copy-start(bf16[8192,128]{1,0:T(8,128)(2,1)} %get-tuple-element.108.refs_7_.refs_6_) | copy-start | bytes 6291460 | tf_op jit(solution)/shard_map/cond
  61.8 8.9 %copy-start.1 = (bf16[1024,1024]{1,0:T(8,128)(2,1)S(1)}, bf16[1024,1024]{1,0:T(8,128)(2,1)}, u32[]{:S(2)}) copy-start(bf16[1024,1024]{1,0:T(8,128)(2,1)} %constant_dynamic-slice_fusion.5.wq_ref) | copy-start | bytes 6291460 | tf_op jit(solution)/shard_map/cond
  61.8 8.9 %copy-start.13 = (bf16[1024,128]{1,0:T(8,128)(2,1)S(1)}, bf16[1024,128]{1,0:T(8,128)(2,1)}, u32[]{:S(2)}) copy-start(bf16[1024,128]{1,0:T(8,128)(2,1)} %get-tuple-element.124.wv_ref) | copy-start | bytes 786436 | tf_op jit(solution)/shard_map/cond
  61.8 8.9 %copy-start.14 = (bf16[1024,128]{1,0:T(8,128)(2,1)S(1)}, bf16[1024,128]{1,0:T(8,128)(2,1)}, u32[]{:S(2)}) copy-start(bf16[1024,128]{1,0:T(8,128)(2,1)} %get-tuple-element.123.wk_ref) | copy-start | bytes 786436 | tf_op jit(solution)/shard_map/cond
  61.8 8.9 %copy-start.17 = (f32[256,128]{1,0:T(8,128)S(1)}, f32[256,128]{1,0:T(8,128)}, u32[]{:S(2)}) copy-start(f32[256,128]{1,0:T(8,128)} %get-tuple-element.127.sin_ref) | copy-start | bytes 393220 | tf_op jit(solution)/shard_map/cond
  61.8 8.9 %copy-start.21 = (bf16[640,256]{1,0:T(8,128)(2,1)S(1)}, bf16[640,256]{1,0:T(8,128)(2,1)}, u32[]{:S(2)}) copy-start(bf16[640,256]{1,0:T(8,128)(2,1)} %copy-done.20) | copy-start | bytes 983044 | tf_op jit(solution)/shard_map/cond
  61.9 8.9 %copy-start.31 = (bf16[40,2,128,128]{3,2,1,0:T(8,128)(2,1)S(1)}, bf16[40,2,128,128]{3,2,1,0:T(8,128)(2,1)}, u32[]{:S(2)}) copy-start(bf16[40,2,128,128]{3,2,1,0:T(8,128)(2,1)} %get-tuple-element.128.pool_ref) | copy-start | bytes 7864324 | tf_op jit(solution)/shard_map/cond
  61.9 7.6 %collective-permute-start.16 = (bf16[128,1024]{1,0:T(8,128)(2,1)S(1)}, bf16[128,1024]{1,0:T(8,128)(2,1)S(1)}, u32[]{:S(2)}, u32[]{:S(2)}) collective-permute-start(bf16[128,1024]{1,0:T(8,128)(2,1)S(1)} %slice.17), channel_id=1, source_target_pairs={{0,6},{1,7},{2,0},{3,1},{4,2},{5,3},{6,4},{7,5},{8,14},{9,15},{10,... | collective-permute-start | bytes 786440 | tf_op jit(solution)/shard_map/cond/branch_1_fun/ppermute | solution.py:521
  64.2 6.4 %collective-permute-start.15 = (bf16[128,1024]{1,0:T(8,128)(2,1)S(1)}, bf16[128,1024]{1,0:T(8,128)(2,1)S(1)}, u32[]{:S(2)}, u32[]{:S(2)}) collective-permute-start(bf16[128,1024]{1,0:T(8,128)(2,1)S(1)} %slice.16), channel_id=1, source_target_pairs={{0,2},{1,3},{2,4},{3,5},{4,6},{5,7},{6,0},{7,1},{8,10},{9,11},{10,... | collective-permute-start | bytes 786440 | tf_op jit(solution)/shard_map/cond/branch_1_fun/ppermute | solution.py:521
  78.0 26.0 %copy-start.11 = (bf16[256,640]{1,0:T(8,128)(2,1)S(1)}, bf16[256,640]{1,0:T(8,128)(2,1)}, u32[]{:S(2)}) copy-start(bf16[256,640]{1,0:T(8,128)(2,1)} %copy-done.10) | copy-start | bytes 983044 | tf_op jit(solution)/shard_map/cond
  78.0 27.5 %copy-start.9 = (bf16[256,640]{1,0:T(8,128)(2,1)S(1)}, bf16[256,640]{1,0:T(8,128)(2,1)}, u32[]{:S(2)}) copy-start(bf16[256,640]{1,0:T(8,128)(2,1)} %copy-done.8) | copy-start | bytes 983044 | tf_op jit(solution)/shard_map/cond
  104.6 2.4 %collective-permute-start.17 = (bf16[256,1024]{1,0:T(8,128)(2,1)S(1)}, bf16[256,1024]{1,0:T(8,128)(2,1)S(1)}, u32[]{:S(2)}, u32[]{:S(2)}) collective-permute-start(bf16[256,1024]{1,0:T(8,128)(2,1)S(1)} %branch_1_fun.15), channel_id=1, source_target_pairs={{0,8},{8,0},{16,24},{24,16},{32,40},{40,32},{48,56},{56,48},{64,72... | collective-permute-start | bytes 1572872 | tf_op jit(solution)/shard_map/cond/branch_1_fun/ppermute | solution.py:542
  107.2 0.8 copy-start.27

commit v3 on v2

--- a/solution.py
+++ b/solution.py
@@ -302,48 +302,60 @@
     acc[:, wide:] += mm(x, wkv)
 
 
-def project_kernel(width, count, first, order_ref, sum_ref, *refs):
-    blocks = refs[:count]
-    gain_ref, wq_ref, wk_ref, wv_ref = refs[count : count + 4]
-    before = None if first else refs[count + 4]
+def project_kernel(width, places, first, order_ref, sum_ref, *refs):
+    count = len(places)
+    pieces = sum(len(place) for place in places)
+    blocks = refs[:pieces]
+    gain_ref, wq_ref, wk_ref, wv_ref = refs[pieces : pieces + 4]
+    before = None if first else refs[pieces + 4]
     acc_ref, x_ref, wq_held, wkv_held, x_sems, w_sems = refs[-6:]
     part = x_ref.shape[2]
 
-    def copies(i, block):
+    def copies(i):
         at = chunk(order_ref[i], part)
         return [
-            pltpu.make_async_copy(block, x_ref.at[i], x_sems.at[i]),
             pltpu.make_async_copy(wq_ref.at[at], wq_held.at[i], w_sems.at[i, 0]),
             pltpu.make_async_copy(wk_ref.at[at], wkv_held.at[i, :, :HEAD], w_sems.at[i, 1]),
             pltpu.make_async_copy(wv_ref.at[at], wkv_held.at[i, :, HEAD:], w_sems.at[i, 2]),
         ]
 
-    for i in range(count):
-        for copy in copies(i, blocks[i]):
+    for i, place in enumerate(places):
+        for block, first_row in place:
+            cut = pl.ds(first_row, blocks[block].shape[0])
+            pltpu.make_async_copy(blocks[block], x_ref.at[i, cut], x_sems.at[i]).start()
+        for copy in copies(i):
             copy.start()
     scale = row_scale(sum_ref, width)[:, 0:1]
     acc_ref[...] = jnp.zeros_like(acc_ref) if first else before[...]
 
     @pl.loop(0, count)
     def _(i):
-        for copy in copies(i, blocks[0]):
+        pltpu.make_async_copy(x_ref.at[i], x_ref.at[i], x_sems.at[i]).wait()
+        for copy in copies(i):
             copy.wait()
         x = normed(x_ref[i], scale, gain_ref[order_ref[i]])
         add_products(acc_ref, x, wq_held[i], wkv_held[i])
 
 
 def project(order, sums, blocks, gain, wq, wk, wv, before=None):
-    rows, part = blocks[0].shape
+    part = blocks[0][0].shape[1]
+    rows = sum(piece.shape[0] for piece in blocks[0])
     columns = wq.shape[1] + wk.shape[1] + wv.shape[1]
     count = len(blocks)
+    pieces = [piece for block in blocks for piece in block]
+    places, number = [], 0
+    for block in blocks:
+        starts = [sum(piece.shape[0] for piece in block[:i]) for i in range(len(block))]
+        places.append([(number + i, start) for i, start in enumerate(starts)])
+        number += len(block)
     smem = pl.BlockSpec(memory_space=pltpu.SMEM)
     vmem = pl.BlockSpec(memory_space=pltpu.VMEM)
     hbm = pl.BlockSpec(memory_space=pltpu.HBM)
     extra = [] if before is None else [before]
     return pl.pallas_call(
-        functools.partial(project_kernel, wq.shape[0], count, before is None),
+        functools.partial(project_kernel, wq.shape[0], places, before is None),
         out_shape=jax.ShapeDtypeStruct((rows, columns), F32),
-        in_specs=[smem, vmem] + [hbm] * count + [vmem, hbm, hbm, hbm] + [vmem] * len(extra),
+        in_specs=[smem, vmem] + [hbm] * number + [vmem, hbm, hbm, hbm] + [vmem] * len(extra),
         out_specs=vmem,
         scratch_shapes=[
             pltpu.VMEM((count, rows, part), BF16),
@@ -358,7 +370,7 @@
             bytes_accessed=2 * part * count * columns,
             transcendentals=0,
         ),
-    )(order, sums, *blocks, gain, wq, wk, wv, *extra)
+    )(order, sums, *pieces, gain, wq, wk, wv, *extra)
 
 
 def attend_kernel(
@@ -522,16 +534,28 @@
 
     sums = lax.all_to_all(row_sums(mine, team), "tensor", 0, 0)
     b30, b10, b01 = shift(mine, 1, 0), shift(mine, -1, 0), shift(mine, 0, 1)
+    half = rows // 2
     (b30,) = lax.optimization_barrier((b30,))
-    b20, b31 = shift(b30, 1, 0), shift(b30, 0, 1)
-    second = (b20, shift(b01, -1, 0), b31)
+    b20, b31_low = shift(b30, 1, 0), shift(b30[:half], 0, 1)
+    b01, b10, sums = lax.optimization_barrier((b01, b10, sums))
+    b11_high = shift(b01[half:], -1, 0)
+    b31_high, b11_low = shift(b30[half:], 0, 1), shift(b01[:half], -1, 0)
+    b31_low, b11_high = lax.optimization_barrier((b31_low, b11_high))
+    low, high = shift(b31_low, 1, 0), shift(b11_high, -1, 0)
     acc = project(
-        order((0, 0), (3, 0), (1, 0), (0, 1)), sums, [mine, b30, b10, b01], gain, wq, wk, wv
+        order((0, 0), (3, 0), (1, 0), (0, 1)), sums, [[mine], [b30], [b10], [b01]], gain, wq, wk, wv
     )
-    b20, b11, b31, acc = lax.optimization_barrier((*second, acc))
-    half = rows // 2
-    low, high = shift(b31[:half], 1, 0), shift(b11[half:], -1, 0)
-    acc = project(order((2, 0), (1, 1), (3, 1)), sums, [b20, b11, b31], gain, wq, wk, wv, acc)
+    b20, b11_low, b31_high, acc = lax.optimization_barrier((b20, b11_low, b31_high, acc))
+    acc = project(
+        order((2, 0), (1, 1), (3, 1)),
+        sums,
+        [[b20], [b11_low, b11_high], [b31_low, b31_high]],
+        gain,
+        wq,
+        wk,
+        wv,
+        acc,
+    )
     low, high, acc = lax.optimization_barrier((low, high, acc))
     back = attend(
         info, sums, low, high, last_gain, *last, acc, cos, sin, kv_pool, back_hot

time: 108 us -> 107 us (level)
  local copies, waits for them, and re-layouts: 9.07 us -> 7.11 us
  starting transfers between devices: 26.3 us -> 27.7 us
  blocking collectives: 26 us -> 24.9 us
    all_to_all x1, waiting for transfers between devices: 7.98 us -> 9.92 us  [after_leave(): lax.all_to_all(send.reshape(groups, wide // groups, width), 'sample', 0, 0)]
    ppermute x8 -> x10, waiting for transfers between devices: 7.75 us -> 5.91 us  [shift(): return lax.ppermute(block, 'tensor', moves(dy, dz))]
    cond x26 -> x20, local copies, waits for them, and re-layouts: 1.5 us -> 0.05 us
    ppermute x8 -> x10, starting transfers between devices: 14.6 us -> 16 us  [shift(): return lax.ppermute(block, 'tensor', moves(dy, dz))]
    all_to_all x1, blocking collectives: 26 us -> 24.9 us  [after_leave(): lax.all_to_all(back.reshape(groups, -1, back.shape[1]), 'sample', 0, 0)]
  transfers between devices with their start and end apart: 12 -> 14, of which waited for: 7 -> 6; matrix products, arithmetic and copies ran while one was open for 8% -> 7% of each run, Pallas kernels for 15% -> 15%
where the time goes in v3:
time: 107 us
  starting transfers between devices  27.7 us (26%)
  Pallas kernels  26.7 us (25%)
  blocking collectives  24.9 us (23%)
  waiting for transfers between devices  16.9 us (16%)
  local copies, waits for them, and re-layouts  7.11 us (7%)
  other arithmetic  1.93 us (2%)
    all_to_all x1, blocking collectives, after_leave(): lax.all_to_all(back.reshape(groups, -1, back.shape[1]), 'sample', 0, 0)  24.9 us
    ppermute x10, starting transfers between devices, shift(): return lax.ppermute(block, 'tensor', moves(dy, dz))  16 us
    pallas_call x2, Pallas kernels, project(): pl.pallas_call(functools.partial(project_kernel, wq.shape[0], places, bef...  11.6 us
    all_to_all x1, waiting for transfers between devices, after_leave(): lax.all_to_all(send.reshape(groups, wide // groups, width), 'sample', 0, 0)  9.92 us
    pallas_call x1, Pallas kernels, attend(): pl.pallas_call(functools.partial(attend_kernel, 8 * part), out_shape=jax....  7.29 us
    all_to_all x1, starting transfers between devices, after_leave(): lax.all_to_all(send.reshape(groups, wide // groups, width), 'sample', 0, 0)  6.13 us
    ppermute x10, waiting for transfers between devices, shift(): return lax.ppermute(block, 'tensor', moves(dy, dz))  5.91 us
    dynamic_slice x2, local copies, waits for them, and re-layouts, after_leave(): lax.dynamic_slice_in_dim(w, place(2, 1) * width, width)  4.95 us
  transfers between devices with their start and end apart: 14, of which 6 were waited for; matrix products, arithmetic and copies ran while one was open for 7% of the time, Pallas kernels for 15%

profile of v3, /device:TPU:1, one launch (start us, length us, event | category | flops | bytes accessed | tf_op | source)
XLA Modules:
  0.0 106.8 jit_solution(17652872421897200830)
XLA Ops:
  0.0 1.4 %collective-permute-start.22 = (bf16[256,1024]{1,0:T(8,128)(2,1)}, bf16[256,1024]{1,0:T(8,128)(2,1)S(1)}, u32[]{:S(2)}, u32[]{:S(2)}) collective-permute-start(bf16[256,1024]{1,0:T(8,128)(2,1)} %own_ref.1), channel_id=1, source_target_pairs={{0,8},{8,0},{16,24},{24,16},{32,40},{40,32},{48,56},{56,48},{64,72... | collective-permute-start | bytes 1572872 | tf_op jit(solution)/shard_map/ppermute | solution.py:590
  1.4 1.6 %shard_map.102 = (bf16[640,256]{1,0:T(8,128)(2,1)S(1)}, bf16[640,256]{1,0:T(8,128)(2,1)S(1)}, s32[1]{0:T(128)}) custom-call(s32[1]{0:T(128)} %bitcast.28.me_ref, s32[1,1024]{1,0:T(1,128)} %bitcast.41, s32[1,128]{1,0:T(1,128)} %bitcast.45), custom_call_target="tpu_custom_call" | custom-call | flops 1000000000 | bytes 1048576 | tf_op jit(solution)/shard_map/pallas_call | solution.py:106
  3.0 0.0 copy-start.25
  3.0 0.0 copy-start.26
  3.1 0.0 copy-start.29
  3.1 0.0 copy-start.30
  3.1 0.0 copy-start.31
  3.1 0.1 collective-permute-done.22.other_ref
  3.2 1.9 %shard_map.103 = bf16[640,1024]{1,0:T(8,128)(2,1)} custom-call(bf16[640,256]{1,0:T(8,128)(2,1)S(1)} %get-tuple-element.153.own_hot_ref, bf16[640,256]{1,0:T(8,128)(2,1)S(1)} %get-tuple-element.154.other_hot_ref, bf16[256,1024]{1,0:T(8,128)(2,1)S(1)} %copy-done.23, bf16[256,1024]{1,0:T(8,128)(2,1)S(1)} %collective-permute-done.22.other_ref), custom_call_target="tpu_custom_call" | custom-call | tf_op jit(solution)/shard_map/pallas_call | solution.py:228
  5.8 100.2 %conditional.1 = (bf16[256,1024]{1,0:T(8,128)(2,1)S(1)}) conditional(s32[]{:T(128)} %bitcast.31, (s32[1024]{0:T(1024)S(1)}, s32[128]{0:T(128)S(1)}, s32[128]{0:T(128)S(1)}, s32[128,5]{0,1:T(8,128)S(1)}, s32[1]{0:T(128)}, /*index=5*/bf16[256,1024]{1,0:T(8,128)(2,1)S(1)}, bf16[256,1024]{1,0:T(8,128)(2,1)S(1)}, bf16[8192]{0:T(1024)(128)(2,1)S(1)}, ...), branch_computations={%region_0.1_spmd, %region_1.2_spmd} | conditional | flops 20448665600 | bytes 182706240 | solution.py:604
  6.0 6.1 %all-to-all-start.3 = ((bf16[16,40,1024]{2,1,0:T(8,128)(2,1)}), bf16[16,40,1024]{2,1,0:T(8,128)(2,1)S(1)}, u32[]{:S(2)}, u32[]{:S(2)}) async-start(bf16[16,40,1024]{2,1,0:T(8,128)(2,1)} %bitcast.40), calls=%async_computation.3 | async-start | bytes 2621440 | tf_op jit(solution)/shard_map/cond/branch_1_fun/all_to_all | solution.py:501
  12.2 0.1 tile.12
  12.3 0.1 copy.20
  12.5 1.7 %branch_1_fun.8 = (bf16[256,640]{1,0:T(8,128)(2,1)S(1)}, bf16[640,256]{1,0:T(8,128)(2,1)S(1)}, bf16[256,640]{1,0:T(8,128)(2,1)S(1)}, bf16[256,640]{1,0:T(8,128)(2,1)S(1)}, s32[8,8]{1,0:T(8,128)S(1)}) custom-call(s32[1]{0:T(128)} %get-tuple-element.99.me_ref, s32[1,1024]{1,0:T(1,128)S(1)} %bitcast.44, s32[1,128]{1,0:T(1,128)S(1)} %bitcast.48, ...), custom_call_target="tpu_custom_call" | custom-call | flops 2000000000 | bytes 1048576 | tf_op jit(solution)/shard_map/cond/branch_1_fun/pallas_call | solution.py:194
  14.2 0.0 copy-start.17
  14.2 0.2 multiply_reduce_fusion.1
  14.4 0.1 broadcast_in_dim.6
  14.4 0.1 reshape.99
  14.5 0.5 fusion.1
  15.1 0.9 pad_maximum_fusion.2
  15.9 1.9 %constant_dynamic-slice_fusion.3 = (bf16[1024,128]{1,0:T(8,128)(2,1)}, bf16[1024,128]{1,0:T(8,128)(2,1)}) fusion(bf16[8192,128]{1,0:T(8,128)(2,1)} %get-tuple-element.113.refs_7_.refs_8_, s32[]{:T(128)S(6)} %select_n.149, bf16[8192,128]{1,0:T(8,128)(2,1)} %get-tuple-element.112.refs_6_.refs_7_), kind=kLoop, calls=%fused_computation.20 | loop fusion | bytes 1048580 | tf_op jit(solution)/shard_map/cond/branch_1_fun/dynamic_slice | solution.py:510
  17.8 3.1 %constant_dynamic-slice_fusion.5.wq_ref = bf16[1024,1024]{1,0:T(8,128)(2,1)} fusion(bf16[8192,1024]{1,0:T(8,128)(2,1)} %get-tuple-element.111.refs_5_.refs_6_, s32[]{:T(128)S(6)} %select_n.149), kind=kLoop, calls=%fused_computation.22 | loop fusion | bytes 4194308 | tf_op jit(solution)/shard_map/cond/branch_1_fun/dynamic_slice | solution.py:510
  20.9 0.0 copy-done.17
  20.9 9.9 %all-to-all-done.3 = bf16[16,40,1024]{2,1,0:T(8,128)(2,1)S(1)} async-done(((bf16[16,40,1024]{2,1,0:T(8,128)(2,1)}), bf16[16,40,1024]{2,1,0:T(8,128)(2,1)S(1)}, u32[]{:S(2)}, u32[]{:S(2)}) %all-to-all-start.3) | async-done | bytes 1310752 | tf_op jit(solution)/shard_map/cond/branch_1_fun/all_to_all | solution.py:501
  30.8 0.6 branch_1_fun.9.rows_ref.refs_0_
  31.4 1.4 %collective-permute-start.13 = (bf16[256,1024]{1,0:T(8,128)(2,1)S(1)}, bf16[256,1024]{1,0:T(8,128)(2,1)S(1)}, u32[]{:S(2)}, u32[]{:S(2)}) collective-permute-start(bf16[256,1024]{1,0:T(8,128)(2,1)S(1)} %branch_1_fun.9.rows_ref.refs_0_), channel_id=1, source_target_pairs={{0,2},{1,3},{2,4},{3,5},{4,6},{5,7},{6,0},{7,1},{8,10},{9,11},{10,... | collective-permute-start | bytes 1572872 | tf_op jit(solution)/shard_map/cond/branch_1_fun/ppermute | solution.py:533
  32.8 1.5 %collective-permute-start.12 = (bf16[256,1024]{1,0:T(8,128)(2,1)S(1)}, bf16[256,1024]{1,0:T(8,128)(2,1)S(1)}, u32[]{:S(2)}, u32[]{:S(2)}) collective-permute-start(bf16[256,1024]{1,0:T(8,128)(2,1)S(1)} %branch_1_fun.9.rows_ref.refs_0_), channel_id=1, source_target_pairs={{0,6},{1,7},{2,0},{3,1},{4,2},{5,3},{6,4},{7,5},{8,14},{9,15},{10,... | collective-permute-start | bytes 1572872 | tf_op jit(solution)/shard_map/cond/branch_1_fun/ppermute | solution.py:533
  34.3 3.3 %collective-permute-start.11 = (bf16[256,1024]{1,0:T(8,128)(2,1)S(1)}, bf16[256,1024]{1,0:T(8,128)(2,1)S(1)}, u32[]{:S(2)}, u32[]{:S(2)}) collective-permute-start(bf16[256,1024]{1,0:T(8,128)(2,1)S(1)} %branch_1_fun.9.rows_ref.refs_0_), channel_id=1, source_target_pairs={{0,1},{1,0},{2,3},{3,2},{4,5},{5,4},{6,7},{7,6},{8,9},{9,8},{10,11... | collective-permute-start | bytes 1572872 | tf_op jit(solution)/shard_map/cond/branch_1_fun/ppermute | solution.py:533
  37.6 0.1 pad_add_fusion.2.order_ref
  37.7 0.1 pad_add_fusion.3.order_ref
  37.7 0.8 branch_1_fun.10
  38.6 3.3 %all-to-all-start.4 = ((f32[8,1,256]{2,1,0:T(1,128)}), f32[8,1,256]{2,1,0:T(1,128)S(1)}, u32[]{:S(2)}, u32[]{:S(2)}) async-start(f32[8,1,256]{2,1,0:T(1,128)} %branch_1_fun.10), calls=%async_computation.4 | async-start | bytes 16384 | tf_op jit(solution)/shard_map/cond/branch_1_fun/all_to_all | solution.py:535
  41.9 3.7 %collective-permute-done.13.refs_1_ = bf16[256,1024]{1,0:T(8,128)(2,1)S(1)} collective-permute-done((bf16[256,1024]{1,0:T(8,128)(2,1)S(1)}, bf16[256,1024]{1,0:T(8,128)(2,1)S(1)}, u32[]{:S(2)}, u32[]{:S(2)}) %collective-permute-start.13) | collective-permute-done | bytes 524320 | tf_op jit(solution)/shard_map/cond/branch_1_fun/ppermute | solution.py:533
  45.5 0.8 fusion.4
  46.4 0.0 collective-permute-start.18
  46.4 3.3 %collective-permute-start.20 = (bf16[128,1024]{1,0:T(8,128)(2,1)}, bf16[128,1024]{1,0:T(8,128)(2,1)}, u32[]{:S(2)}, u32[]{:S(2)}) collective-permute-start(bf16[128,1024]{1,0:T(8,128)(2,1)} %get-tuple-element.213), channel_id=1, source_target_pairs={{0,1},{1,0},{2,3},{3,2},{4,5},{5,4},{6,7},{7,6},{8,9},{9,8},{10,11... | collective-permute-start | bytes 786440 | tf_op jit(solution)/shard_map/cond/branch_1_fun/ppermute | solution.py:533
  49.7 0.0 collective-permute-start.14
  49.7 0.0 all-to-all-done.4.sum_ref
  49.7 0.0 collective-permute-done.12.refs_2_
  49.7 0.0 collective-permute-done.11.refs_3_
  49.8 2.7 %collective-permute-start.19 = (bf16[128,1024]{1,0:T(8,128)(2,1)S(1)}, bf16[128,1024]{1,0:T(8,128)(2,1)S(1)}, u32[]{:S(2)}, u32[]{:S(2)}) collective-permute-start(bf16[128,1024]{1,0:T(8,128)(2,1)S(1)} %get-tuple-element.215), channel_id=1, source_target_pairs={{0,6},{1,7},{2,0},{3,1},{4,2},{5,3},{6,4},{7,5},{8,14},{9,15},{10,... | collective-permute-start | bytes 786440 | tf_op jit(solution)/shard_map/cond/branch_1_fun/ppermute | solution.py:533
  52.5 0.2 collective-permute-start.15
  52.7 6.6 %branch_1_fun.11.refs_9_ = f32[256,1280]{1,0:T(8,128)S(1)} custom-call(s32[4]{0:T(128)S(1)} %pad_add_fusion.3.order_ref, f32[8,1,256]{2,1,0:T(1,128)S(1)} %all-to-all-done.4.sum_ref, bf16[256,1024]{1,0:T(8,128)(2,1)S(1)} %branch_1_fun.9.rows_ref.refs_0_, bf16[256,1024]{1,0:T(8,128)(2,1)S(1)} %collective-permute-done.13.refs_1_, ...), custom_call_target="tpu_custom_call" | custom-call | flops 5368709120 | bytes 10485760 | tf_op jit(solution)/shard_map/cond/branch_1_fun/pallas_call | solution.py:355
  59.3 0.0 copy-start.18
  59.4 0.0 copy-start.28
  59.4 1.0 collective-permute-done.14.refs_3_
  60.3 1.3 %collective-permute-done.15.refs_2_ = bf16[128,1024]{1,0:T(8,128)(2,1)S(1)} collective-permute-done((bf16[128,1024]{1,0:T(8,128)(2,1)S(1)}, bf16[128,1024]{1,0:T(8,128)(2,1)S(1)}, u32[]{:S(2)}, u32[]{:S(2)}) %collective-permute-start.15) | collective-permute-done | bytes 262176 | tf_op jit(solution)/shard_map/cond/branch_1_fun/ppermute | solution.py:533
  61.6 0.8 collective-permute-start.16
  62.4 2.7 %collective-permute-start.17 = (bf16[128,1024]{1,0:T(8,128)(2,1)S(1)}, bf16[128,1024]{1,0:T(8,128)(2,1)S(1)}, u32[]{:S(2)}, u32[]{:S(2)}) collective-permute-start(bf16[128,1024]{1,0:T(8,128)(2,1)S(1)} %collective-permute-done.15.refs_2_), channel_id=1, source_target_pairs={{0,6},{1,7},{2,0},{3,1},{4,2},{5,3},{6,4},{7,5},{8,14},{9,15},{10,... | collective-permute-start | bytes 786440 | tf_op jit(solution)/shard_map/cond/branch_1_fun/ppermute | solution.py:533
  65.1 0.0 collective-permute-done.20.refs_4_
  65.1 0.0 collective-permute-done.19.refs_1_
  65.1 0.0 collective-permute-done.18.refs_0_
  65.2 5.0 %branch_1_fun.12.before_ref = f32[256,1280]{1,0:T(8,128)S(1)} custom-call(s32[3]{0:T(128)S(1)} %pad_add_fusion.2.order_ref, f32[8,1,256]{2,1,0:T(1,128)S(1)} %all-to-all-done.4.sum_ref, bf16[256,1024]{1,0:T(8,128)(2,1)S(1)} %collective-permute-done.18.refs_0_, bf16[128,1024]{1,0:T(8,128)(2,1)S(1)} %collective-permute-done.19.refs_1_, ...), custom_call_target="tpu_custom_call" | custom-call | flops 4026531840 | bytes 7864320 | tf_op jit(solution)/shard_map/cond/branch_1_fun/pallas_call | solution.py:355
  70.2 0.0 collective-permute-done.16.low_ref
  70.2 0.0 collective-permute-done.17.high_ref
  70.3 7.3 %branch_1_fun.13 = bf16[640,1024]{1,0:T(8,128)(2,1)S(1)} custom-call(s32[8,8]{1,0:T(8,128)S(1)} %get-tuple-element.116.info_ref, f32[8,1,256]{2,1,0:T(1,128)S(1)} %all-to-all-done.4.sum_ref, bf16[128,1024]{1,0:T(8,128)(2,1)S(1)} %collective-permute-done.16.low_ref, bf16[128,1024]{1,0:T(8,128)(2,1)S(1)} %collective-permute-done.17.high_ref, ...), custom_call_target="tpu_custom_call" | custom-call | flops 4026531840 | bytes 2621440 | tf_op jit(solution)/shard_map/cond/branch_1_fun/pallas_call | solution.py:470
  77.6 24.9 %all_to_all.25 = bf16[16,40,1024]{2,1,0:T(8,128)(2,1)S(1)} all-to-all(bf16[16,40,1024]{2,1,0:T(8,128)(2,1)S(1)} %bitcast.39), channel_id=1, replica_groups=mesh['sample'=16,'tensor'=8] {'sample'}, dimensions={0} | all-to-all | bytes 2621440 | tf_op jit(solution)/shard_map/cond/branch_1_fun/all_to_all | solution.py:563
  102.4 0.6 branch_1_fun.15
  103.0 0.9 collective-permute-start.21
  103.9 0.6 branch_1_fun.14
  104.5 0.9 collective-permute-done.21
  105.5 0.2 add.208
  106.0 0.0 copy-start.24
  106.0 0.8 copy-done.24
  (32 shorter events, 0.2 us)
Async XLA Ops:
  0.0 3.2 %copy-start.23 = (bf16[256,1024]{1,0:T(8,128)(2,1)S(1)}, bf16[256,1024]{1,0:T(8,128)(2,1)}, u32[]{:S(2)}) copy-start(bf16[256,1024]{1,0:T(8,128)(2,1)} %own_ref.1) | copy-start | bytes 1572868
  0.0 3.2 %collective-permute-start.22 = (bf16[256,1024]{1,0:T(8,128)(2,1)}, bf16[256,1024]{1,0:T(8,128)(2,1)S(1)}, u32[]{:S(2)}, u32[]{:S(2)}) collective-permute-start(bf16[256,1024]{1,0:T(8,128)(2,1)} %own_ref.1), channel_id=1, source_target_pairs={{0,8},{8,0},{16,24},{24,16},{32,40},{40,32},{48,56},{56,48},{64,72... | collective-permute-start | bytes 1572872 | tf_op jit(solution)/shard_map/ppermute | solution.py:590
  3.0 2.7 %copy-start.25 = (bf16[8192]{0:T(1024)(128)(2,1)S(1)}, bf16[8192]{0:T(1024)(128)(2,1)}, u32[]{:S(2)}) copy-start(bf16[8192]{0:T(1024)(128)(2,1)} %param.13) | copy-start | bytes 49156
  3.0 2.7 %copy-start.26 = (s32[128,5]{0,1:T(8,128)S(1)}, s32[128,5]{0,1:T(8,128)}, u32[]{:S(2)}) copy-start(s32[128,5]{0,1:T(8,128)} %param.20) | copy-start | bytes 7684
  3.1 2.7 %copy-start.29 = (s32[1024]{0:T(1024)S(1)}, s32[1024]{0:T(1024)}, u32[]{:S(2)}) copy-start(s32[1024]{0:T(1024)} %param.21) | copy-start | bytes 12292
  3.1 2.7 %copy-start.30 = (s32[128]{0:T(128)S(1)}, s32[128]{0:T(128)}, u32[]{:S(2)}) copy-start(s32[128]{0:T(128)} %param.18) | copy-start | bytes 1540
  3.1 2.7 %copy-start.31 = (s32[128]{0:T(128)S(1)}, s32[128]{0:T(128)}, u32[]{:S(2)}) copy-start(s32[128]{0:T(128)} %param.19) | copy-start | bytes 1540
  6.0 24.8 %all-to-all-start.3 = ((bf16[16,40,1024]{2,1,0:T(8,128)(2,1)}), bf16[16,40,1024]{2,1,0:T(8,128)(2,1)S(1)}, u32[]{:S(2)}, u32[]{:S(2)}) async-start(bf16[16,40,1024]{2,1,0:T(8,128)(2,1)} %bitcast.40), calls=%async_computation.3 | async-start | bytes 2621440 | tf_op jit(solution)/shard_map/cond/branch_1_fun/all_to_all | solution.py:501
  14.2 6.7 %copy-start.17 = (bf16[640,256]{1,0:T(8,128)(2,1)}, bf16[640,256]{1,0:T(8,128)(2,1)S(1)}, u32[]{:S(2)}) copy-start(bf16[640,256]{1,0:T(8,128)(2,1)S(1)} %get-tuple-element.139.back_ref) | copy-start | bytes 983044 | tf_op jit(solution)/shard_map/cond
  31.4 14.1 %collective-permute-start.13 = (bf16[256,1024]{1,0:T(8,128)(2,1)S(1)}, bf16[256,1024]{1,0:T(8,128)(2,1)S(1)}, u32[]{:S(2)}, u32[]{:S(2)}) collective-permute-start(bf16[256,1024]{1,0:T(8,128)(2,1)S(1)} %branch_1_fun.9.rows_ref.refs_0_), channel_id=1, source_target_pairs={{0,2},{1,3},{2,4},{3,5},{4,6},{5,7},{6,0},{7,1},{8,10},{9,11},{10,... | collective-permute-start | bytes 1572872 | tf_op jit(solution)/shard_map/cond/branch_1_fun/ppermute | solution.py:533
  32.8 17.0 %collective-permute-start.12 = (bf16[256,1024]{1,0:T(8,128)(2,1)S(1)}, bf16[256,1024]{1,0:T(8,128)(2,1)S(1)}, u32[]{:S(2)}, u32[]{:S(2)}) collective-permute-start(bf16[256,1024]{1,0:T(8,128)(2,1)S(1)} %branch_1_fun.9.rows_ref.refs_0_), channel_id=1, source_target_pairs={{0,6},{1,7},{2,0},{3,1},{4,2},{5,3},{6,4},{7,5},{8,14},{9,15},{10,... | collective-permute-start | bytes 1572872 | tf_op jit(solution)/shard_map/cond/branch_1_fun/ppermute | solution.py:533
  34.3 15.4 %collective-permute-start.11 = (bf16[256,1024]{1,0:T(8,128)(2,1)S(1)}, bf16[256,1024]{1,0:T(8,128)(2,1)S(1)}, u32[]{:S(2)}, u32[]{:S(2)}) collective-permute-start(bf16[256,1024]{1,0:T(8,128)(2,1)S(1)} %branch_1_fun.9.rows_ref.refs_0_), channel_id=1, source_target_pairs={{0,1},{1,0},{2,3},{3,2},{4,5},{5,4},{6,7},{7,6},{8,9},{9,8},{10,11... | collective-permute-start | bytes 1572872 | tf_op jit(solution)/shard_map/cond/branch_1_fun/ppermute | solution.py:533
  38.6 11.2 %all-to-all-start.4 = ((f32[8,1,256]{2,1,0:T(1,128)}), f32[8,1,256]{2,1,0:T(1,128)S(1)}, u32[]{:S(2)}, u32[]{:S(2)}) async-start(f32[8,1,256]{2,1,0:T(1,128)} %branch_1_fun.10), calls=%async_computation.4 | async-start | bytes 16384 | tf_op jit(solution)/shard_map/cond/branch_1_fun/all_to_all | solution.py:535
  46.4 18.8 %collective-permute-start.18 = (bf16[256,1024]{1,0:T(8,128)(2,1)S(1)}, bf16[256,1024]{1,0:T(8,128)(2,1)S(1)}, u32[]{:S(2)}, u32[]{:S(2)}) collective-permute-start(bf16[256,1024]{1,0:T(8,128)(2,1)S(1)} %collective-permute-done.13.refs_1_), channel_id=1, source_target_pairs={{0,2},{1,3},{2,4},{3,5},{4,6},{5,7},{6,0},{7,1},{8,10},{9,11},{10,... | collective-permute-start | bytes 1572872 | tf_op jit(solution)/shard_map/cond/branch_1_fun/ppermute | solution.py:533
  46.4 18.7 %collective-permute-start.20 = (bf16[128,1024]{1,0:T(8,128)(2,1)}, bf16[128,1024]{1,0:T(8,128)(2,1)}, u32[]{:S(2)}, u32[]{:S(2)}) collective-permute-start(bf16[128,1024]{1,0:T(8,128)(2,1)} %get-tuple-element.213), channel_id=1, source_target_pairs={{0,1},{1,0},{2,3},{3,2},{4,5},{5,4},{6,7},{7,6},{8,9},{9,8},{10,11... | collective-permute-start | bytes 786440 | tf_op jit(solution)/shard_map/cond/branch_1_fun/ppermute | solution.py:533
  49.7 10.7 %collective-permute-start.14 = (bf16[128,1024]{1,0:T(8,128)(2,1)}, bf16[128,1024]{1,0:T(8,128)(2,1)}, u32[]{:S(2)}, u32[]{:S(2)}) collective-permute-start(bf16[128,1024]{1,0:T(8,128)(2,1)} %get-tuple-element.214), channel_id=1, source_target_pairs={{0,1},{1,0},{2,3},{3,2},{4,5},{5,4},{6,7},{7,6},{8,9},{9,8},{10,11... | collective-permute-start | bytes 786440 | tf_op jit(solution)/shard_map/cond/branch_1_fun/ppermute | solution.py:533
  49.8 15.4 %collective-permute-start.19 = (bf16[128,1024]{1,0:T(8,128)(2,1)S(1)}, bf16[128,1024]{1,0:T(8,128)(2,1)S(1)}, u32[]{:S(2)}, u32[]{:S(2)}) collective-permute-start(bf16[128,1024]{1,0:T(8,128)(2,1)S(1)} %get-tuple-element.215), channel_id=1, source_target_pairs={{0,6},{1,7},{2,0},{3,1},{4,2},{5,3},{6,4},{7,5},{8,14},{9,15},{10,... | collective-permute-start | bytes 786440 | tf_op jit(solution)/shard_map/cond/branch_1_fun/ppermute | solution.py:533
  52.5 12.6 %copy-start.20 = (bf16[8192,128]{1,0:T(8,128)(2,1)S(1)}, bf16[8192,128]{1,0:T(8,128)(2,1)}, u32[]{:S(2)}) copy-start(bf16[8192,128]{1,0:T(8,128)(2,1)} %get-tuple-element.112.refs_6_.refs_7_) | copy-start | bytes 6291460 | tf_op jit(solution)/shard_map/cond
  52.5 12.6 %copy-start.22 = (bf16[8192,128]{1,0:T(8,128)(2,1)S(1)}, bf16[8192,128]{1,0:T(8,128)(2,1)}, u32[]{:S(2)}) copy-start(bf16[8192,128]{1,0:T(8,128)(2,1)} %get-tuple-element.113.refs_7_.refs_8_) | copy-start | bytes 6291460 | tf_op jit(solution)/shard_map/cond
  52.5 9.1 %collective-permute-start.15 = (bf16[128,1024]{1,0:T(8,128)(2,1)S(1)}, bf16[128,1024]{1,0:T(8,128)(2,1)S(1)}, u32[]{:S(2)}, u32[]{:S(2)}) collective-permute-start(bf16[128,1024]{1,0:T(8,128)(2,1)S(1)} %get-tuple-element.216), channel_id=1, source_target_pairs={{0,6},{1,7},{2,0},{3,1},{4,2},{5,3},{6,4},{7,5},{8,14},{9,15},{10,... | collective-permute-start | bytes 786440 | tf_op jit(solution)/shard_map/cond/branch_1_fun/ppermute | solution.py:533
  59.3 10.9 %copy-start.2 = (bf16[1024,1024]{1,0:T(8,128)(2,1)S(1)}, bf16[1024,1024]{1,0:T(8,128)(2,1)}, u32[]{:S(2)}) copy-start(bf16[1024,1024]{1,0:T(8,128)(2,1)} %constant_dynamic-slice_fusion.5.wq_ref) | copy-start | bytes 6291460 | tf_op jit(solution)/shard_map/cond
  59.3 10.9 %copy-start.9 = (bf16[1024,128]{1,0:T(8,128)(2,1)S(1)}, bf16[1024,128]{1,0:T(8,128)(2,1)}, u32[]{:S(2)}) copy-start(bf16[1024,128]{1,0:T(8,128)(2,1)} %get-tuple-element.134.wv_ref) | copy-start | bytes 786436 | tf_op jit(solution)/shard_map/cond
  59.3 10.9 %copy-start.10 = (bf16[1024,128]{1,0:T(8,128)(2,1)S(1)}, bf16[1024,128]{1,0:T(8,128)(2,1)}, u32[]{:S(2)}) copy-start(bf16[1024,128]{1,0:T(8,128)(2,1)} %get-tuple-element.133.wk_ref) | copy-start | bytes 786436 | tf_op jit(solution)/shard_map/cond
  59.3 10.9 %copy-start.13 = (f32[256,128]{1,0:T(8,128)S(1)}, f32[256,128]{1,0:T(8,128)}, u32[]{:S(2)}) copy-start(f32[256,128]{1,0:T(8,128)} %get-tuple-element.136.cos_ref) | copy-start | bytes 393220 | tf_op jit(solution)/shard_map/cond
  59.3 10.9 %copy-start.14 = (f32[256,128]{1,0:T(8,128)S(1)}, f32[256,128]{1,0:T(8,128)}, u32[]{:S(2)}) copy-start(f32[256,128]{1,0:T(8,128)} %get-tuple-element.137.sin_ref) | copy-start | bytes 393220 | tf_op jit(solution)/shard_map/cond
  59.3 10.9 %copy-start.18 = (bf16[640,256]{1,0:T(8,128)(2,1)S(1)}, bf16[640,256]{1,0:T(8,128)(2,1)}, u32[]{:S(2)}) copy-start(bf16[640,256]{1,0:T(8,128)(2,1)} %copy-done.17) | copy-start | bytes 983044 | tf_op jit(solution)/shard_map/cond
  59.4 10.9 %copy-start.28 = (bf16[40,2,128,128]{3,2,1,0:T(8,128)(2,1)S(1)}, bf16[40,2,128,128]{3,2,1,0:T(8,128)(2,1)}, u32[]{:S(2)}) copy-start(bf16[40,2,128,128]{3,2,1,0:T(8,128)(2,1)} %get-tuple-element.138.pool_ref) | copy-start | bytes 7864324 | tf_op jit(solution)/shard_map/cond
  61.6 8.6 %collective-permute-start.16 = (bf16[128,1024]{1,0:T(8,128)(2,1)}, bf16[128,1024]{1,0:T(8,128)(2,1)S(1)}, u32[]{:S(2)}, u32[]{:S(2)}) collective-permute-start(bf16[128,1024]{1,0:T(8,128)(2,1)} %collective-permute-done.14.refs_3_), channel_id=1, source_target_pairs={{0,2},{1,3},{2,4},{3,5},{4,6},{5,7},{6,0},{7,1},{8,10},{9,11},{10,... | collective-permute-start | bytes 786440 | tf_op jit(solution)/shard_map/cond/branch_1_fun/ppermute | solution.py:533
  62.4 7.8 %collective-permute-start.17 = (bf16[128,1024]{1,0:T(8,128)(2,1)S(1)}, bf16[128,1024]{1,0:T(8,128)(2,1)S(1)}, u32[]{:S(2)}, u32[]{:S(2)}) collective-permute-start(bf16[128,1024]{1,0:T(8,128)(2,1)S(1)} %collective-permute-done.15.refs_2_), channel_id=1, source_target_pairs={{0,6},{1,7},{2,0},{3,1},{4,2},{5,3},{6,4},{7,5},{8,14},{9,15},{10,... | collective-permute-start | bytes 786440 | tf_op jit(solution)/shard_map/cond/branch_1_fun/ppermute | solution.py:533
  103.0 2.4 %collective-permute-start.21 = (bf16[256,1024]{1,0:T(8,128)(2,1)S(1)}, bf16[256,1024]{1,0:T(8,128)(2,1)S(1)}, u32[]{:S(2)}, u32[]{:S(2)}) collective-permute-start(bf16[256,1024]{1,0:T(8,128)(2,1)S(1)} %branch_1_fun.15), channel_id=1, source_target_pairs={{0,8},{8,0},{16,24},{24,16},{32,40},{40,32},{48,56},{56,48},{64,72... | collective-permute-start | bytes 1572872 | tf_op jit(solution)/shard_map/cond/branch_1_fun/ppermute | solution.py:566
  106.0 0.8 copy-start.24

commit v4 on v3

--- a/solution.py
+++ b/solution.py
@@ -537,8 +537,9 @@
     half = rows // 2
     (b30,) = lax.optimization_barrier((b30,))
     b20, b31_low = shift(b30, 1, 0), shift(b30[:half], 0, 1)
-    b01, b10, sums = lax.optimization_barrier((b01, b10, sums))
+    b01, b10 = lax.optimization_barrier((b01, b10))
     b11_high = shift(b01[half:], -1, 0)
+    b30, b01, sums = lax.optimization_barrier((b30, b01, sums))
     b31_high, b11_low = shift(b30[half:], 0, 1), shift(b01[:half], -1, 0)
     b31_low, b11_high = lax.optimization_barrier((b31_low, b11_high))
     low, high = shift(b31_low, 1, 0), shift(b11_high, -1, 0)

time: 107 us -> 106 us (level)
  starting transfers between devices: 27.7 us -> 25.4 us
  local copies, waits for them, and re-layouts: 7.11 us -> 9.06 us
    ppermute x10, starting transfers between devices: 16 us -> 13.7 us  [shift(): return lax.ppermute(block, 'tensor', moves(dy, dz))]
    slice x0 -> x2, local copies, waits for them, and re-layouts: none -> 1.45 us  [the longest x1 0.73 us: after_leave(): b11_high = shift(b01[half:], -1, 0)]
  transfers between devices with their start and end apart: 14 -> 14, of which waited for: 6 -> 6; matrix products, arithmetic and copies ran while one was open for 7% -> 9% of each run, Pallas kernels for 15% -> 15%
where the time goes in v4:
time: 106 us; the launch traced here: 105 us
  Pallas kernels  26.2 us (25%)
  starting transfers between devices  25.4 us (24%)
  blocking collectives  24.7 us (23%)
  waiting for transfers between devices  16.6 us (16%)
  local copies, waits for them, and re-layouts  9.06 us (9%)
  other arithmetic  1.94 us (2%)
    all_to_all x1, blocking collectives, after_leave(): lax.all_to_all(back.reshape(groups, -1, back.shape[1]), 'sample', 0, 0)  24.7 us
    ppermute x10, starting transfers between devices, shift(): return lax.ppermute(block, 'tensor', moves(dy, dz))  13.7 us
    pallas_call x2, Pallas kernels, project(): pl.pallas_call(functools.partial(project_kernel, wq.shape[0], places, bef...  11.1 us
    all_to_all x1, waiting for transfers between devices, after_leave(): lax.all_to_all(send.reshape(groups, wide // groups, width), 'sample', 0, 0)  9.35 us
    pallas_call x1, Pallas kernels, attend(): pl.pallas_call(functools.partial(attend_kernel, 8 * part), out_shape=jax....  7.28 us
    ppermute x10, waiting for transfers between devices, shift(): return lax.ppermute(block, 'tensor', moves(dy, dz))  6.24 us
    all_to_all x1, starting transfers between devices, after_leave(): lax.all_to_all(send.reshape(groups, wide // groups, width), 'sample', 0, 0)  6.13 us
    dynamic_slice x2, local copies, waits for them, and re-layouts, after_leave(): lax.dynamic_slice_in_dim(w, place(2, 1) * width, width)  4.95 us
  transfers between devices with their start and end apart: 14, of which 6 were waited for; matrix products, arithmetic and copies ran while one was open for 9% of the time, Pallas kernels for 15%

profile of v4, /device:TPU:1, one launch (start us, length us, event | category | flops | bytes accessed | tf_op | source)
XLA Modules:
  0.0 105.5 jit_solution(8891956482600636985)
XLA Ops:
  0.0 1.4 %collective-permute-start.22 = (bf16[256,1024]{1,0:T(8,128)(2,1)}, bf16[256,1024]{1,0:T(8,128)(2,1)S(1)}, u32[]{:S(2)}, u32[]{:S(2)}) collective-permute-start(bf16[256,1024]{1,0:T(8,128)(2,1)} %own_ref.1), channel_id=1, source_target_pairs={{0,8},{8,0},{16,24},{24,16},{32,40},{40,32},{48,56},{56,48},{64,72... | collective-permute-start | bytes 1572872 | tf_op jit(solution)/shard_map/ppermute | solution.py:591
  1.4 1.6 %shard_map.102 = (bf16[640,256]{1,0:T(8,128)(2,1)S(1)}, bf16[640,256]{1,0:T(8,128)(2,1)S(1)}, s32[1]{0:T(128)}) custom-call(s32[1]{0:T(128)} %bitcast.28.me_ref, s32[1,1024]{1,0:T(1,128)} %bitcast.41, s32[1,128]{1,0:T(1,128)} %bitcast.45), custom_call_target="tpu_custom_call" | custom-call | flops 1000000000 | bytes 1048576 | tf_op jit(solution)/shard_map/pallas_call | solution.py:106
  3.0 0.0 copy-start.25
  3.0 0.0 copy-start.26
  3.1 0.0 copy-start.29
  3.1 0.0 copy-start.30
  3.1 0.0 copy-start.31
  3.1 0.1 collective-permute-done.22.other_ref
  3.2 1.9 %shard_map.103 = bf16[640,1024]{1,0:T(8,128)(2,1)} custom-call(bf16[640,256]{1,0:T(8,128)(2,1)S(1)} %get-tuple-element.157.own_hot_ref, bf16[640,256]{1,0:T(8,128)(2,1)S(1)} %get-tuple-element.158.other_hot_ref, bf16[256,1024]{1,0:T(8,128)(2,1)S(1)} %copy-done.23, bf16[256,1024]{1,0:T(8,128)(2,1)S(1)} %collective-permute-done.22.other_ref), custom_call_target="tpu_custom_call" | custom-call | tf_op jit(solution)/shard_map/pallas_call | solution.py:228
  5.8 98.9 %conditional.1 = (bf16[256,1024]{1,0:T(8,128)(2,1)S(1)}) conditional(s32[]{:T(128)} %bitcast.31, (s32[1024]{0:T(1024)S(1)}, s32[128]{0:T(128)S(1)}, s32[128]{0:T(128)S(1)}, s32[128,5]{0,1:T(8,128)S(1)}, s32[1]{0:T(128)}, /*index=5*/bf16[256,1024]{1,0:T(8,128)(2,1)S(1)}, bf16[256,1024]{1,0:T(8,128)(2,1)S(1)}, bf16[8192]{0:T(1024)(128)(2,1)S(1)}, ...), branch_computations={%region_0.1_spmd, %region_1.2_spmd} | conditional | flops 20448665600 | bytes 182706240 | solution.py:605
  6.0 6.1 %all-to-all-start.3 = ((bf16[16,40,1024]{2,1,0:T(8,128)(2,1)}), bf16[16,40,1024]{2,1,0:T(8,128)(2,1)S(1)}, u32[]{:S(2)}, u32[]{:S(2)}) async-start(bf16[16,40,1024]{2,1,0:T(8,128)(2,1)} %bitcast.40), calls=%async_computation.3 | async-start | bytes 2621440 | tf_op jit(solution)/shard_map/cond/branch_1_fun/all_to_all | solution.py:501
  12.2 0.6 reshape.100
  12.8 0.1 tile.12
  12.9 0.1 copy.20
  13.0 1.7 %branch_1_fun.8 = (bf16[256,640]{1,0:T(8,128)(2,1)S(1)}, bf16[640,256]{1,0:T(8,128)(2,1)S(1)}, bf16[256,640]{1,0:T(8,128)(2,1)S(1)}, bf16[256,640]{1,0:T(8,128)(2,1)S(1)}, s32[8,8]{1,0:T(8,128)S(1)}) custom-call(s32[1]{0:T(128)} %get-tuple-element.101.me_ref, s32[1,1024]{1,0:T(1,128)S(1)} %bitcast.44, s32[1,128]{1,0:T(1,128)S(1)} %bitcast.48, ...), custom_call_target="tpu_custom_call" | custom-call | flops 2000000000 | bytes 1048576 | tf_op jit(solution)/shard_map/cond/branch_1_fun/pallas_call | solution.py:194
  14.7 0.0 copy-start.17
  14.8 0.2 multiply_reduce_fusion.1
  14.9 0.1 broadcast_in_dim.6
  15.0 0.1 reshape.99
  15.1 0.5 fusion.1
  15.7 0.9 pad_maximum_fusion.2
  16.5 1.9 %constant_dynamic-slice_fusion.3 = (bf16[1024,128]{1,0:T(8,128)(2,1)}, bf16[1024,128]{1,0:T(8,128)(2,1)}) fusion(bf16[8192,128]{1,0:T(8,128)(2,1)} %get-tuple-element.115.refs_7_.refs_8_, s32[]{:T(128)S(6)} %select_n.149, bf16[8192,128]{1,0:T(8,128)(2,1)} %get-tuple-element.114.refs_6_.refs_7_), kind=kLoop, calls=%fused_computation.20 | loop fusion | bytes 1048580 | tf_op jit(solution)/shard_map/cond/branch_1_fun/dynamic_slice | solution.py:510
  18.4 3.1 %constant_dynamic-slice_fusion.5.wq_ref = bf16[1024,1024]{1,0:T(8,128)(2,1)} fusion(bf16[8192,1024]{1,0:T(8,128)(2,1)} %get-tuple-element.113.refs_5_.refs_6_, s32[]{:T(128)S(6)} %select_n.149), kind=kLoop, calls=%fused_computation.22 | loop fusion | bytes 4194308 | tf_op jit(solution)/shard_map/cond/branch_1_fun/dynamic_slice | solution.py:510
  21.5 9.3 %all-to-all-done.3 = bf16[16,40,1024]{2,1,0:T(8,128)(2,1)S(1)} async-done(((bf16[16,40,1024]{2,1,0:T(8,128)(2,1)}), bf16[16,40,1024]{2,1,0:T(8,128)(2,1)S(1)}, u32[]{:S(2)}, u32[]{:S(2)}) %all-to-all-start.3) | async-done | bytes 1310752 | tf_op jit(solution)/shard_map/cond/branch_1_fun/all_to_all | solution.py:501
  30.8 0.6 branch_1_fun.9.rows_ref.refs_0_
  31.4 1.4 %collective-permute-start.11 = (bf16[256,1024]{1,0:T(8,128)(2,1)S(1)}, bf16[256,1024]{1,0:T(8,128)(2,1)S(1)}, u32[]{:S(2)}, u32[]{:S(2)}) collective-permute-start(bf16[256,1024]{1,0:T(8,128)(2,1)S(1)} %branch_1_fun.9.rows_ref.refs_0_), channel_id=1, source_target_pairs={{0,2},{1,3},{2,4},{3,5},{4,6},{5,7},{6,0},{7,1},{8,10},{9,11},{10,... | collective-permute-start | bytes 1572872 | tf_op jit(solution)/shard_map/cond/branch_1_fun/ppermute | solution.py:533
  32.8 1.5 %collective-permute-start.13 = (bf16[256,1024]{1,0:T(8,128)(2,1)S(1)}, bf16[256,1024]{1,0:T(8,128)(2,1)S(1)}, u32[]{:S(2)}, u32[]{:S(2)}) collective-permute-start(bf16[256,1024]{1,0:T(8,128)(2,1)S(1)} %branch_1_fun.9.rows_ref.refs_0_), channel_id=1, source_target_pairs={{0,6},{1,7},{2,0},{3,1},{4,2},{5,3},{6,4},{7,5},{8,14},{9,15},{10,... | collective-permute-start | bytes 1572872 | tf_op jit(solution)/shard_map/cond/branch_1_fun/ppermute | solution.py:533
  34.3 3.3 %collective-permute-start.12 = (bf16[256,1024]{1,0:T(8,128)(2,1)S(1)}, bf16[256,1024]{1,0:T(8,128)(2,1)S(1)}, u32[]{:S(2)}, u32[]{:S(2)}) collective-permute-start(bf16[256,1024]{1,0:T(8,128)(2,1)S(1)} %branch_1_fun.9.rows_ref.refs_0_), channel_id=1, source_target_pairs={{0,1},{1,0},{2,3},{3,2},{4,5},{5,4},{6,7},{7,6},{8,9},{9,8},{10,11... | collective-permute-start | bytes 1572872 | tf_op jit(solution)/shard_map/cond/branch_1_fun/ppermute | solution.py:533
  37.6 0.1 pad_add_fusion.2.order_ref
  37.7 0.8 branch_1_fun.10
  38.5 3.3 %all-to-all-start.4 = ((f32[8,1,256]{2,1,0:T(1,128)}), f32[8,1,256]{2,1,0:T(1,128)S(1)}, u32[]{:S(2)}, u32[]{:S(2)}) async-start(f32[8,1,256]{2,1,0:T(1,128)} %branch_1_fun.10), calls=%async_computation.4 | async-start | bytes 16384 | tf_op jit(solution)/shard_map/cond/branch_1_fun/all_to_all | solution.py:535
  41.8 3.7 %collective-permute-done.11.refs_1_ = bf16[256,1024]{1,0:T(8,128)(2,1)S(1)} collective-permute-done((bf16[256,1024]{1,0:T(8,128)(2,1)S(1)}, bf16[256,1024]{1,0:T(8,128)(2,1)S(1)}, u32[]{:S(2)}, u32[]{:S(2)}) %collective-permute-start.11) | collective-permute-done | bytes 524320 | tf_op jit(solution)/shard_map/cond/branch_1_fun/ppermute | solution.py:533
  45.5 0.0 collective-permute-start.18
  45.6 0.1 pad_add_fusion.3.order_ref
  45.6 0.7 copy.17.refs_4_.refs_5_
  46.4 0.7 slice.31
  47.1 1.6 %collective-permute-done.12.refs_3_ = bf16[256,1024]{1,0:T(8,128)(2,1)S(1)} collective-permute-done((bf16[256,1024]{1,0:T(8,128)(2,1)S(1)}, bf16[256,1024]{1,0:T(8,128)(2,1)S(1)}, u32[]{:S(2)}, u32[]{:S(2)}) %collective-permute-start.12) | collective-permute-done | bytes 524320 | tf_op jit(solution)/shard_map/cond/branch_1_fun/ppermute | solution.py:533
  48.7 0.7 slice.27
  49.5 1.2 %collective-permute-start.15 = (bf16[128,1024]{1,0:T(8,128)(2,1)}, bf16[128,1024]{1,0:T(8,128)(2,1)}, u32[]{:S(2)}, u32[]{:S(2)}) collective-permute-start(bf16[128,1024]{1,0:T(8,128)(2,1)} %slice.27), channel_id=1, source_target_pairs={{0,6},{1,7},{2,0},{3,1},{4,2},{5,3},{6,4},{7,5},{8,14},{9,15},{10,... | collective-permute-start | bytes 786440 | tf_op jit(solution)/shard_map/cond/branch_1_fun/ppermute | solution.py:533
  50.7 0.0 copy-start.20
  50.7 0.0 copy-start.22
  50.7 3.2 %collective-permute-start.14 = (bf16[128,1024]{1,0:T(8,128)(2,1)}, bf16[128,1024]{1,0:T(8,128)(2,1)S(1)}, u32[]{:S(2)}, u32[]{:S(2)}) collective-permute-start(bf16[128,1024]{1,0:T(8,128)(2,1)} %slice.31), channel_id=1, source_target_pairs={{0,1},{1,0},{2,3},{3,2},{4,5},{5,4},{6,7},{7,6},{8,9},{9,8},{10,11... | collective-permute-start | bytes 786440 | tf_op jit(solution)/shard_map/cond/branch_1_fun/ppermute | solution.py:533
  54.0 0.1 collective-permute-start.20
  54.1 0.2 collective-permute-start.19
  54.3 6.1 %branch_1_fun.11.refs_9_ = f32[256,1280]{1,0:T(8,128)S(1)} custom-call(s32[4]{0:T(128)S(1)} %pad_add_fusion.3.order_ref, f32[8,1,256]{2,1,0:T(1,128)S(1)} %all-to-all-done.4.sum_ref, bf16[256,1024]{1,0:T(8,128)(2,1)S(1)} %branch_1_fun.9.rows_ref.refs_0_, bf16[256,1024]{1,0:T(8,128)(2,1)S(1)} %collective-permute-done.11.refs_1_, ...), custom_call_target="tpu_custom_call" | custom-call | flops 5368709120 | bytes 10485760 | tf_op jit(solution)/shard_map/cond/branch_1_fun/pallas_call | solution.py:355
  60.4 0.0 copy-start.18
  60.4 0.0 copy-start.28
  60.4 0.0 collective-permute-done.15.refs_2_
  60.4 1.3 %collective-permute-start.16 = (bf16[128,1024]{1,0:T(8,128)(2,1)S(1)}, bf16[128,1024]{1,0:T(8,128)(2,1)S(1)}, u32[]{:S(2)}, u32[]{:S(2)}) collective-permute-start(bf16[128,1024]{1,0:T(8,128)(2,1)S(1)} %collective-permute-done.14.refs_3_), channel_id=1, source_target_pairs={{0,2},{1,3},{2,4},{3,5},{4,6},{5,7},{6,0},{7,1},{8,10},{9,11},{10,... | collective-permute-start | bytes 786440 | tf_op jit(solution)/shard_map/cond/branch_1_fun/ppermute | solution.py:533
  61.7 1.4 %collective-permute-start.17 = (bf16[128,1024]{1,0:T(8,128)(2,1)}, bf16[128,1024]{1,0:T(8,128)(2,1)S(1)}, u32[]{:S(2)}, u32[]{:S(2)}) collective-permute-start(bf16[128,1024]{1,0:T(8,128)(2,1)} %collective-permute-done.15.refs_2_), channel_id=1, source_target_pairs={{0,6},{1,7},{2,0},{3,1},{4,2},{5,3},{6,4},{7,5},{8,14},{9,15},{10,... | collective-permute-start | bytes 786440 | tf_op jit(solution)/shard_map/cond/branch_1_fun/ppermute | solution.py:533
  63.2 0.9 collective-permute-done.20.refs_4_
  64.1 0.0 collective-permute-done.19.refs_1_
  64.1 0.0 collective-permute-done.18.refs_0_
  64.1 5.0 %branch_1_fun.12.before_ref = f32[256,1280]{1,0:T(8,128)S(1)} custom-call(s32[3]{0:T(128)S(1)} %pad_add_fusion.2.order_ref, f32[8,1,256]{2,1,0:T(1,128)S(1)} %all-to-all-done.4.sum_ref, bf16[256,1024]{1,0:T(8,128)(2,1)S(1)} %collective-permute-done.18.refs_0_, bf16[128,1024]{1,0:T(8,128)(2,1)S(1)} %collective-permute-done.19.refs_1_, ...), custom_call_target="tpu_custom_call" | custom-call | flops 4026531840 | bytes 7864320 | tf_op jit(solution)/shard_map/cond/branch_1_fun/pallas_call | solution.py:355
  69.1 0.0 collective-permute-done.17.high_ref
  69.2 7.3 %branch_1_fun.13 = bf16[640,1024]{1,0:T(8,128)(2,1)S(1)} custom-call(s32[8,8]{1,0:T(8,128)S(1)} %get-tuple-element.118.info_ref, f32[8,1,256]{2,1,0:T(1,128)S(1)} %all-to-all-done.4.sum_ref, bf16[128,1024]{1,0:T(8,128)(2,1)S(1)} %collective-permute-done.16.low_ref, bf16[128,1024]{1,0:T(8,128)(2,1)S(1)} %collective-permute-done.17.high_ref, ...), custom_call_target="tpu_custom_call" | custom-call | flops 4026531840 | bytes 2621440 | tf_op jit(solution)/shard_map/cond/branch_1_fun/pallas_call | solution.py:470
  76.5 24.7 %all_to_all.25 = bf16[16,40,1024]{2,1,0:T(8,128)(2,1)S(1)} all-to-all(bf16[16,40,1024]{2,1,0:T(8,128)(2,1)S(1)} %bitcast.39), channel_id=1, replica_groups=mesh['sample'=16,'tensor'=8] {'sample'}, dimensions={0} | all-to-all | bytes 2621440 | tf_op jit(solution)/shard_map/cond/branch_1_fun/all_to_all | solution.py:564
  101.2 0.6 branch_1_fun.15
  101.8 0.9 collective-permute-start.21
  102.6 0.6 branch_1_fun.14
  103.2 0.9 collective-permute-done.21
  104.2 0.2 add.208
  104.7 0.0 copy-start.24
  104.7 0.8 copy-done.24
  (34 shorter events, 0.1 us)
Async XLA Ops:
  0.0 3.2 %copy-start.23 = (bf16[256,1024]{1,0:T(8,128)(2,1)S(1)}, bf16[256,1024]{1,0:T(8,128)(2,1)}, u32[]{:S(2)}) copy-start(bf16[256,1024]{1,0:T(8,128)(2,1)} %own_ref.1) | copy-start | bytes 1572868
  0.0 3.2 %collective-permute-start.22 = (bf16[256,1024]{1,0:T(8,128)(2,1)}, bf16[256,1024]{1,0:T(8,128)(2,1)S(1)}, u32[]{:S(2)}, u32[]{:S(2)}) collective-permute-start(bf16[256,1024]{1,0:T(8,128)(2,1)} %own_ref.1), channel_id=1, source_target_pairs={{0,8},{8,0},{16,24},{24,16},{32,40},{40,32},{48,56},{56,48},{64,72... | collective-permute-start | bytes 1572872 | tf_op jit(solution)/shard_map/ppermute | solution.py:591
  3.0 2.7 %copy-start.25 = (bf16[8192]{0:T(1024)(128)(2,1)S(1)}, bf16[8192]{0:T(1024)(128)(2,1)}, u32[]{:S(2)}) copy-start(bf16[8192]{0:T(1024)(128)(2,1)} %param.13) | copy-start | bytes 49156
  3.0 2.7 %copy-start.26 = (s32[128,5]{0,1:T(8,128)S(1)}, s32[128,5]{0,1:T(8,128)}, u32[]{:S(2)}) copy-start(s32[128,5]{0,1:T(8,128)} %param.20) | copy-start | bytes 7684
  3.1 2.7 %copy-start.29 = (s32[1024]{0:T(1024)S(1)}, s32[1024]{0:T(1024)}, u32[]{:S(2)}) copy-start(s32[1024]{0:T(1024)} %param.21) | copy-start | bytes 12292
  3.1 2.7 %copy-start.30 = (s32[128]{0:T(128)S(1)}, s32[128]{0:T(128)}, u32[]{:S(2)}) copy-start(s32[128]{0:T(128)} %param.18) | copy-start | bytes 1540
  3.1 2.7 %copy-start.31 = (s32[128]{0:T(128)S(1)}, s32[128]{0:T(128)}, u32[]{:S(2)}) copy-start(s32[128]{0:T(128)} %param.19) | copy-start | bytes 1540
  6.0 24.8 %all-to-all-start.3 = ((bf16[16,40,1024]{2,1,0:T(8,128)(2,1)}), bf16[16,40,1024]{2,1,0:T(8,128)(2,1)S(1)}, u32[]{:S(2)}, u32[]{:S(2)}) async-start(bf16[16,40,1024]{2,1,0:T(8,128)(2,1)} %bitcast.40), calls=%async_computation.3 | async-start | bytes 2621440 | tf_op jit(solution)/shard_map/cond/branch_1_fun/all_to_all | solution.py:501
  14.7 6.7 %copy-start.17 = (bf16[640,256]{1,0:T(8,128)(2,1)}, bf16[640,256]{1,0:T(8,128)(2,1)S(1)}, u32[]{:S(2)}) copy-start(bf16[640,256]{1,0:T(8,128)(2,1)S(1)} %get-tuple-element.143.back_ref) | copy-start | bytes 983044 | tf_op jit(solution)/shard_map/cond
  31.4 14.1 %collective-permute-start.11 = (bf16[256,1024]{1,0:T(8,128)(2,1)S(1)}, bf16[256,1024]{1,0:T(8,128)(2,1)S(1)}, u32[]{:S(2)}, u32[]{:S(2)}) collective-permute-start(bf16[256,1024]{1,0:T(8,128)(2,1)S(1)} %branch_1_fun.9.rows_ref.refs_0_), channel_id=1, source_target_pairs={{0,2},{1,3},{2,4},{3,5},{4,6},{5,7},{6,0},{7,1},{8,10},{9,11},{10,... | collective-permute-start | bytes 1572872 | tf_op jit(solution)/shard_map/cond/branch_1_fun/ppermute | solution.py:533
  32.8 14.3 %collective-permute-start.13 = (bf16[256,1024]{1,0:T(8,128)(2,1)S(1)}, bf16[256,1024]{1,0:T(8,128)(2,1)S(1)}, u32[]{:S(2)}, u32[]{:S(2)}) collective-permute-start(bf16[256,1024]{1,0:T(8,128)(2,1)S(1)} %branch_1_fun.9.rows_ref.refs_0_), channel_id=1, source_target_pairs={{0,6},{1,7},{2,0},{3,1},{4,2},{5,3},{6,4},{7,5},{8,14},{9,15},{10,... | collective-permute-start | bytes 1572872 | tf_op jit(solution)/shard_map/cond/branch_1_fun/ppermute | solution.py:533
  34.3 14.4 %collective-permute-start.12 = (bf16[256,1024]{1,0:T(8,128)(2,1)S(1)}, bf16[256,1024]{1,0:T(8,128)(2,1)S(1)}, u32[]{:S(2)}, u32[]{:S(2)}) collective-permute-start(bf16[256,1024]{1,0:T(8,128)(2,1)S(1)} %branch_1_fun.9.rows_ref.refs_0_), channel_id=1, source_target_pairs={{0,1},{1,0},{2,3},{3,2},{4,5},{5,4},{6,7},{7,6},{8,9},{9,8},{10,11... | collective-permute-start | bytes 1572872 | tf_op jit(solution)/shard_map/cond/branch_1_fun/ppermute | solution.py:533
  38.5 12.2 %all-to-all-start.4 = ((f32[8,1,256]{2,1,0:T(1,128)}), f32[8,1,256]{2,1,0:T(1,128)S(1)}, u32[]{:S(2)}, u32[]{:S(2)}) async-start(f32[8,1,256]{2,1,0:T(1,128)} %branch_1_fun.10), calls=%async_computation.4 | async-start | bytes 16384 | tf_op jit(solution)/shard_map/cond/branch_1_fun/all_to_all | solution.py:535
  45.5 18.5 %collective-permute-start.18 = (bf16[256,1024]{1,0:T(8,128)(2,1)S(1)}, bf16[256,1024]{1,0:T(8,128)(2,1)S(1)}, u32[]{:S(2)}, u32[]{:S(2)}) collective-permute-start(bf16[256,1024]{1,0:T(8,128)(2,1)S(1)} %collective-permute-done.11.refs_1_), channel_id=1, source_target_pairs={{0,2},{1,3},{2,4},{3,5},{4,6},{5,7},{6,0},{7,1},{8,10},{9,11},{10,... | collective-permute-start | bytes 1572872 | tf_op jit(solution)/shard_map/cond/branch_1_fun/ppermute | solution.py:533
  49.5 11.0 %collective-permute-start.15 = (bf16[128,1024]{1,0:T(8,128)(2,1)}, bf16[128,1024]{1,0:T(8,128)(2,1)}, u32[]{:S(2)}, u32[]{:S(2)}) collective-permute-start(bf16[128,1024]{1,0:T(8,128)(2,1)} %slice.27), channel_id=1, source_target_pairs={{0,6},{1,7},{2,0},{3,1},{4,2},{5,3},{6,4},{7,5},{8,14},{9,15},{10,... | collective-permute-start | bytes 786440 | tf_op jit(solution)/shard_map/cond/branch_1_fun/ppermute | solution.py:533
  50.7 13.4 %copy-start.20 = (bf16[8192,128]{1,0:T(8,128)(2,1)S(1)}, bf16[8192,128]{1,0:T(8,128)(2,1)}, u32[]{:S(2)}) copy-start(bf16[8192,128]{1,0:T(8,128)(2,1)} %get-tuple-element.114.refs_6_.refs_7_) | copy-start | bytes 6291460 | tf_op jit(solution)/shard_map/cond
  50.7 13.4 %copy-start.22 = (bf16[8192,128]{1,0:T(8,128)(2,1)S(1)}, bf16[8192,128]{1,0:T(8,128)(2,1)}, u32[]{:S(2)}) copy-start(bf16[8192,128]{1,0:T(8,128)(2,1)} %get-tuple-element.115.refs_7_.refs_8_) | copy-start | bytes 6291460 | tf_op jit(solution)/shard_map/cond
  50.7 9.7 %collective-permute-start.14 = (bf16[128,1024]{1,0:T(8,128)(2,1)}, bf16[128,1024]{1,0:T(8,128)(2,1)S(1)}, u32[]{:S(2)}, u32[]{:S(2)}) collective-permute-start(bf16[128,1024]{1,0:T(8,128)(2,1)} %slice.31), channel_id=1, source_target_pairs={{0,1},{1,0},{2,3},{3,2},{4,5},{5,4},{6,7},{7,6},{8,9},{9,8},{10,11... | collective-permute-start | bytes 786440 | tf_op jit(solution)/shard_map/cond/branch_1_fun/ppermute | solution.py:533
  54.0 10.1 %collective-permute-start.20 = (bf16[128,1024]{1,0:T(8,128)(2,1)S(1)}, bf16[128,1024]{1,0:T(8,128)(2,1)S(1)}, u32[]{:S(2)}, u32[]{:S(2)}) collective-permute-start(bf16[128,1024]{1,0:T(8,128)(2,1)S(1)} %slice.29), channel_id=1, source_target_pairs={{0,1},{1,0},{2,3},{3,2},{4,5},{5,4},{6,7},{7,6},{8,9},{9,8},{10,11... | collective-permute-start | bytes 786440 | tf_op jit(solution)/shard_map/cond/branch_1_fun/ppermute | solution.py:533
  54.1 10.0 %collective-permute-start.19 = (bf16[128,1024]{1,0:T(8,128)(2,1)S(1)}, bf16[128,1024]{1,0:T(8,128)(2,1)S(1)}, u32[]{:S(2)}, u32[]{:S(2)}) collective-permute-start(bf16[128,1024]{1,0:T(8,128)(2,1)S(1)} %slice.28), channel_id=1, source_target_pairs={{0,6},{1,7},{2,0},{3,1},{4,2},{5,3},{6,4},{7,5},{8,14},{9,15},{10,... | collective-permute-start | bytes 786440 | tf_op jit(solution)/shard_map/cond/branch_1_fun/ppermute | solution.py:533
  60.3 8.8 %copy-start.2 = (bf16[1024,1024]{1,0:T(8,128)(2,1)S(1)}, bf16[1024,1024]{1,0:T(8,128)(2,1)}, u32[]{:S(2)}) copy-start(bf16[1024,1024]{1,0:T(8,128)(2,1)} %constant_dynamic-slice_fusion.5.wq_ref) | copy-start | bytes 6291460 | tf_op jit(solution)/shard_map/cond
  60.4 8.8 %copy-start.9 = (bf16[1024,128]{1,0:T(8,128)(2,1)S(1)}, bf16[1024,128]{1,0:T(8,128)(2,1)}, u32[]{:S(2)}) copy-start(bf16[1024,128]{1,0:T(8,128)(2,1)} %get-tuple-element.138.wv_ref) | copy-start | bytes 786436 | tf_op jit(solution)/shard_map/cond
  60.4 8.8 %copy-start.10 = (bf16[1024,128]{1,0:T(8,128)(2,1)S(1)}, bf16[1024,128]{1,0:T(8,128)(2,1)}, u32[]{:S(2)}) copy-start(bf16[1024,128]{1,0:T(8,128)(2,1)} %get-tuple-element.137.wk_ref) | copy-start | bytes 786436 | tf_op jit(solution)/shard_map/cond
  60.4 8.8 %copy-start.13 = (f32[256,128]{1,0:T(8,128)S(1)}, f32[256,128]{1,0:T(8,128)}, u32[]{:S(2)}) copy-start(f32[256,128]{1,0:T(8,128)} %get-tuple-element.140.cos_ref) | copy-start | bytes 393220 | tf_op jit(solution)/shard_map/cond
  60.4 8.8 %copy-start.14 = (f32[256,128]{1,0:T(8,128)S(1)}, f32[256,128]{1,0:T(8,128)}, u32[]{:S(2)}) copy-start(f32[256,128]{1,0:T(8,128)} %get-tuple-element.141.sin_ref) | copy-start | bytes 393220 | tf_op jit(solution)/shard_map/cond
  60.4 8.8 %copy-start.18 = (bf16[640,256]{1,0:T(8,128)(2,1)S(1)}, bf16[640,256]{1,0:T(8,128)(2,1)}, u32[]{:S(2)}) copy-start(bf16[640,256]{1,0:T(8,128)(2,1)} %copy-done.17) | copy-start | bytes 983044 | tf_op jit(solution)/shard_map/cond
  60.4 8.8 %copy-start.28 = (bf16[40,2,128,128]{3,2,1,0:T(8,128)(2,1)S(1)}, bf16[40,2,128,128]{3,2,1,0:T(8,128)(2,1)}, u32[]{:S(2)}) copy-start(bf16[40,2,128,128]{3,2,1,0:T(8,128)(2,1)} %get-tuple-element.142.pool_ref) | copy-start | bytes 7864324 | tf_op jit(solution)/shard_map/cond
  60.4 8.7 %collective-permute-start.16 = (bf16[128,1024]{1,0:T(8,128)(2,1)S(1)}, bf16[128,1024]{1,0:T(8,128)(2,1)S(1)}, u32[]{:S(2)}, u32[]{:S(2)}) collective-permute-start(bf16[128,1024]{1,0:T(8,128)(2,1)S(1)} %collective-permute-done.14.refs_3_), channel_id=1, source_target_pairs={{0,2},{1,3},{2,4},{3,5},{4,6},{5,7},{6,0},{7,1},{8,10},{9,11},{10,... | collective-permute-start | bytes 786440 | tf_op jit(solution)/shard_map/cond/branch_1_fun/ppermute | solution.py:533
  61.7 7.4 %collective-permute-start.17 = (bf16[128,1024]{1,0:T(8,128)(2,1)}, bf16[128,1024]{1,0:T(8,128)(2,1)S(1)}, u32[]{:S(2)}, u32[]{:S(2)}) collective-permute-start(bf16[128,1024]{1,0:T(8,128)(2,1)} %collective-permute-done.15.refs_2_), channel_id=1, source_target_pairs={{0,6},{1,7},{2,0},{3,1},{4,2},{5,3},{6,4},{7,5},{8,14},{9,15},{10,... | collective-permute-start | bytes 786440 | tf_op jit(solution)/shard_map/cond/branch_1_fun/ppermute | solution.py:533
  101.8 2.4 %collective-permute-start.21 = (bf16[256,1024]{1,0:T(8,128)(2,1)S(1)}, bf16[256,1024]{1,0:T(8,128)(2,1)S(1)}, u32[]{:S(2)}, u32[]{:S(2)}) collective-permute-start(bf16[256,1024]{1,0:T(8,128)(2,1)S(1)} %branch_1_fun.15), channel_id=1, source_target_pairs={{0,8},{8,0},{16,24},{24,16},{32,40},{40,32},{48,56},{56,48},{64,72... | collective-permute-start | bytes 1572872 | tf_op jit(solution)/shard_map/cond/branch_1_fun/ppermute | solution.py:567
  104.7 0.8 copy-start.24
